TPU v7x, 512 devices: a whole 4x4x16 slice. The times are simulated.
512 devices in a mesh: lat: 64 (over y, z), lev: 8 (over x, core).
Axes of the slice: x: 4, y: 4, z: 16, core: 2. Of those that a mesh axis runs over, the one named last changes fastest.
Arguments:
- grid_fields: bfloat16 [32, 1280, 2688], P('lev', 'lat'), may hold values from -6 to 6
- legendre: bfloat16 [1024, 2, 640, 512], P(('lat', 'lev')), may hold values from -0.15625 to 0.15625
- weights: float32 [640], replicated, may hold values from 0.2 to 1.6
- kept_waves: int32 [1280], P('lat'), may hold values from 8 to 1024, as said below
- slot_wavenumber: int32 [1024], replicated, may hold values from 0 to 1023, as said below
- diffusion: float32 [32], replicated, may hold values from 0.5 to 50
Outputs:
- grid_out: float32 [32, 1280, 2688], P('lev', 'lat')
- spectral: float32 [1024, 2, 32, 2, 512], P(('lat', 'lev'))
- spectrum: float32 [1024], replicated
Inputs may be any that keep to these rules, and one draw needn't show every extreme that they name: kept_waves[j] wavenumbers are retained at latitude j; it equals 1024 at the two latitudes nearest the equator. `slot_wavenumber`: a permutation of 0 to 1023 whose entries 2k and 2k + 1 add up to 1023; device d of the lat, lev mesh in that order owns slots d * 2 to (d + 1) * 2 - 1.
All inputs are finite; a program needn't handle non-finite values.
Results may differ from a plain program's by a relative error of at most 0.0071.
Values may be sent and summed in bfloat16 or wider, within the bound.
No kernel may reach another device: no remote copies, remote signals or barrier semaphores. Data moves between devices by JAX's collectives and lax.ppermute only.
A program may use at most 128 MiB of HBM per device.

v0:
```python
import math

import jax
import jax.numpy as jnp
from jax import lax
from jax.sharding import PartitionSpec as P

NLAT = 1280
MM = 1024


def dft_table(points, wave_count):
    sample = jnp.arange(points, dtype=jnp.int32)[:, None]
    number = jnp.arange(wave_count, dtype=jnp.int32)[None, :]
    angles = (sample * number % points).astype(jnp.float32) * (2.0 * math.pi / points)
    norm_scale = 1.0 / math.sqrt(points)
    return (jnp.concatenate([jnp.cos(angles), -jnp.sin(angles)], axis=1) * norm_scale).astype(
        jnp.bfloat16
    )


def spread_by_degree(values, offsets):
    width = values.shape[1]
    padded = jnp.concatenate([jnp.zeros_like(values), values], axis=1)

    def placed(row_values, offset_value):
        return lax.dynamic_slice_in_dim(row_values, width - offset_value, width)

    return jax.vmap(placed)(padded, offsets)


def body(grid_fields, legendre, weights, kept_waves, slot_wavenumber, diffusion):
    lat_count = lax.axis_size("lat")
    lev_count = lax.axis_size("lev")
    level_dev, band_dev, points = grid_fields.shape
    slot_dev = legendre.shape[0]
    half_wave = legendre.shape[3]
    north_groups = lat_count // 2
    levels = level_dev * lev_count
    transform = dft_table(points, MM)
    fourier_raw = jnp.dot(
        grid_fields.reshape(level_dev * band_dev, points),
        transform,
        preferred_element_type=jnp.float32,
    )
    fourier_raw = fourier_raw.reshape(level_dev, band_dev, 2, MM)
    latitude = lax.axis_index("lat") * band_dev + jnp.arange(band_dev, dtype=jnp.int32)
    mirror = jnp.minimum(latitude, NLAT - 1 - latitude)
    kept_mask = jnp.arange(MM, dtype=jnp.int32)[None, :] < kept_waves[:, None]
    factor = jnp.where(kept_mask, jnp.take(weights, mirror)[:, None], 0.0)
    fourier = (fourier_raw * factor[None, :, None, :]).astype(jnp.bfloat16)
    slotted = jnp.take(fourier, slot_wavenumber, axis=3)
    outgoing = slotted.reshape(level_dev, band_dev, 2, lat_count, lev_count, slot_dev)
    outgoing = outgoing.transpose(3, 4, 0, 2, 5, 1).reshape(
        lat_count, lev_count, level_dev * 2 * slot_dev * band_dev
    )
    arrived = lax.all_to_all(
        lax.all_to_all(outgoing, "lat", split_axis=0, concat_axis=0, tiled=True),
        "lev",
        split_axis=1,
        concat_axis=2,
        tiled=True,
    )
    arrived = arrived.reshape(lat_count, lev_count, level_dev, 2, slot_dev, band_dev)
    northern = arrived[:north_groups].astype(jnp.float32)
    southern = arrived[north_groups:][::-1, :, :, :, :, ::-1].astype(jnp.float32)
    combined = jnp.stack([northern + southern, northern - southern]).astype(jnp.bfloat16)
    table_local = legendre.reshape(slot_dev, 2, north_groups, band_dev, half_wave)
    device = lax.axis_index("lat") * lev_count + lax.axis_index("lev")
    owned_waves = lax.dynamic_slice_in_dim(slot_wavenumber, device * slot_dev, slot_dev)
    spectral_raw = jnp.einsum(
        "tqaji,qablrtj->tqblri", table_local, combined, preferred_element_type=jnp.float32
    )
    spectral_raw = spectral_raw.reshape(slot_dev, 2, levels, 2, half_wave)
    parity = jnp.arange(2, dtype=jnp.int32)[None, :, None, None, None]
    column = jnp.arange(half_wave, dtype=jnp.int32)[None, None, None, None, :]
    degree = owned_waves[:, None, None, None, None] + 2 * column + parity
    spectral = jnp.where(degree < MM, spectral_raw, 0.0)
    degree_float = degree.astype(jnp.float32)
    damping_ratio = degree_float * (degree_float + 1.0) / (MM * (MM + 1.0))
    damped = (
        spectral / (1.0 + diffusion[None, None, :, None, None] * damping_ratio * damping_ratio)
    ).astype(jnp.bfloat16)
    damped_local = damped.reshape(slot_dev, 2, lev_count, level_dev, 2, half_wave)
    halves = jnp.einsum(
        "tqaji,tqblri->qablrtj", table_local, damped_local, preferred_element_type=jnp.float32
    )
    north_back = (halves[0] + halves[1]).astype(jnp.bfloat16)
    south_back = (halves[0] - halves[1]).astype(jnp.bfloat16)[::-1, :, :, :, :, ::-1]
    leaving = jnp.concatenate([north_back, south_back], axis=0).reshape(
        1, lat_count, levels * 2 * slot_dev * band_dev
    )
    returned = lax.all_to_all(
        lax.all_to_all(leaving, "lat", split_axis=1, concat_axis=1, tiled=True),
        "lev",
        split_axis=2,
        concat_axis=0,
        tiled=True,
    )
    returned = returned.reshape(lev_count, lat_count, level_dev, 2, slot_dev, band_dev)
    returned = returned.transpose(2, 5, 3, 1, 0, 4).reshape(level_dev, band_dev, 2, MM)
    position = jnp.argsort(slot_wavenumber)
    coefficients = jnp.where(
        kept_mask[None, :, None, :],
        jnp.take(returned, position, axis=3),
        jnp.zeros((), jnp.bfloat16),
    )
    grid_out = lax.dot_general(
        coefficients.reshape(level_dev * band_dev, 2 * MM),
        transform,
        (((1,), (1,)), ((), ())),
        preferred_element_type=jnp.float32,
    )
    grid_out = (grid_out * math.sqrt(points / MM)).reshape(level_dev, band_dev, points)
    energy = jnp.sum(spectral * spectral, axis=(2, 3))
    energy = jnp.swapaxes(energy, 1, 2).reshape(slot_dev, MM)
    local_sum = jnp.sum(spread_by_degree(energy, owned_waves), axis=0)
    summed = lax.psum(local_sum, ("lat", "lev"))
    spectrum = summed / (2.0 * levels * (jnp.arange(MM, dtype=jnp.float32) + 1.0))
    return (grid_out, spectral, spectrum)


def solution(mesh):
    in_specs = (P("lev", "lat", None), P(("lat", "lev"), None, None, None), P(), P("lat"), P(), P())
    out_specs = (P("lev", "lat", None), P(("lat", "lev"), None, None, None, None), P())
    return jax.shard_map(body, mesh=mesh, in_specs=in_specs, out_specs=out_specs, check_vma=False)
```

profile of v0, /device:TPU:1, one launch (start us, length us, event | category | flops | bytes accessed | tf_op | source)
XLA Modules:
  0.0 342.1 jit_solution(2479318632705025869)
XLA Ops:
  0.7 47.2 %sine_negate_fusion = (f32[2688,1024]{1,0:T(8,128)}, f32[2688,1024]{1,0:T(8,128)}) fusion(), kind=kLoop, calls=%fused_computation.9 | loop fusion | flops 27525120 | bytes 22020096 | tf_op jit(solution)/shard_map/neg | solution.py:17
  47.9 0.7 gather_fusion
  48.8 8.4 %convolution_bitcast_fusion = f32[80,2048]{1,0:T(8,128)S(1)} fusion(bf16[80,2688]{1,0:T(8,128)(2,1)S(1)} %reshape.209, f32[2688,1024]{1,0:T(8,128)} %get-tuple-element.83, f32[2688,1024]{1,0:T(8,128)} %get-tuple-element.84), kind=kOutput, calls=%fused_computation.20 | convolution fusion | flops 897318912 | bytes 23105536 | tf_op jit(solution)/shard_map/dot_general | solution.py:41
  58.3 2.6 copy.146
  61.0 6.0 %gather_fusion.1 = bf16[1024,4,20,2]{2,1,3,0:T(4,128)(2,1)S(1)} fusion(bf16[4,20,2,1024]{1,0,3,2:T(4,128)(2,1)} %copy.146, s32[1024]{0:T(1024)S(1)} %fusion.35), kind=kCustom, calls=%fused_computation.clone | custom fusion | bytes 659456 | tf_op jit(solution)/shard_map/jit(_take)/gather | solution.py:52
  67.0 3.8 %select_bitcast_fusion = bf16[4,20,2,1024]{1,0,2,3:T(4,128)(2,1)S(1)} fusion(bf16[1024,4,20,2]{2,1,3,0:T(4,128)(2,1)S(1)} %gather_fusion.1, pred[1024]{0:T(1024)(128)(4,1)S(1)} %compare_and_fusion.1), kind=kLoop, calls=%fused_computation.22 | loop fusion | flops 163840 | bytes 656384 | tf_op jit(solution)/shard_map/jit(_take)/select_n | solution.py:52
  71.1 2.5 copy.148
  73.6 1.3 copy.149
  74.8 19.3 %all-to-all-start = ((bf16[64,8,320]{2,1,0:T(8,128)(2,1)}), bf16[64,8,320]{2,1,0:T(8,128)(2,1)S(1)}, u32[]{:S(2)}, u32[]{:S(2)}) async-start(bf16[64,8,320]{2,1,0:T(8,128)(2,1)} %copy.149), calls=%async_computation | async-start | bytes 786432 | tf_op jit(solution)/shard_map/all_to_all | solution.py:58
  94.9 24.0 %all-to-all-done = bf16[64,8,320]{2,1,0:T(8,128)(2,1)S(1)} async-done(((bf16[64,8,320]{2,1,0:T(8,128)(2,1)}), bf16[64,8,320]{2,1,0:T(8,128)(2,1)S(1)}, u32[]{:S(2)}, u32[]{:S(2)}) %all-to-all-start) | async-done | bytes 327712 | tf_op jit(solution)/shard_map/all_to_all | solution.py:58
  118.9 0.8 copy.150
  119.7 6.9 %all-to-all-start.1 = ((bf16[64,8,320]{2,0,1:T(8,128)(2,1)}), bf16[64,8,320]{2,0,1:T(8,128)(2,1)S(1)}, u32[]{:S(2)}, u32[]{:S(2)}) async-start(bf16[64,8,320]{2,0,1:T(8,128)(2,1)} %copy.150), calls=%async_computation.1 | async-start | bytes 786432 | tf_op jit(solution)/shard_map/all_to_all | solution.py:57
  126.6 4.4 %copy.157 = bf16[2,2,640,512]{3,1,2,0:T(2,128)(2,1)S(1)} copy(bf16[2,2,640,512]{3,2,1,0:T(8,128)(2,1)} %param.9) | data formatting | bytes 5242880 | tf_op args[1]
  131.3 3.3 all-to-all-done.1
  134.6 0.8 fusion.45
  135.4 1.3 copy.185
  136.8 0.9 copy.153
  137.6 2.3 rev.6
  139.9 2.1 copy.184
  142.0 1.4 fusion.27
  143.5 1.9 fusion.19
  145.4 0.7 multiply_reduce_fusion
  146.1 2.4 fusion.11
  148.7 0.8 rev.7
  150.4 1.6 copy.163
  152.5 2.6 reduce.1
  155.1 0.8 reshape.275
  155.9 6.3 %all-to-all-start.2 = ((bf16[64,2,1280]{2,1,0:T(2,128)(2,1)}), bf16[64,2,1280]{2,1,0:T(2,128)(2,1)S(1)}, u32[]{:S(2)}, u32[]{:S(2)}) async-start(bf16[64,2,1280]{2,1,0:T(2,128)(2,1)} %reshape.275), calls=%async_computation.2 | async-start | bytes 655360 | tf_op jit(solution)/shard_map/all_to_all | solution.py:94
  162.2 4.4 %sort.17 = (s32[1024]{0:T(1024)}, s32[1024]{0:T(1024)S(1)}) sort(s32[1024]{0:T(1024)S(1)} %copy-done.3, s32[1024]{0:T(1024)S(1)} %iota.50), dimensions={0}, to_apply=%region_0.2 | sort | flops 10240 | bytes 16384 | tf_op jit(solution)/shard_map/jit(argsort)/sort | solution.py:102
  167.6 4.1 %while.1 = (s32[]{:T(128)}, f32[2,2048]{1,0:T(2,128)S(1)}, s32[2,2]{1,0:T(2,128)S(1)}, f32[2,1024]{1,0:T(2,128)S(1)}, s32[]{:T(128)}, /*index=5*/s32[]{:T(128)}) while((s32[]{:T(128)}, f32[2,2048]{1,0:T(2,128)S(1)}, s32[2,2]{1,0:T(2,128)S(1)}, f32[2,1024]{1,0:T(2,128)S(1)}, s32[]{:T(128)}, /*index=5*/s32[]{:T(128)}) %tuple.44), condition=%wide.while_cond, body=%wide.while_body.sunk | while | flops 2 | bytes 16497 | solution.py:27
  168.2 1.4 dynamic-slice.7
  170.3 1.4 dynamic-slice.7
  171.7 104.0 %psum.7 = f32[1024]{0:T(1024)S(1)} all-reduce(f32[1024]{0:T(1024)S(1)} %reduce_sum.19), channel_id=1, replica_groups=mesh['lat'=64,'lev'=8] {'lat','lev'}, use_global_device_ids=true, to_apply=%region_3.5 | all-reduce | flops 1024 | bytes 8192 | tf_op jit(solution)/shard_map/psum | solution.py:118
  276.0 1.1 copy.164
  277.1 14.2 %reduce.2 = bf16[2560,64]{1,0:T(8,128)(2,1)S(1)} reduce(bf16[2560,1,64]{2,1,0:T(2,128)(2,1)S(1)} %bitcast.66, bf16[]{:T(256)} %broadcast.252), dimensions={1}, to_apply=%bitcast.54.reduce_sub_computation | reduce | bytes 655362
  291.3 1.2 reshape.277
  292.5 4.0 %all-to-all-start.3 = ((bf16[8,2,10240]{2,1,0:T(2,128)(2,1)}), bf16[8,2,10240]{2,1,0:T(2,128)(2,1)S(1)}, u32[]{:S(2)}, u32[]{:S(2)}) async-start(bf16[8,2,10240]{2,1,0:T(2,128)(2,1)} %reshape.277), calls=%async_computation.3 | async-start | bytes 655360 | tf_op jit(solution)/shard_map/all_to_all | solution.py:93
  297.5 1.1 broadcast_select_fusion
  298.6 5.1 %all-to-all-done.3 = bf16[8,2,10240]{2,1,0:T(2,128)(2,1)S(1)} async-done(((bf16[8,2,10240]{2,1,0:T(2,128)(2,1)}), bf16[8,2,10240]{2,1,0:T(2,128)(2,1)S(1)}, u32[]{:S(2)}, u32[]{:S(2)}) %all-to-all-start.3) | async-done | bytes 327712 | tf_op jit(solution)/shard_map/all_to_all | solution.py:93
  303.7 0.7 reshape.278
  304.4 0.8 copy.165
  306.0 2.4 copy.167
  308.4 3.0 copy.168
  311.4 10.5 %gather_fusion.2 = bf16[1024,4,20,2]{2,1,3,0:T(4,128)(2,1)} fusion(bf16[4,20,2,1024]{1,0,3,2:T(4,128)(2,1)} %copy.168, s32[1024]{0:T(1024)S(1)} %fusion.36), kind=kCustom, calls=%fused_computation.1.clone | custom fusion | bytes 659456 | tf_op jit(solution)/shard_map/jit(_take)/gather | solution.py:105
  321.9 8.5 %bitcast_select_fusion = bf16[4,20,2,1024]{1,0,2,3:T(4,128)(2,1)S(1)} fusion(bf16[1024,4,20,2]{2,1,3,0:T(4,128)(2,1)} %gather_fusion.2, pred[1024]{0:T(1024)(128)(4,1)S(1)} %compare_and_fusion, pred[20,1024]{0,1:T(8,128)(4,1)S(1)} %copy.143), kind=kLoop, calls=%fused_computation.21 | loop fusion | flops 327680 | bytes 676864 | tf_op jit(solution)/shard_map/jit(_where)/select_n | solution.py:103
  330.4 1.5 copy.169
  331.9 9.0 %convolution_multiply_fusion = f32[80,2688]{1,0:T(8,128)S(1)} fusion(bf16[80,2048]{1,0:T(8,128)(2,1)S(1)} %bitcast.77, f32[2688,1024]{1,0:T(8,128)} %get-tuple-element.83, f32[2688,1024]{1,0:T(8,128)} %get-tuple-element.84), kind=kOutput, calls=%fused_computation.15 | convolution fusion | flops 897533952 | bytes 23207936 | tf_op jit(solution)/shard_map/dot_general | solution.py:108
  341.0 1.1 copy.173
  (67 shorter events, 8.8 us)
Async XLA Ops:
  0.6 47.3 %copy-start = (f32[640]{0:T(1024)S(1)}, f32[640]{0:T(1024)}, u32[]{:S(2)}) copy-start(f32[640]{0:T(1024)} %param.10) | copy-start | bytes 7684
  0.7 47.2 %copy-start.3 = (s32[1024]{0:T(1024)S(1)}, s32[1024]{0:T(1024)}, u32[]{:S(2)}) copy-start(s32[1024]{0:T(1024)} %param.12) | copy-start | bytes 12292
  0.7 47.9 %copy-start.2 = (bf16[4,20,2688]{2,0,1:T(4,128)(2,1)S(1)}, bf16[4,20,2688]{2,0,1:T(4,128)(2,1)}, u32[]{:S(2)}) copy-start(bf16[4,20,2688]{2,0,1:T(4,128)(2,1)} %param.8) | copy-start | bytes 1290244
  48.8 9.0 %copy-start.5 = (s32[20]{0:T(128)S(1)}, s32[20]{0:T(128)}, u32[]{:S(2)}) copy-start(s32[20]{0:T(128)} %param.11) | copy-start | bytes 244
  74.8 44.0 %all-to-all-start = ((bf16[64,8,320]{2,1,0:T(8,128)(2,1)}), bf16[64,8,320]{2,1,0:T(8,128)(2,1)S(1)}, u32[]{:S(2)}, u32[]{:S(2)}) async-start(bf16[64,8,320]{2,1,0:T(8,128)(2,1)} %copy.149), calls=%async_computation | async-start | bytes 786432 | tf_op jit(solution)/shard_map/all_to_all | solution.py:58
  119.7 14.9 %all-to-all-start.1 = ((bf16[64,8,320]{2,0,1:T(8,128)(2,1)}), bf16[64,8,320]{2,0,1:T(8,128)(2,1)S(1)}, u32[]{:S(2)}, u32[]{:S(2)}) async-start(bf16[64,8,320]{2,0,1:T(8,128)(2,1)} %copy.150), calls=%async_computation.1 | async-start | bytes 786432 | tf_op jit(solution)/shard_map/all_to_all | solution.py:57
  126.6 4.5 %copy-start.7 = (f32[32]{0:T(128)S(1)}, f32[32]{0:T(128)}, u32[]{:S(2)}) copy-start(f32[32]{0:T(128)} %param.13) | copy-start | bytes 388
  150.1 16.8 %copy-start.6 = (s32[2,1]{0,1:T(1,128)S(1)}, s32[2,1]{0,1:T(1,128)}, u32[]{:S(2)}) copy-start(s32[2,1]{0,1:T(1,128)} %get-tuple-element.71) | copy-start | bytes 28
  150.1 17.0 %copy-start.4 = (f32[2,2,512]{2,1,0:T(2,128)S(1)}, f32[2,2,512]{2,1,0:T(2,128)}, u32[]{:S(2)}) copy-start(f32[2,2,512]{2,1,0:T(2,128)} %get-tuple-element.79) | copy-start | bytes 24580
  155.9 119.9 %all-to-all-start.2 = ((bf16[64,2,1280]{2,1,0:T(2,128)(2,1)}), bf16[64,2,1280]{2,1,0:T(2,128)(2,1)S(1)}, u32[]{:S(2)}, u32[]{:S(2)}) async-start(bf16[64,2,1280]{2,1,0:T(2,128)(2,1)} %reshape.275), calls=%async_computation.2 | async-start | bytes 655360 | tf_op jit(solution)/shard_map/all_to_all | solution.py:94
  292.5 11.1 %all-to-all-start.3 = ((bf16[8,2,10240]{2,1,0:T(2,128)(2,1)}), bf16[8,2,10240]{2,1,0:T(2,128)(2,1)S(1)}, u32[]{:S(2)}, u32[]{:S(2)}) async-start(bf16[8,2,10240]{2,1,0:T(2,128)(2,1)} %reshape.277), calls=%async_computation.3 | async-start | bytes 655360 | tf_op jit(solution)/shard_map/all_to_all | solution.py:93
  331.9 10.2 %copy-start.1 = (f32[640]{0:T(1024)S(1)}, f32[640]{0:T(1024)}, u32[]{:S(2)}) copy-start(f32[640]{0:T(1024)} %param.10) | copy-start | bytes 7684
where the time goes:
time: 343 us; the launch traced here: 342 us
  blocking collectives  104 us (30%)
  other arithmetic  86.7 us (25%)
  local copies, waits for them, and re-layouts  59.8 us (17%)
  starting transfers between devices  36.4 us (11%)
  waiting for transfers between devices  32.4 us (9%)
  matrix products  21.6 us (6%)
    psum x1, blocking collectives, body(): summed = lax.psum(local_sum, ('lat', 'lev'))  104 us
    neg x1, other arithmetic, dft_table(): -jnp.sin(angles)  47.2 us
    all_to_all x1, waiting for transfers between devices, body(): lax.all_to_all(outgoing, 'lat', split_axis=0, concat_axis=0, tiled=True)  24 us
    all_to_all x1, starting transfers between devices, body(): lax.all_to_all(outgoing, 'lat', split_axis=0, concat_axis=0, tiled=True)  19.3 us
    unnamed x3, other arithmetic  16.8 us
    unnamed x29, local copies, waits for them, and re-layouts  12.8 us
    gather x1, local copies, waits for them, and re-layouts, body(): jnp.take(returned, position, axis=3)  10.5 us
    dot_general x1, matrix products, body(): lax.dot_general(coefficients.reshape(level_dev * band_dev, 2 * MM), trans...  8.98 us
  transfers between devices with their start and end apart: 4, of which 3 were waited for; matrix products, arithmetic and copies ran while one was open for 5% of the time, Pallas kernels for 0%

commit v1 on v0

v1 whole, which is shorter than its diff:
```python
import math

import jax
import jax.numpy as jnp
import ml_dtypes
import numpy as np
from jax import lax
from jax.experimental import pallas as pl
from jax.experimental.pallas import tpu as pltpu
from jax.sharding import Mesh
from jax.sharding import PartitionSpec as P

NLAT = 1280
NLON = 2688
MM = 1024
HALF = MM // 2
LEVELS = 32
BAND = 20
LEV = 4
ROWS = BAND * LEV
LATS = 64
LEVS = 8
NORTH = LATS // 2
STEPS = 4
BLOCK = MM // STEPS
TILES = BAND // 4
LANES = 128

BF16 = jnp.bfloat16
F32 = jnp.float32
VMEM = pl.BlockSpec(memory_space=pltpu.VMEM)
SMEM = pl.BlockSpec(memory_space=pltpu.SMEM)
PARAMS = pltpu.CompilerParams(vmem_limit_bytes=48 * 1024 * 1024)


def dft_tables():
    sample = np.arange(NLON, dtype=np.int32)[:, None]
    number = np.arange(MM, dtype=np.int32)[None, :]
    angles = (sample * number % NLON).astype(np.float32) * np.float32(2.0 * math.pi / NLON)
    norm_scale = np.float32(1.0 / math.sqrt(NLON))
    cosine = (np.cos(angles) * norm_scale).astype(ml_dtypes.bfloat16)
    sine = (-np.sin(angles) * norm_scale).astype(ml_dtypes.bfloat16)
    both = np.stack([cosine, sine], axis=1).reshape(NLON, 2, STEPS, BLOCK)
    forward = np.ascontiguousarray(both.transpose(2, 0, 1, 3)).reshape(STEPS, NLON, 2 * BLOCK)
    inverse = np.ascontiguousarray(forward.transpose(0, 2, 1))
    return forward, inverse


def iota(shape, dim):
    return lax.broadcasted_iota(jnp.int32, shape, dim)


def slot_choice(slots_ref, step):
    number = iota((BLOCK, MM), 0) + step * BLOCK
    return jnp.where(slots_ref[...] == number, 1.0, 0.0).astype(BF16)


def per_latitude(ref, zero, start=None, mirrored=False):
    band = iota((ROWS, LANES), 0) // LEV
    column = jnp.full((ROWS, LANES), zero)
    for j in range(BAND):
        if mirrored:
            latitude = start * BAND + j
            scalar = ref[jnp.minimum(latitude, NLAT - 1 - latitude)]
        else:
            scalar = ref[j]
        column = jnp.where(band == j, scalar, column)
    return column


def row_choice(southern):
    to = iota((2 * ROWS, 2 * ROWS), 0)
    source = iota((2 * ROWS, 2 * ROWS), 1)
    band = to // (2 * LEV)
    band = jnp.where(southern, BAND - 1 - band, band)
    wanted = (to % 2) * ROWS + band * LEV + to // 2 % LEV
    return jnp.where(source == wanted, 1.0, 0.0).astype(BF16)


def fourier_kernel(lat_ref, kept_ref, weights_ref, slots_ref, x_ref, table_ref, o_ref, kept, factor, acc):
    step = pl.program_id(0)
    lat = lat_ref[0]

    @pl.when(step == 0)
    def _():
        kept[...] = per_latitude(kept_ref, jnp.int32(0))
        factor[...] = per_latitude(weights_ref, F32(0.0), lat, True)
        acc[...] = jnp.zeros_like(acc)

    raw = jnp.dot(x_ref[...], table_ref[0], preferred_element_type=F32)
    number = iota((ROWS, BLOCK), 1) + step * BLOCK
    mask = number < jnp.concatenate([kept[...]] * (BLOCK // LANES), axis=1)
    scale = jnp.where(mask, jnp.concatenate([factor[...]] * (BLOCK // LANES), axis=1), 0.0)
    fourier = jnp.concatenate([raw[:, :BLOCK] * scale, raw[:, BLOCK:] * scale], axis=0).astype(BF16)
    acc[...] += jnp.dot(fourier, slot_choice(slots_ref, step), preferred_element_type=F32)

    @pl.when(step == STEPS - 1)
    def _():
        choice = row_choice(lat >= NORTH)
        rows = jnp.dot(choice, acc[...].astype(BF16), preferred_element_type=F32).astype(BF16)
        for b in range(LEVS):
            o_ref[b] = rows[:, b * LANES : (b + 1) * LANES]


def gather_kernel(y_ref, o_ref, rows):
    for j in range(BAND):
        block = jnp.concatenate([y_ref[b, 8 * j : 8 * j + 8, :].astype(F32) for b in range(LEVS)], axis=0)
        turned = block.T
        rows[:, j % 4, (j // 4) * LANES : (j // 4 + 1) * LANES] = jnp.concatenate(
            [turned[:LATS], turned[LATS:]], axis=1
        )
    o_ref[...] = rows[...].astype(BF16)


def scatter_kernel(z_ref, o_ref, rows):
    rows[...] = z_ref[...].astype(F32)
    for j in range(BAND):
        block = rows[:, j % 4, (j // 4) * LANES : (j // 4 + 1) * LANES]
        turned = jnp.concatenate([block[:, :LATS], block[:, LATS:]], axis=0).T
        for b in range(LEVS):
            o_ref[b, 8 * j : 8 * j + 8, :] = turned[8 * b : 8 * b + 8].astype(BF16)


def legendre_kernel(waves_ref, diffusion_ref, z_ref, table_ref, spectral_ref, energy_ref, o_ref, comb):
    for group in range(NORTH * TILES // 4):
        north, south = [], []
        for u in range(4 * group, 4 * group + 4):
            a, tile = divmod(u, TILES)
            lanes = slice(tile * LANES, (tile + 1) * LANES)
            north.append(z_ref[a, :, lanes].astype(F32))
            south.append(z_ref[LATS - 1 - a, :, lanes].astype(F32))
        north = jnp.concatenate(north, axis=0)
        south = jnp.concatenate(south, axis=0)
        comb[0, 16 * group : 16 * group + 16, :] = north + south
        comb[1, 16 * group : 16 * group + 16, :] = north - south
    column = iota((64, HALF), 1)
    power = [jnp.zeros((1, HALF), F32), jnp.zeros((1, HALF), F32)]
    halves = []
    for q in range(2):
        left = comb[q].T.astype(BF16)
        parts = []
        for t in range(2):
            wave = waves_ref[t]
            raw = jnp.dot(left[64 * t : 64 * t + 64], table_ref[t, q], preferred_element_type=F32)
            degree = wave + 2 * column + q
            spectral = jnp.where(degree < MM, raw, 0.0)
            spectral_ref[t, q] = spectral
            degree = degree.astype(F32)
            ratio = degree * (degree + 1.0) / (MM * (MM + 1.0))
            damped = (spectral / (1.0 + diffusion_ref[...] * ratio * ratio)).astype(BF16)
            parts.append(
                lax.dot_general(
                    table_ref[t, q], damped, (((1,), (1,)), ((), ())), preferred_element_type=F32
                )
            )
            energy = jnp.sum(spectral * spectral, axis=0, keepdims=True)
            first = wave + q
            moved = pltpu.roll(jnp.broadcast_to(energy, (8, HALF)), first // 2 % HALF, 1)[:1]
            for odd in range(2):
                power[odd] += jnp.where(first % 2 == odd, moved, 0.0)
        halves.append(jnp.concatenate(parts, axis=1))
    energy_ref[...] = jnp.concatenate(power, axis=0)
    north = halves[0] + halves[1]
    south = halves[0] - halves[1]
    for u in range(NORTH * TILES):
        a, tile = divmod(u, TILES)
        lanes = slice(tile * LANES, (tile + 1) * LANES)
        o_ref[a, :, lanes] = north[4 * u : 4 * u + 4].astype(BF16)
        o_ref[LATS - 1 - a, :, lanes] = south[4 * u : 4 * u + 4].astype(BF16)


def grid_kernel(lat_ref, kept_ref, slots_ref, y_ref, table_ref, o_ref, kept, rows, acc):
    step = pl.program_id(0)

    @pl.when(step == 0)
    def _():
        kept[...] = per_latitude(kept_ref, jnp.int32(0))
        choice = row_choice(lat_ref[0] >= NORTH)
        back = jnp.concatenate([y_ref[b] for b in range(LEVS)], axis=1)
        rows[...] = lax.dot_general(
            choice, back, (((0,), (0,)), ((), ())), preferred_element_type=F32
        ).astype(BF16)
        acc[...] = jnp.zeros_like(acc)

    numbered = lax.dot_general(
        rows[...], slot_choice(slots_ref, step), (((1,), (1,)), ((), ())), preferred_element_type=F32
    )
    number = iota((ROWS, BLOCK), 1) + step * BLOCK
    mask = number < jnp.concatenate([kept[...]] * (BLOCK // LANES), axis=1)
    coefficients = jnp.concatenate(
        [jnp.where(mask, numbered[:ROWS], 0.0), jnp.where(mask, numbered[ROWS:], 0.0)], axis=1
    ).astype(BF16)
    acc[...] += jnp.dot(coefficients, table_ref[0], preferred_element_type=F32)

    @pl.when(step == STEPS - 1)
    def _():
        o_ref[...] = acc[...] * math.sqrt(NLON / MM)


def exchange(x, axes):
    return lax.all_to_all(x, axes, split_axis=0, concat_axis=0, tiled=True)


def body(grid_fields, legendre, weights, kept_waves, slot_wavenumber, diffusion):
    forward_table, inverse_table = dft_tables()
    lat = lax.axis_index(("y", "z")).astype(jnp.int32)
    lev = lax.axis_index(("x", "core")).astype(jnp.int32)
    lat_ref = lat.reshape(1)
    slots = slot_wavenumber.reshape(LATS, LEVS, 2).transpose(1, 2, 0).reshape(1, MM)
    waves = lax.dynamic_slice_in_dim(slot_wavenumber, (lat * LEVS + lev) * 2, 2)
    x = grid_fields.transpose(1, 0, 2).reshape(ROWS, NLON)

    sent = pl.pallas_call(
        fourier_kernel,
        grid=(STEPS,),
        in_specs=[
            SMEM,
            SMEM,
            SMEM,
            VMEM,
            VMEM,
            pl.BlockSpec((1, NLON, 2 * BLOCK), lambda i: (i, 0, 0)),
        ],
        out_specs=VMEM,
        out_shape=jax.ShapeDtypeStruct((LEVS, 2 * ROWS, LANES), BF16),
        scratch_shapes=[
            pltpu.VMEM((ROWS, LANES), jnp.int32),
            pltpu.VMEM((ROWS, LANES), F32),
            pltpu.VMEM((2 * ROWS, MM), F32),
        ],
        compiler_params=PARAMS,
        name="fourier",
    )(lat_ref, kept_waves, weights, slots, x, jnp.asarray(forward_table))
    arrived = exchange(sent, ("x", "core"))
    gathered = pl.pallas_call(
        gather_kernel,
        in_specs=[VMEM],
        out_specs=VMEM,
        out_shape=jax.ShapeDtypeStruct((LATS, 4, TILES * LANES), BF16),
        scratch_shapes=[pltpu.VMEM((LATS, 4, TILES * LANES), F32)],
        compiler_params=PARAMS,
        name="gather",
    )(arrived)
    gathered = exchange(gathered, ("y", "z"))
    spectral, energy, back = pl.pallas_call(
        legendre_kernel,
        in_specs=[SMEM, VMEM, VMEM, VMEM],
        out_specs=[VMEM, VMEM, VMEM],
        out_shape=[
            jax.ShapeDtypeStruct((2, 2, 2 * LEVELS, HALF), F32),
            jax.ShapeDtypeStruct((2, HALF), F32),
            jax.ShapeDtypeStruct((LATS, 4, TILES * LANES), BF16),
        ],
        scratch_shapes=[pltpu.VMEM((2, NLAT // 2, LANES), F32)],
        compiler_params=PARAMS,
        name="legendre",
    )(waves, jnp.repeat(diffusion, 2).reshape(2 * LEVELS, 1), gathered, legendre)

    power = jnp.sum(
        exchange(jnp.broadcast_to(energy.reshape(1, LEVS, LANES), (LEVS, LEVS, LANES)), ("x", "core")), axis=0
    )
    power = lax.dynamic_slice_in_dim(power, lev, 1)
    power = jnp.sum(
        exchange(jnp.broadcast_to(power.reshape(1, 1, LANES), (LATS, 1, LANES)), ("y", "z")), axis=0
    )
    power = exchange(jnp.broadcast_to(power.reshape(1, 1, LANES), (LEVS, 1, LANES)), ("x", "core"))
    summed = power.reshape(2, HALF).T.reshape(MM)
    spectrum = summed / (2.0 * LEVELS * (jnp.arange(MM, dtype=F32) + 1.0))

    back = exchange(back, ("y", "z"))
    scattered = pl.pallas_call(
        scatter_kernel,
        in_specs=[VMEM],
        out_specs=VMEM,
        out_shape=jax.ShapeDtypeStruct((LEVS, 2 * ROWS, LANES), BF16),
        scratch_shapes=[pltpu.VMEM((LATS, 4, TILES * LANES), F32)],
        compiler_params=PARAMS,
        name="scatter",
    )(back)
    returned = exchange(scattered, ("x", "core"))
    grid_out = pl.pallas_call(
        grid_kernel,
        grid=(STEPS,),
        in_specs=[
            SMEM,
            SMEM,
            VMEM,
            VMEM,
            pl.BlockSpec((1, 2 * BLOCK, NLON), lambda i: (i, 0, 0)),
        ],
        out_specs=VMEM,
        out_shape=jax.ShapeDtypeStruct((ROWS, NLON), F32),
        scratch_shapes=[
            pltpu.VMEM((ROWS, LANES), jnp.int32),
            pltpu.VMEM((2 * ROWS, MM), BF16),
            pltpu.VMEM((ROWS, NLON), F32),
        ],
        compiler_params=PARAMS,
        name="grid",
    )(lat_ref, kept_waves, slots, returned, jnp.asarray(inverse_table))
    grid_out = grid_out.reshape(BAND, LEV, NLON).transpose(1, 0, 2)
    return grid_out, spectral.reshape(2, 2, LEVELS, 2, HALF), spectrum


def solution(mesh):
    fine = Mesh(mesh.devices.reshape(4, 16, 4, 2), ("y", "z", "x", "core"))
    lat, lev = ("y", "z"), ("x", "core")
    both = lat + lev
    in_specs = (P(lev, lat, None), P(both, None, None, None), P(), P(lat), P(), P())
    out_specs = (P(lev, lat, None), P(both, None, None, None, None), P())
    return jax.shard_map(body, mesh=fine, in_specs=in_specs, out_specs=out_specs, check_vma=False)
```

time: 343 us -> 157 us (0.46)
  other arithmetic: 86.7 us -> 1.31 us
  blocking collectives: 104 us -> 36 us
  local copies, waits for them, and re-layouts: 59.8 us -> 9.7 us
  matrix products: 21.6 us -> 0 us
  waiting for transfers between devices: 32.4 us -> 52.5 us
  Pallas kernels: 0 us -> 19.1 us
    psum x1 -> x0, blocking collectives: 104 us -> none  [body(): summed = lax.psum(local_sum, ('lat', 'lev'))]
    neg x1 -> x0, other arithmetic: 47.2 us -> none  [dft_table(): -jnp.sin(angles)]
    all_to_all x0 -> x2, blocking collectives: none -> 36 us  [exchange(): return lax.all_to_all(x, axes, split_axis=0, concat_axis=0, tiled=True)]
    dot_general x4 -> x0, matrix products: 21.6 us -> none  [the longest x1 8.98 us: body(): lax.dot_general(coefficients.reshape(level_dev * band_dev, 2 * MM), trans...]
    gather x11 -> x0, local copies, waits for them, and re-layouts: 21.2 us -> none  [the longest x1 10.5 us: body(): jnp.take(returned, position, axis=3)]
    all_to_all x4 -> x5, waiting for transfers between devices: 32.4 us -> 52.5 us  [exchange(): return lax.all_to_all(x, axes, split_axis=0, concat_axis=0, tiled=True)]
    pallas_call x0 -> x5, Pallas kernels: none -> 19.1 us  [the longest x1 7.39 us: body(): pl.pallas_call(grid_kernel, grid=(STEPS,), in_specs=[SMEM, SMEM, VMEM, VM...]
    unnamed x3 -> x0, other arithmetic: 16.8 us -> none
  transfers between devices with their start and end apart: 4 -> 5, of which waited for: 3 -> 5; matrix products, arithmetic and copies ran while one was open for 5% -> 3% of each run, Pallas kernels for 0% -> 1%
where the time goes in v1:
time: 157 us
  waiting for transfers between devices  52.5 us (33%)
  starting transfers between devices  37.3 us (24%)
  blocking collectives  36 us (23%)
  Pallas kernels  19.1 us (12%)
  local copies, waits for them, and re-layouts  9.7 us (6%)
    all_to_all x5, waiting for transfers between devices, exchange(): return lax.all_to_all(x, axes, split_axis=0, concat_axis=0, tiled=True)  52.5 us
    all_to_all x5, starting transfers between devices, exchange(): return lax.all_to_all(x, axes, split_axis=0, concat_axis=0, tiled=True)  37.3 us
    all_to_all x2, blocking collectives, exchange(): return lax.all_to_all(x, axes, split_axis=0, concat_axis=0, tiled=True)  36 us
    pallas_call x1, Pallas kernels, body(): pl.pallas_call(grid_kernel, grid=(STEPS,), in_specs=[SMEM, SMEM, VMEM, VM...  7.39 us
    pallas_call x1, Pallas kernels, body(): pl.pallas_call(fourier_kernel, grid=(STEPS,), in_specs=[SMEM, SMEM, SMEM,...  6.57 us
  transfers between devices with their start and end apart: 5, of which 5 were waited for; matrix products, arithmetic and copies ran while one was open for 3% of the time, Pallas kernels for 1%

profile of v1, /device:TPU:1, one launch (start us, length us, event | category | flops | bytes accessed | tf_op | source)
XLA Modules:
  0.0 156.7 jit_solution(7472750124879534638)
XLA Ops:
  0.6 0.0 copy-start
  0.6 1.0 reshape.43
  1.7 0.1 copy.23
  1.8 0.1 reshape.44.slots_ref
  1.9 1.1 reshape.45.x_ref
  3.1 0.0 copy-start.2
  3.1 0.7 copy-done.2
  3.8 0.0 copy-start.3
  3.8 0.7 copy-done.3
  4.4 0.0 copy-start.5
  4.4 0.0 copy-start.4
  4.4 6.6 %fourier.1 = bf16[8,160,128]{2,1,0:T(8,128)(2,1)S(1)} custom-call(s32[1]{0:T(128)} %bitcast.lat_ref, s32[20]{0:T(128)S(1)} %copy-done.3, f32[640]{0:T(1024)S(1)} %copy-done.2, s32[1,1024]{1,0:T(1,128)S(1)} %reshape.44.slots_ref, bf16[80,2688]{1,0:T(8,128)(2,1)S(1)} %reshape.45.x_ref, bf16[4,2688,512]{2,1,0:T(8,128)(2,1)} %constant.37.clone.table_ref), custom_call_target="tpu_custom_call" | custom-call | tf_op jit(solution)/shard_map/fourier/pallas_call | solution.py:213
  11.0 16.7 %all_to_all.35.y_ref = bf16[8,160,128]{2,1,0:T(8,128)(2,1)S(1)} all-to-all(bf16[8,160,128]{2,1,0:T(8,128)(2,1)S(1)} %fourier.1), channel_id=1, replica_groups=mesh['y'=4,'z'=16,'x'=4,'core'=2] {'x','core'}, dimensions={0} | all-to-all | bytes 655360 | tf_op jit(solution)/shard_map/all_to_all | solution.py:201
  27.7 1.5 gather.1
  29.3 14.8 %all-to-all-start.1 = ((bf16[64,4,640]{2,1,0:T(4,128)(2,1)}), bf16[64,4,640]{2,1,0:T(4,128)(2,1)S(1)}, u32[]{:S(2)}, u32[]{:S(2)}) async-start(bf16[64,4,640]{2,1,0:T(4,128)(2,1)} %gather.1), calls=%async_computation.1 | async-start | bytes 655360 | tf_op jit(solution)/shard_map/all_to_all | solution.py:201
  44.1 0.8 dynamic_slice.6.waves_ref
  44.9 0.0 copy-done.5
  44.9 0.1 broadcast_in_dim.22
  44.9 0.1 reshape_reshape.4.diffusion_ref
  45.0 20.1 %all-to-all-done.1.z_ref = bf16[64,4,640]{2,1,0:T(4,128)(2,1)S(1)} async-done(((bf16[64,4,640]{2,1,0:T(4,128)(2,1)}), bf16[64,4,640]{2,1,0:T(4,128)(2,1)S(1)}, u32[]{:S(2)}, u32[]{:S(2)}) %all-to-all-start.1) | async-done | bytes 327712 | tf_op jit(solution)/shard_map/all_to_all | solution.py:201
  65.1 0.0 copy-done
  65.1 2.0 %legendre.1 = (f32[2,2,64,512]{3,2,1,0:T(8,128)S(1)}, f32[2,512]{1,0:T(2,128)S(1)}, bf16[64,4,640]{2,1,0:T(4,128)(2,1)S(1)}) custom-call(s32[2]{0:T(128)S(1)} %dynamic_slice.6.waves_ref, f32[64,1]{1,0:T(8,128)S(1)} %reshape_reshape.4.diffusion_ref, bf16[64,4,640]{2,1,0:T(4,128)(2,1)S(1)} %all-to-all-done.1.z_ref, bf16[2,2,640,512]{3,2,1,0:T(8,128)(2,1)S(1)} %copy-done), custom_call_target="tpu_custom_call" | custom-call | tf_op jit(solution)/shard_map/legendre/pallas_call | solution.py:245
  67.2 0.0 copy-start.1
  67.2 0.7 copy-done.1
  67.9 0.6 broadcast_in_dim.24
  68.5 6.9 %all-to-all-start.4 = ((f32[8,8,128]{2,1,0:T(8,128)}), f32[8,8,128]{2,1,0:T(8,128)S(1)}, u32[]{:S(2)}, u32[]{:S(2)}) async-start(f32[8,8,128]{2,1,0:T(8,128)} %broadcast_in_dim.24), calls=%async_computation.4 | async-start | bytes 65536 | tf_op jit(solution)/shard_map/all_to_all | solution.py:201
  75.4 4.7 %all-to-all-done.4 = f32[8,8,128]{2,1,0:T(8,128)S(1)} async-done(((f32[8,8,128]{2,1,0:T(8,128)}), f32[8,8,128]{2,1,0:T(8,128)S(1)}, u32[]{:S(2)}, u32[]{:S(2)}) %all-to-all-start.4) | async-done | bytes 32800 | tf_op jit(solution)/shard_map/all_to_all | solution.py:201
  80.2 19.3 %all_to_all.36 = f32[64,1,128]{2,1,0:T(1,128)S(1)} all-to-all(f32[64,1,128]{2,1,0:T(1,128)S(1)} %broadcast_in_dim.26), channel_id=1, replica_groups=mesh['y'=4,'z'=16,'x'=4,'core'=2] {'y','z'}, dimensions={0} | all-to-all | bytes 65536 | tf_op jit(solution)/shard_map/all_to_all | solution.py:201
  99.4 4.6 %all-to-all-start.2 = ((bf16[64,4,640]{2,1,0:T(4,128)(2,1)}), bf16[64,4,640]{2,1,0:T(4,128)(2,1)S(1)}, u32[]{:S(2)}, u32[]{:S(2)}) async-start(bf16[64,4,640]{2,1,0:T(4,128)(2,1)} %copy-done.1), calls=%async_computation.2 | async-start | bytes 655360 | tf_op jit(solution)/shard_map/all_to_all | solution.py:201
  104.1 20.8 %all-to-all-done.2.z_ref = bf16[64,4,640]{2,1,0:T(4,128)(2,1)S(1)} async-done(((bf16[64,4,640]{2,1,0:T(4,128)(2,1)}), bf16[64,4,640]{2,1,0:T(4,128)(2,1)S(1)}, u32[]{:S(2)}, u32[]{:S(2)}) %all-to-all-start.2) | async-done | bytes 327712 | tf_op jit(solution)/shard_map/all_to_all | solution.py:201
  124.9 0.6 broadcast_in_dim.27
  125.5 7.0 %all-to-all-start.6 = ((f32[8,1,128]{2,1,0:T(1,128)}), f32[8,1,128]{2,1,0:T(1,128)S(1)}, u32[]{:S(2)}, u32[]{:S(2)}) async-start(f32[8,1,128]{2,1,0:T(1,128)} %broadcast_in_dim.27), calls=%async_computation.6 | async-start | bytes 8192 | tf_op jit(solution)/shard_map/all_to_all | solution.py:201
  132.5 1.6 %scatter.1 = bf16[8,160,128]{2,1,0:T(8,128)(2,1)} custom-call(bf16[64,4,640]{2,1,0:T(4,128)(2,1)S(1)} %all-to-all-done.2.z_ref), custom_call_target="tpu_custom_call" | custom-call | tf_op jit(solution)/shard_map/scatter/pallas_call | solution.py:271
  134.1 2.9 %all-to-all-done.6 = f32[8,1,128]{2,1,0:T(1,128)S(1)} async-done(((f32[8,1,128]{2,1,0:T(1,128)}), f32[8,1,128]{2,1,0:T(1,128)S(1)}, u32[]{:S(2)}, u32[]{:S(2)}) %all-to-all-start.6) | async-done | bytes 4128 | tf_op jit(solution)/shard_map/all_to_all | solution.py:201
  137.0 4.0 %all-to-all-start.3 = ((bf16[8,160,128]{2,1,0:T(8,128)(2,1)}), bf16[8,160,128]{2,1,0:T(8,128)(2,1)S(1)}, u32[]{:S(2)}, u32[]{:S(2)}) async-start(bf16[8,160,128]{2,1,0:T(8,128)(2,1)} %scatter.1), calls=%async_computation.3 | async-start | bytes 655360 | tf_op jit(solution)/shard_map/all_to_all | solution.py:201
  141.0 1.1 reshape.47
  142.1 0.5 broadcast.6
  142.6 0.7 reduce.4
  143.3 0.1 copy.26
  143.5 0.2 reshape.49
  143.6 0.6 multiply_divide_fusion
  144.2 3.9 %all-to-all-done.3.y_ref = bf16[8,160,128]{2,1,0:T(8,128)(2,1)S(1)} async-done(((bf16[8,160,128]{2,1,0:T(8,128)(2,1)}), bf16[8,160,128]{2,1,0:T(8,128)(2,1)S(1)}, u32[]{:S(2)}, u32[]{:S(2)}) %all-to-all-start.3) | async-done | bytes 327712 | tf_op jit(solution)/shard_map/all_to_all | solution.py:201
  148.2 0.0 copy-done.4
  148.2 7.4 %grid.1 = f32[80,2688]{1,0:T(8,128)S(1)} custom-call(s32[1]{0:T(128)} %bitcast.lat_ref, s32[20]{0:T(128)S(1)} %copy-done.4, s32[1,1024]{1,0:T(1,128)S(1)} %reshape.44.slots_ref, bf16[8,160,128]{2,1,0:T(8,128)(2,1)S(1)} %all-to-all-done.3.y_ref, bf16[4,512,2688]{2,1,0:T(8,128)(2,1)} %constant.38.clone.table_ref), custom_call_target="tpu_custom_call" | custom-call | tf_op jit(solution)/shard_map/grid/pallas_call | solution.py:281
  155.6 1.2 reshape.46
  (6 shorter events, 0.1 us)
Async XLA Ops:
  0.6 64.5 %copy-start = (bf16[2,2,640,512]{3,2,1,0:T(8,128)(2,1)S(1)}, bf16[2,2,640,512]{3,2,1,0:T(8,128)(2,1)}, u32[]{:S(2)}) copy-start(bf16[2,2,640,512]{3,2,1,0:T(8,128)(2,1)} %table_ref.3) | copy-start | bytes 7864324
  3.1 0.7 copy-start.2
  3.8 0.7 copy-start.3
  4.4 40.5 %copy-start.5 = (f32[32]{0:T(128)S(1)}, f32[32]{0:T(128)}, u32[]{:S(2)}) copy-start(f32[32]{0:T(128)} %param.13) | copy-start | bytes 388
  4.4 143.7 %copy-start.4 = (s32[20]{0:T(128)S(1)}, s32[20]{0:T(128)}, u32[]{:S(2)}) copy-start(s32[20]{0:T(128)} %kept_ref.3) | copy-start | bytes 244
  29.3 35.9 %all-to-all-start.1 = ((bf16[64,4,640]{2,1,0:T(4,128)(2,1)}), bf16[64,4,640]{2,1,0:T(4,128)(2,1)S(1)}, u32[]{:S(2)}, u32[]{:S(2)}) async-start(bf16[64,4,640]{2,1,0:T(4,128)(2,1)} %gather.1), calls=%async_computation.1 | async-start | bytes 655360 | tf_op jit(solution)/shard_map/all_to_all | solution.py:201
  67.2 0.7 copy-start.1
  68.5 11.6 %all-to-all-start.4 = ((f32[8,8,128]{2,1,0:T(8,128)}), f32[8,8,128]{2,1,0:T(8,128)S(1)}, u32[]{:S(2)}, u32[]{:S(2)}) async-start(f32[8,8,128]{2,1,0:T(8,128)} %broadcast_in_dim.24), calls=%async_computation.4 | async-start | bytes 65536 | tf_op jit(solution)/shard_map/all_to_all | solution.py:201
  99.4 25.4 %all-to-all-start.2 = ((bf16[64,4,640]{2,1,0:T(4,128)(2,1)}), bf16[64,4,640]{2,1,0:T(4,128)(2,1)S(1)}, u32[]{:S(2)}, u32[]{:S(2)}) async-start(bf16[64,4,640]{2,1,0:T(4,128)(2,1)} %copy-done.1), calls=%async_computation.2 | async-start | bytes 655360 | tf_op jit(solution)/shard_map/all_to_all | solution.py:201
  125.5 11.5 %all-to-all-start.6 = ((f32[8,1,128]{2,1,0:T(1,128)}), f32[8,1,128]{2,1,0:T(1,128)S(1)}, u32[]{:S(2)}, u32[]{:S(2)}) async-start(f32[8,1,128]{2,1,0:T(1,128)} %broadcast_in_dim.27), calls=%async_computation.6 | async-start | bytes 8192 | tf_op jit(solution)/shard_map/all_to_all | solution.py:201
  137.0 11.2 %all-to-all-start.3 = ((bf16[8,160,128]{2,1,0:T(8,128)(2,1)}), bf16[8,160,128]{2,1,0:T(8,128)(2,1)S(1)}, u32[]{:S(2)}, u32[]{:S(2)}) async-start(bf16[8,160,128]{2,1,0:T(8,128)(2,1)} %scatter.1), calls=%async_computation.3 | async-start | bytes 655360 | tf_op jit(solution)/shard_map/all_to_all | solution.py:201

commit v2 on v1

v2 whole, which is shorter than its diff:
```python
import math

import jax
import jax.numpy as jnp
import ml_dtypes
import numpy as np
from jax import lax
from jax.experimental import pallas as pl
from jax.experimental.pallas import tpu as pltpu
from jax.sharding import Mesh
from jax.sharding import PartitionSpec as P

NLAT = 1280
NLON = 2688
MM = 1024
HALF = MM // 2
LEVELS = 32
BAND = 20
LEV = 4
ROWS = BAND * LEV
LATS = 64
LEVS = 8
NORTH = LATS // 2
STEPS = 4
BLOCK = MM // STEPS
TILES = BAND // 4
LANES = 128
DATA = TILES * LANES

BF16 = jnp.bfloat16
F32 = jnp.float32
VMEM = pl.BlockSpec(memory_space=pltpu.VMEM)
HBM = pl.BlockSpec(memory_space=pltpu.HBM)
SMEM = pl.BlockSpec(memory_space=pltpu.SMEM)
PARAMS = pltpu.CompilerParams(vmem_limit_bytes=48 * 1024 * 1024)


def dft_tables():
    sample = np.arange(NLON, dtype=np.int32)[:, None]
    number = np.arange(MM, dtype=np.int32)[None, :]
    angles = (sample * number % NLON).astype(np.float32) * np.float32(2.0 * math.pi / NLON)
    norm_scale = np.float32(1.0 / math.sqrt(NLON))
    cosine = (np.cos(angles) * norm_scale).astype(ml_dtypes.bfloat16)
    sine = (-np.sin(angles) * norm_scale).astype(ml_dtypes.bfloat16)
    both = np.stack([cosine, sine], axis=1).reshape(NLON, 2, STEPS, BLOCK)
    forward = np.ascontiguousarray(both.transpose(2, 0, 1, 3)).reshape(STEPS, NLON, 2 * BLOCK)
    inverse = np.ascontiguousarray(forward.transpose(0, 2, 1))
    return forward, inverse


def iota(shape, dim):
    return lax.broadcasted_iota(jnp.int32, shape, dim)


def slot_choice(order, step):
    number = iota((BLOCK, MM), 0) + step * BLOCK
    return jnp.where(order == number, 1.0, 0.0).astype(BF16)


def slot_order(slots):
    digits = jnp.concatenate([slots // 32, slots % 32], axis=0).astype(F32).astype(BF16)
    source = iota((LANES, MM), 0)
    to = iota((LANES, MM), 1)
    choice = jnp.where(source == to % 8 * 16 + to // LANES * 2 + to // LATS % 2, 1.0, 0.0).astype(BF16)
    moved = jnp.dot(digits, choice, preferred_element_type=F32)
    row = iota((16, MM), 0)
    mine = row % 8 == iota((16, MM), 1) % LATS // 8
    value = jnp.where(mine, moved * jnp.where(row < 8, 32.0, 1.0), 0.0)
    return jnp.sum(value, axis=0, keepdims=True).astype(jnp.int32)


def kept_column(kept):
    shape = (ROWS, BAND)
    chosen = jnp.where(iota(shape, 1) == iota(shape, 0) // LEV, kept.astype(F32), 0.0)
    return jnp.sum(chosen, axis=1, keepdims=True).astype(jnp.int32)


def weight_column(weights, lat):
    shape = (ROWS, NLAT // 2)
    latitude = lat * BAND + iota(shape, 0) // LEV
    chosen = jnp.where(iota(shape, 1) == jnp.minimum(latitude, NLAT - 1 - latitude), weights, 0.0)
    return jnp.sum(chosen, axis=1, keepdims=True)


def row_choice(southern):
    to = iota((2 * ROWS, 2 * ROWS), 0)
    source = iota((2 * ROWS, 2 * ROWS), 1)
    band = to // (2 * LEV)
    band = jnp.where(southern, BAND - 1 - band, band)
    wanted = (to % 2) * ROWS + band * LEV + to // 2 % LEV
    return jnp.where(source == wanted, 1.0, 0.0).astype(BF16)


def fourier_kernel(
    lat_ref, kept_hbm, weights_hbm, slots_hbm, x_hbm, table_hbm, o_ref, order_ref, kept_v, weights_v, slots_v, x_v,
    table_v, rows, acc, sems
):
    small = [
        pltpu.make_async_copy(slots_hbm, slots_v, sems.at[0]),
        pltpu.make_async_copy(x_hbm, x_v, sems.at[1]),
        pltpu.make_async_copy(kept_hbm, kept_v, sems.at[2]),
        pltpu.make_async_copy(weights_hbm, weights_v, sems.at[3]),
    ]
    blocks = [pltpu.make_async_copy(table_hbm.at[i], table_v.at[i], sems.at[4 + i]) for i in range(STEPS)]
    for copy in small + blocks:
        copy.start()
    lat = lat_ref[0]
    small[0].wait()
    order = slot_order(slots_v[...])
    order_ref[...] = order
    small[1].wait()
    for group in range(ROWS // 16):
        rows[16 * group : 16 * group + 16, :] = jnp.concatenate(
            [x_v[4 * group + i].astype(F32) for i in range(4)], axis=0
        ).astype(BF16)
    small[2].wait()
    small[3].wait()
    kept = kept_column(kept_v[...])
    weight = weight_column(weights_v[...], lat)
    for step in range(STEPS):
        blocks[step].wait()
        raw = jnp.dot(rows[...], table_v[step], preferred_element_type=F32)
        number = iota((ROWS, BLOCK), 1) + step * BLOCK
        scale = jnp.where(number < kept, weight, 0.0)
        fourier = jnp.concatenate([raw[:, :BLOCK] * scale, raw[:, BLOCK:] * scale], axis=0).astype(BF16)
        part = jnp.dot(fourier, slot_choice(order, step), preferred_element_type=F32)
        if step == 0:
            acc[...] = part
        else:
            acc[...] += part
    choice = row_choice(lat >= NORTH)
    moved = jnp.dot(choice, acc[...].astype(BF16), preferred_element_type=F32).astype(BF16)
    for b in range(LEVS):
        o_ref[b] = moved[:, b * LANES : (b + 1) * LANES]


def gather_kernel(y_ref, o_ref, rows):
    for j in range(BAND):
        block = jnp.concatenate([y_ref[b, 8 * j : 8 * j + 8, :].astype(F32) for b in range(LEVS)], axis=0)
        turned = block.T
        rows[:, j % 4, (j // 4) * LANES : (j // 4 + 1) * LANES] = jnp.concatenate(
            [turned[:LATS], turned[LATS:]], axis=1
        )
    o_ref[...] = rows[...].astype(BF16)


def scatter_kernel(z_ref, o_ref, rows):
    rows[...] = z_ref[...].astype(F32)
    for j in range(BAND):
        block = rows[:, j % 4, (j // 4) * LANES : (j // 4 + 1) * LANES]
        turned = jnp.concatenate([block[:, :LATS], block[:, LATS:]], axis=0).T
        for b in range(LEVS):
            o_ref[b, 8 * j : 8 * j + 8, :] = turned[8 * b : 8 * b + 8].astype(BF16)
    power = jnp.sum(rows[:, :, DATA:], axis=0)
    power = jnp.concatenate([power[:, :LANES], power[:, LANES:]], axis=0)
    high = power.astype(BF16)
    both = jnp.concatenate([high.astype(F32), power - high.astype(F32)], axis=0).astype(BF16)
    for b in range(LEVS):
        o_ref[b, 2 * ROWS :, :] = both


def legendre_kernel(waves_ref, diffusion_ref, z_ref, table_ref, spectral_ref, o_ref, comb):
    for group in range(NORTH * TILES // 4):
        north, south = [], []
        for u in range(4 * group, 4 * group + 4):
            a, tile = divmod(u, TILES)
            lanes = slice(tile * LANES, (tile + 1) * LANES)
            north.append(z_ref[a, :, lanes].astype(F32))
            south.append(z_ref[LATS - 1 - a, :, lanes].astype(F32))
        north = jnp.concatenate(north, axis=0)
        south = jnp.concatenate(south, axis=0)
        comb[0, 16 * group : 16 * group + 16, :] = north + south
        comb[1, 16 * group : 16 * group + 16, :] = north - south
    column = iota((64, HALF), 1)
    power = [jnp.zeros((1, HALF), F32), jnp.zeros((1, HALF), F32)]
    halves = []
    for q in range(2):
        left = comb[q].T.astype(BF16)
        parts = []
        for t in range(2):
            wave = waves_ref[t]
            raw = jnp.dot(left[64 * t : 64 * t + 64], table_ref[t, q], preferred_element_type=F32)
            degree = wave + 2 * column + q
            spectral = jnp.where(degree < MM, raw, 0.0)
            spectral_ref[t, q] = spectral
            degree = degree.astype(F32)
            ratio = degree * (degree + 1.0) / (MM * (MM + 1.0))
            damped = (spectral / (1.0 + diffusion_ref[...] * ratio * ratio)).astype(BF16)
            parts.append(
                lax.dot_general(
                    table_ref[t, q], damped, (((1,), (1,)), ((), ())), preferred_element_type=F32
                )
            )
            energy = jnp.sum(spectral * spectral, axis=0, keepdims=True)
            first = wave + q
            moved = pltpu.roll(jnp.broadcast_to(energy, (8, HALF)), first // 2 % HALF, 1)[:1]
            for odd in range(2):
                power[odd] += jnp.where(first % 2 == odd, moved, 0.0)
        halves.append(jnp.concatenate(parts, axis=1))
    source = iota((LANES, 2 * LANES), 0)
    to = iota((LANES, 2 * LANES), 1)
    natural = jnp.zeros((8, 2 * LANES), F32)
    for odd in range(2):
        quarters = [power[odd][:, i * LANES : (i + 1) * LANES] for i in range(4)]
        quarters = jnp.concatenate(quarters + quarters, axis=0).astype(BF16)
        choice = jnp.where(to == 2 * source + odd, 1.0, 0.0).astype(BF16)
        natural += jnp.dot(quarters, choice, preferred_element_type=F32)
    natural = natural[:4].astype(BF16)
    for a in range(LATS):
        o_ref[a, :, DATA:] = natural
    north = halves[0] + halves[1]
    south = halves[0] - halves[1]
    for u in range(NORTH * TILES):
        a, tile = divmod(u, TILES)
        lanes = slice(tile * LANES, (tile + 1) * LANES)
        o_ref[a, :, lanes] = north[4 * u : 4 * u + 4].astype(BF16)
        o_ref[LATS - 1 - a, :, lanes] = south[4 * u : 4 * u + 4].astype(BF16)


def grid_kernel(lat_ref, kept_ref, order_ref, y_ref, table_ref, o_ref, spectrum_ref, acc):
    kept = kept_column(kept_ref[...])
    choice = row_choice(lat_ref[0] >= NORTH)
    back = jnp.concatenate([y_ref[b, : 2 * ROWS, :] for b in range(LEVS)], axis=1)
    rows = lax.dot_general(choice, back, (((0,), (0,)), ((), ())), preferred_element_type=F32).astype(BF16)
    for step in range(STEPS):
        numbered = lax.dot_general(
            rows, slot_choice(order_ref[...], step), (((1,), (1,)), ((), ())), preferred_element_type=F32
        )
        mask = iota((ROWS, BLOCK), 1) + step * BLOCK < kept
        coefficients = jnp.concatenate(
            [jnp.where(mask, numbered[:ROWS], 0.0), jnp.where(mask, numbered[ROWS:], 0.0)], axis=1
        ).astype(BF16)
        part = jnp.dot(coefficients, table_ref[step], preferred_element_type=F32)
        if step == 0:
            acc[...] = part
        else:
            acc[...] += part
    for j in range(BAND):
        o_ref[j] = acc[LEV * j : LEV * (j + 1), :] * math.sqrt(NLON / MM)
    power = jnp.zeros((16, LANES), F32)
    for b in range(LEVS):
        power += y_ref[b, 2 * ROWS :, :].astype(F32)
    power = power[:8] + power[8:]
    power = jnp.concatenate([power[i // 2 + 4 * (i % 2)][None] for i in range(8)], axis=0)
    degree = (iota((8, LANES), 0) * LANES + iota((8, LANES), 1)).astype(F32)
    spectrum_ref[...] = power / (2.0 * LEVELS * (degree + 1.0))


def exchange(x, axes):
    return lax.all_to_all(x, axes, split_axis=0, concat_axis=0, tiled=True)


def body(grid_fields, legendre, weights, kept_waves, slot_wavenumber, diffusion):
    forward_table, inverse_table = dft_tables()
    lat = lax.axis_index(("y", "z")).astype(jnp.int32)
    lev = lax.axis_index(("x", "core")).astype(jnp.int32)
    lat_ref = lat.reshape(1)
    waves = lax.dynamic_slice_in_dim(slot_wavenumber, (lat * LEVS + lev) * 2, 2)
    kept_row = kept_waves.reshape(1, BAND)
    chunk = (LATS, 4, DATA + 2 * LANES)

    sent, order = pl.pallas_call(
        fourier_kernel,
        in_specs=[SMEM, HBM, HBM, HBM, HBM, HBM],
        out_specs=[VMEM, VMEM],
        out_shape=[
            jax.ShapeDtypeStruct((LEVS, 2 * ROWS, LANES), BF16),
            jax.ShapeDtypeStruct((1, MM), jnp.int32),
        ],
        scratch_shapes=[
            pltpu.VMEM((1, BAND), jnp.int32),
            pltpu.VMEM((1, NLAT // 2), F32),
            pltpu.VMEM((8, LANES), jnp.int32),
            pltpu.VMEM((BAND, LEV, NLON), BF16),
            pltpu.VMEM((STEPS, NLON, 2 * BLOCK), BF16),
            pltpu.VMEM((ROWS, NLON), BF16),
            pltpu.VMEM((2 * ROWS, MM), F32),
            pltpu.SemaphoreType.DMA((4 + STEPS,)),
        ],
        compiler_params=PARAMS,
        name="fourier",
    )(
        lat_ref,
        kept_row,
        weights.reshape(1, NLAT // 2),
        slot_wavenumber.reshape(8, LANES),
        grid_fields.transpose(1, 0, 2),
        jnp.asarray(forward_table),
    )
    arrived = exchange(sent, ("x", "core"))
    gathered = pl.pallas_call(
        gather_kernel,
        in_specs=[VMEM],
        out_specs=VMEM,
        out_shape=jax.ShapeDtypeStruct((LATS, 4, DATA), BF16),
        scratch_shapes=[pltpu.VMEM((LATS, 4, DATA), F32)],
        compiler_params=PARAMS,
        name="gather",
    )(arrived)
    gathered = exchange(gathered, ("y", "z"))
    spectral, back = pl.pallas_call(
        legendre_kernel,
        in_specs=[SMEM, VMEM, VMEM, VMEM],
        out_specs=[VMEM, VMEM],
        out_shape=[
            jax.ShapeDtypeStruct((2, 2, 2 * LEVELS, HALF), F32),
            jax.ShapeDtypeStruct(chunk, BF16),
        ],
        scratch_shapes=[pltpu.VMEM((2, NLAT // 2, LANES), F32)],
        compiler_params=PARAMS,
        name="legendre",
    )(waves, jnp.repeat(diffusion, 2).reshape(2 * LEVELS, 1), gathered, legendre)
    back = exchange(back, ("y", "z"))
    scattered = pl.pallas_call(
        scatter_kernel,
        in_specs=[VMEM],
        out_specs=VMEM,
        out_shape=jax.ShapeDtypeStruct((LEVS, 2 * ROWS + 16, LANES), BF16),
        scratch_shapes=[pltpu.VMEM(chunk, F32)],
        compiler_params=PARAMS,
        name="scatter",
    )(back)
    returned = exchange(scattered, ("x", "core"))
    grid_out, spectrum = pl.pallas_call(
        grid_kernel,
        in_specs=[SMEM, VMEM, VMEM, VMEM, VMEM],
        out_specs=[VMEM, VMEM],
        out_shape=[
            jax.ShapeDtypeStruct((BAND, LEV, NLON), F32),
            jax.ShapeDtypeStruct((8, LANES), F32),
        ],
        scratch_shapes=[pltpu.VMEM((ROWS, NLON), F32)],
        compiler_params=PARAMS,
        name="grid",
    )(lat_ref, kept_row, order, returned, jnp.asarray(inverse_table))
    return (
        grid_out.transpose(1, 0, 2),
        spectral.reshape(2, 2, LEVELS, 2, HALF),
        spectrum.reshape(MM),
    )


def solution(mesh):
    fine = Mesh(mesh.devices.reshape(4, 16, 4, 2), ("y", "z", "x", "core"))
    lat, lev = ("y", "z"), ("x", "core")
    both = lat + lev
    in_specs = (P(lev, lat, None), P(both, None, None, None), P(), P(lat), P(), P())
    out_specs = (P(lev, lat, None), P(both, None, None, None, None), P())
    return jax.shard_map(body, mesh=fine, in_specs=in_specs, out_specs=out_specs, check_vma=False)
```

time: 157 us -> 125 us (0.80)
  waiting for transfers between devices: 52.5 us -> 26.8 us
  starting transfers between devices: 37.3 us -> 22.2 us
  blocking collectives: 36 us -> 50.7 us
  local copies, waits for them, and re-layouts: 9.7 us -> 5.21 us
    all_to_all x5 -> x2, waiting for transfers between devices: 52.5 us -> 26.8 us  [exchange(): return lax.all_to_all(x, axes, split_axis=0, concat_axis=0, tiled=True)]
    all_to_all x5 -> x2, starting transfers between devices: 37.3 us -> 22.2 us  [exchange(): return lax.all_to_all(x, axes, split_axis=0, concat_axis=0, tiled=True)]
    all_to_all x2, blocking collectives: 36 us -> 50.7 us  [exchange(): return lax.all_to_all(x, axes, split_axis=0, concat_axis=0, tiled=True)]
    reshape x7 -> x2, local copies, waits for them, and re-layouts: 4.68 us -> 1.94 us  [the longest x1 1.1 us: body(): spectral.reshape(2, 2, LEVELS, 2, HALF)]
  transfers between devices with their start and end apart: 5 -> 2, of which waited for: 5 -> 2; matrix products, arithmetic and copies ran while one was open for 3% -> 2% of each run, Pallas kernels for 1% -> 0%
where the time goes in v2:
time: 125 us
  blocking collectives  50.7 us (41%)
  waiting for transfers between devices  26.8 us (21%)
  starting transfers between devices  22.2 us (18%)
  Pallas kernels  19.2 us (15%)
  local copies, waits for them, and re-layouts  5.21 us (4%)
    all_to_all x2, blocking collectives, exchange(): return lax.all_to_all(x, axes, split_axis=0, concat_axis=0, tiled=True)  50.7 us
    all_to_all x2, waiting for transfers between devices, exchange(): return lax.all_to_all(x, axes, split_axis=0, concat_axis=0, tiled=True)  26.8 us
    all_to_all x2, starting transfers between devices, exchange(): return lax.all_to_all(x, axes, split_axis=0, concat_axis=0, tiled=True)  22.2 us
    pallas_call x1, Pallas kernels, body(): pl.pallas_call(grid_kernel, in_specs=[SMEM, VMEM, VMEM, VMEM, VMEM], out_...  8.42 us
    pallas_call x1, Pallas kernels, body(): pl.pallas_call(fourier_kernel, in_specs=[SMEM, HBM, HBM, HBM, HBM, HBM],...  5.49 us
  transfers between devices with their start and end apart: 2, of which 2 were waited for; matrix products, arithmetic and copies ran while one was open for 2% of the time, Pallas kernels for 0%

profile of v2, /device:TPU:1, one launch (start us, length us, event | category | flops | bytes accessed | tf_op | source)
XLA Modules:
  0.0 124.7 jit_solution(16813347267821187024)
XLA Ops:
  0.6 0.0 copy-start
  0.6 0.8 reshape.26.weights_hbm
  1.5 0.0 copy-start.1
  1.5 1.0 copy-done.1
  2.5 0.0 copy-start.2
  2.5 0.7 copy-done.2
  3.2 0.0 copy-start.3
  3.2 0.7 copy-done.3
  3.8 0.0 copy-start.5
  3.8 0.0 copy-start.4
  3.8 5.5 %fourier.1 = (bf16[8,160,128]{2,1,0:T(8,128)(2,1)S(1)}, s32[1,1024]{1,0:T(1,128)S(1)}) custom-call(s32[1]{0:T(128)} %bitcast.lat_ref, s32[1,20]{1,0:T(1,128)S(1)} %bitcast.10, f32[1,640]{1,0:T(1,128)S(1)} %reshape.26.weights_hbm, s32[8,128]{1,0:T(8,128)S(1)} %bitcast.9, bf16[20,4,2688]{2,1,0:T(4,128)(2,1)S(1)} %bitcast.8, ...), custom_call_target="tpu_custom_call" | custom-call | tf_op jit(solution)/shard_map/fourier/pallas_call | solution.py:262
  9.3 16.7 %all_to_all.20.y_ref = bf16[8,160,128]{2,1,0:T(8,128)(2,1)S(1)} all-to-all(bf16[8,160,128]{2,1,0:T(8,128)(2,1)S(1)} %get-tuple-element.10), channel_id=1, replica_groups=mesh['y'=4,'z'=16,'x'=4,'core'=2] {'x','core'}, dimensions={0} | all-to-all | bytes 655360 | tf_op jit(solution)/shard_map/all_to_all | solution.py:250
  26.1 1.5 %gather.1 = bf16[64,4,640]{2,1,0:T(4,128)(2,1)} custom-call(bf16[8,160,128]{2,1,0:T(8,128)(2,1)S(1)} %all_to_all.20.y_ref), custom_call_target="tpu_custom_call" | custom-call | tf_op jit(solution)/shard_map/gather/pallas_call | solution.py:291
  27.6 14.8 %all-to-all-start.1 = ((bf16[64,4,640]{2,1,0:T(4,128)(2,1)}), bf16[64,4,640]{2,1,0:T(4,128)(2,1)S(1)}, u32[]{:S(2)}, u32[]{:S(2)}) async-start(bf16[64,4,640]{2,1,0:T(4,128)(2,1)} %gather.1), calls=%async_computation.1 | async-start | bytes 655360 | tf_op jit(solution)/shard_map/all_to_all | solution.py:250
  42.5 0.8 dynamic_slice.3.waves_ref
  43.2 0.0 copy-done.5
  43.2 0.1 broadcast_in_dim.3
  43.3 0.1 reshape_reshape.4.diffusion_ref
  43.4 20.1 %all-to-all-done.1.z_ref = bf16[64,4,640]{2,1,0:T(4,128)(2,1)S(1)} async-done(((bf16[64,4,640]{2,1,0:T(4,128)(2,1)}), bf16[64,4,640]{2,1,0:T(4,128)(2,1)S(1)}, u32[]{:S(2)}, u32[]{:S(2)}) %all-to-all-start.1) | async-done | bytes 327712 | tf_op jit(solution)/shard_map/all_to_all | solution.py:250
  63.5 0.0 copy-done
  63.5 2.0 %legendre.1 = (f32[2,2,64,512]{3,2,1,0:T(8,128)S(1)}, bf16[64,4,896]{2,1,0:T(4,128)(2,1)S(1)}) custom-call(s32[2]{0:T(128)S(1)} %dynamic_slice.3.waves_ref, f32[64,1]{1,0:T(8,128)S(1)} %reshape_reshape.4.diffusion_ref, bf16[64,4,640]{2,1,0:T(4,128)(2,1)S(1)} %all-to-all-done.1.z_ref, bf16[2,2,640,512]{3,2,1,0:T(8,128)(2,1)S(1)} %copy-done), custom_call_target="tpu_custom_call" | custom-call | tf_op jit(solution)/shard_map/legendre/pallas_call | solution.py:301
  65.5 33.9 %all_to_all.21.z_ref = bf16[64,4,896]{2,1,0:T(4,128)(2,1)S(1)} all-to-all(bf16[64,4,896]{2,1,0:T(4,128)(2,1)S(1)} %get-tuple-element.11), channel_id=1, replica_groups=mesh['y'=4,'z'=16,'x'=4,'core'=2] {'y','z'}, dimensions={0} | all-to-all | bytes 917504 | tf_op jit(solution)/shard_map/all_to_all | solution.py:250
  99.5 1.7 %scatter.1 = bf16[8,176,128]{2,1,0:T(8,128)(2,1)} custom-call(bf16[64,4,896]{2,1,0:T(4,128)(2,1)S(1)} %all_to_all.21.z_ref), custom_call_target="tpu_custom_call" | custom-call | tf_op jit(solution)/shard_map/scatter/pallas_call | solution.py:314
  101.2 7.4 %all-to-all-start.3 = ((bf16[8,176,128]{2,1,0:T(8,128)(2,1)}), bf16[8,176,128]{2,1,0:T(8,128)(2,1)S(1)}, u32[]{:S(2)}, u32[]{:S(2)}) async-start(bf16[8,176,128]{2,1,0:T(8,128)(2,1)} %scatter.1), calls=%async_computation.3 | async-start | bytes 720896 | tf_op jit(solution)/shard_map/all_to_all | solution.py:250
  108.5 1.1 reshape.28
  109.6 6.6 %all-to-all-done.3.y_ref = bf16[8,176,128]{2,1,0:T(8,128)(2,1)S(1)} async-done(((bf16[8,176,128]{2,1,0:T(8,128)(2,1)}), bf16[8,176,128]{2,1,0:T(8,128)(2,1)S(1)}, u32[]{:S(2)}, u32[]{:S(2)}) %all-to-all-start.3) | async-done | bytes 360480 | tf_op jit(solution)/shard_map/all_to_all | solution.py:250
  116.3 0.0 copy-done.4
  116.3 8.4 %grid.1 = (f32[20,4,2688]{2,1,0:T(4,128)}, f32[8,128]{1,0:T(8,128)}) custom-call(s32[1]{0:T(128)} %bitcast.lat_ref, s32[1,20]{1,0:T(1,128)S(1)} %bitcast.11, s32[1,1024]{1,0:T(1,128)S(1)} %get-tuple-element.9.order_ref, bf16[8,176,128]{2,1,0:T(8,128)(2,1)S(1)} %all-to-all-done.3.y_ref, bf16[4,512,2688]{2,1,0:T(8,128)(2,1)} %constant.32.clone.table_ref), custom_call_target="tpu_custom_call" | custom-call | tf_op jit(solution)/shard_map/grid/pallas_call | solution.py:324
Async XLA Ops:
  0.6 62.9 %copy-start = (bf16[2,2,640,512]{3,2,1,0:T(8,128)(2,1)S(1)}, bf16[2,2,640,512]{3,2,1,0:T(8,128)(2,1)}, u32[]{:S(2)}) copy-start(bf16[2,2,640,512]{3,2,1,0:T(8,128)(2,1)} %table_ref.2) | copy-start | bytes 7864324
  1.5 1.0 copy-start.1
  2.5 0.7 copy-start.2
  3.2 0.7 copy-start.3
  3.8 39.4 %copy-start.5 = (f32[32]{0:T(128)S(1)}, f32[32]{0:T(128)}, u32[]{:S(2)}) copy-start(f32[32]{0:T(128)} %param.13) | copy-start | bytes 388
  3.8 112.4 %copy-start.4 = (s32[20]{0:T(128)S(1)}, s32[20]{0:T(128)}, u32[]{:S(2)}) copy-start(s32[20]{0:T(128)} %param.11) | copy-start | bytes 244
  27.6 35.8 %all-to-all-start.1 = ((bf16[64,4,640]{2,1,0:T(4,128)(2,1)}), bf16[64,4,640]{2,1,0:T(4,128)(2,1)S(1)}, u32[]{:S(2)}, u32[]{:S(2)}) async-start(bf16[64,4,640]{2,1,0:T(4,128)(2,1)} %gather.1), calls=%async_computation.1 | async-start | bytes 655360 | tf_op jit(solution)/shard_map/all_to_all | solution.py:250
  101.2 15.1 %all-to-all-start.3 = ((bf16[8,176,128]{2,1,0:T(8,128)(2,1)}), bf16[8,176,128]{2,1,0:T(8,128)(2,1)S(1)}, u32[]{:S(2)}, u32[]{:S(2)}) async-start(bf16[8,176,128]{2,1,0:T(8,128)(2,1)} %scatter.1), calls=%async_computation.3 | async-start | bytes 720896 | tf_op jit(solution)/shard_map/all_to_all | solution.py:250

commit v3 on v2

--- a/solution.py
+++ b/solution.py
@@ -21,6 +21,7 @@
 LATS = 64
 LEVS = 8
 NORTH = LATS // 2
+QUARTER = NLON // 4
 STEPS = 4
 BLOCK = MM // STEPS
 TILES = BAND // 4
@@ -36,14 +37,14 @@
 
 
 def dft_tables():
-    sample = np.arange(NLON, dtype=np.int32)[:, None]
+    sample = np.arange(QUARTER, dtype=np.int32)[:, None]
     number = np.arange(MM, dtype=np.int32)[None, :]
     angles = (sample * number % NLON).astype(np.float32) * np.float32(2.0 * math.pi / NLON)
     norm_scale = np.float32(1.0 / math.sqrt(NLON))
     cosine = (np.cos(angles) * norm_scale).astype(ml_dtypes.bfloat16)
     sine = (-np.sin(angles) * norm_scale).astype(ml_dtypes.bfloat16)
-    both = np.stack([cosine, sine], axis=1).reshape(NLON, 2, STEPS, BLOCK)
-    forward = np.ascontiguousarray(both.transpose(2, 0, 1, 3)).reshape(STEPS, NLON, 2 * BLOCK)
+    both = np.stack([cosine, sine], axis=1).reshape(QUARTER, 2, BLOCK, STEPS)
+    forward = np.ascontiguousarray(both.transpose(3, 0, 1, 2)).reshape(STEPS, QUARTER, 2 * BLOCK)
     inverse = np.ascontiguousarray(forward.transpose(0, 2, 1))
     return forward, inverse
 
@@ -53,7 +54,7 @@
 
 
 def slot_choice(order, step):
-    number = iota((BLOCK, MM), 0) + step * BLOCK
+    number = iota((BLOCK, MM), 0) * STEPS + step
     return jnp.where(order == number, 1.0, 0.0).astype(BF16)
 
 
@@ -69,17 +70,16 @@
     return jnp.sum(value, axis=0, keepdims=True).astype(jnp.int32)
 
 
-def kept_column(kept):
-    shape = (ROWS, BAND)
-    chosen = jnp.where(iota(shape, 1) == iota(shape, 0) // LEV, kept.astype(F32), 0.0)
-    return jnp.sum(chosen, axis=1, keepdims=True).astype(jnp.int32)
-
-
-def weight_column(weights, lat):
-    shape = (ROWS, NLAT // 2)
-    latitude = lat * BAND + iota(shape, 0) // LEV
-    chosen = jnp.where(iota(shape, 1) == jnp.minimum(latitude, NLAT - 1 - latitude), weights, 0.0)
-    return jnp.sum(chosen, axis=1, keepdims=True)
+def latitude_column(scalars, zero):
+    band = iota((ROWS, 1), 0) // LEV
+    column = jnp.full((ROWS, 1), zero)
+    for j in range(BAND):
+        column = jnp.where(band == j, scalars[j], column)
+    return column
+
+
+def class_mask(kept, step):
+    return iota((ROWS, BLOCK), 1) * STEPS + step < kept
 
 
 def row_choice(southern):
@@ -92,14 +92,14 @@
 
 
 def fourier_kernel(
-    lat_ref, kept_hbm, weights_hbm, slots_hbm, x_hbm, table_hbm, o_ref, order_ref, kept_v, weights_v, slots_v, x_v,
-    table_v, rows, acc, sems
+    lat_ref, kept_hbm, weights_hbm, slots_hbm, x_hbm, table_hbm, o_ref, order_ref, kept_ref, kept_s, weights_s, slots_v, x_v,
+    table_v, even, odd, acc, sems
 ):
     small = [
         pltpu.make_async_copy(slots_hbm, slots_v, sems.at[0]),
         pltpu.make_async_copy(x_hbm, x_v, sems.at[1]),
-        pltpu.make_async_copy(kept_hbm, kept_v, sems.at[2]),
-        pltpu.make_async_copy(weights_hbm, weights_v, sems.at[3]),
+        pltpu.make_async_copy(kept_hbm, kept_s, sems.at[2]),
+        pltpu.make_async_copy(weights_hbm, weights_s, sems.at[3]),
     ]
     blocks = [pltpu.make_async_copy(table_hbm.at[i], table_v.at[i], sems.at[4 + i]) for i in range(STEPS)]
     for copy in small + blocks:
@@ -108,21 +108,44 @@
     small[0].wait()
     order = slot_order(slots_v[...])
     order_ref[...] = order
-    small[1].wait()
-    for group in range(ROWS // 16):
-        rows[16 * group : 16 * group + 16, :] = jnp.concatenate(
-            [x_v[4 * group + i].astype(F32) for i in range(4)], axis=0
-        ).astype(BF16)
     small[2].wait()
     small[3].wait()
-    kept = kept_column(kept_v[...])
-    weight = weight_column(weights_v[...], lat)
+    kept = latitude_column([kept_s[j] for j in range(BAND)], jnp.int32(0))
+    kept_ref[...] = kept
+    latitudes = [lat * BAND + j for j in range(BAND)]
+    weight = latitude_column([weights_s[jnp.minimum(i, NLAT - 1 - i)] for i in latitudes], F32(0.0))
+    small[1].wait()
+
+    def put(ref, place, value):
+        high = value.astype(BF16)
+        low = (value - high.astype(F32)).astype(BF16)
+        for part, half in enumerate((high, low)):
+            ref[pl.ds(place + part * ROWS, 16), :] = half
+
+    for group in range(ROWS // 16):
+        x = jnp.concatenate([x_v[4 * group + i].astype(F32) for i in range(4)], axis=0)
+        x = [x[:, q * QUARTER : (q + 1) * QUARTER] for q in range(4)]
+        sums = x[0] + x[2], x[1] + x[3]
+        put(even.at[0], 16 * group, sums[0] + sums[1])
+        put(even.at[1], 16 * group, sums[0] - sums[1])
+        put(odd, 16 * group, x[0] - x[2])
+        put(odd, 16 * group + 2 * ROWS, x[1] - x[3])
     for step in range(STEPS):
         blocks[step].wait()
-        raw = jnp.dot(rows[...], table_v[step], preferred_element_type=F32)
-        number = iota((ROWS, BLOCK), 1) + step * BLOCK
-        scale = jnp.where(number < kept, weight, 0.0)
-        fourier = jnp.concatenate([raw[:, :BLOCK] * scale, raw[:, BLOCK:] * scale], axis=0).astype(BF16)
+        if step % 2 == 0:
+            raw = jnp.dot(even[step // 2], table_v[step], preferred_element_type=F32)
+            raw = raw[:ROWS] + raw[ROWS:]
+            real, imaginary = raw[:, :BLOCK], raw[:, BLOCK:]
+        else:
+            raw = jnp.dot(odd[...], table_v[step], preferred_element_type=F32)
+            first = raw[:ROWS] + raw[ROWS : 2 * ROWS]
+            second = raw[2 * ROWS : 3 * ROWS] + raw[3 * ROWS :]
+            if step == 3:
+                second = -second
+            real = first[:, :BLOCK] + second[:, BLOCK:]
+            imaginary = first[:, BLOCK:] - second[:, :BLOCK]
+        scale = jnp.where(class_mask(kept, step), weight, 0.0)
+        fourier = jnp.concatenate([real * scale, imaginary * scale], axis=0).astype(BF16)
         part = jnp.dot(fourier, slot_choice(order, step), preferred_element_type=F32)
         if step == 0:
             acc[...] = part
@@ -217,26 +240,31 @@
         o_ref[LATS - 1 - a, :, lanes] = south[4 * u : 4 * u + 4].astype(BF16)
 
 
-def grid_kernel(lat_ref, kept_ref, order_ref, y_ref, table_ref, o_ref, spectrum_ref, acc):
-    kept = kept_column(kept_ref[...])
+def grid_kernel(lat_ref, kept_ref, order_ref, y_ref, table_ref, o_ref, spectrum_ref):
+    kept = kept_ref[...]
     choice = row_choice(lat_ref[0] >= NORTH)
     back = jnp.concatenate([y_ref[b, : 2 * ROWS, :] for b in range(LEVS)], axis=1)
     rows = lax.dot_general(choice, back, (((0,), (0,)), ((), ())), preferred_element_type=F32).astype(BF16)
+    parts = []
     for step in range(STEPS):
         numbered = lax.dot_general(
             rows, slot_choice(order_ref[...], step), (((1,), (1,)), ((), ())), preferred_element_type=F32
         )
-        mask = iota((ROWS, BLOCK), 1) + step * BLOCK < kept
-        coefficients = jnp.concatenate(
-            [jnp.where(mask, numbered[:ROWS], 0.0), jnp.where(mask, numbered[ROWS:], 0.0)], axis=1
-        ).astype(BF16)
-        part = jnp.dot(coefficients, table_ref[step], preferred_element_type=F32)
-        if step == 0:
-            acc[...] = part
-        else:
-            acc[...] += part
+        mask = class_mask(kept, step)
+        real = jnp.where(mask, numbered[:ROWS], 0.0)
+        imaginary = jnp.where(mask, numbered[ROWS:], 0.0)
+        left = jnp.concatenate([real, imaginary], axis=1)
+        if step == 1:
+            left = jnp.concatenate([left, jnp.concatenate([-imaginary, real], axis=1)], axis=0)
+        if step == 3:
+            left = jnp.concatenate([left, jnp.concatenate([imaginary, -real], axis=1)], axis=0)
+        parts.append(jnp.dot(left.astype(BF16), table_ref[step], preferred_element_type=F32))
+    odd = parts[1] + parts[3]
+    plus, minus = parts[0] + parts[2], parts[0] - parts[2]
+    quarters = [plus + odd[:ROWS], minus + odd[ROWS:], plus - odd[:ROWS], minus - odd[ROWS:]]
+    points = jnp.concatenate(quarters, axis=1) * math.sqrt(NLON / MM)
     for j in range(BAND):
-        o_ref[j] = acc[LEV * j : LEV * (j + 1), :] * math.sqrt(NLON / MM)
+        o_ref[j] = points[LEV * j : LEV * (j + 1), :]
     power = jnp.zeros((16, LANES), F32)
     for b in range(LEVS):
         power += y_ref[b, 2 * ROWS :, :].astype(F32)
@@ -246,6 +274,10 @@
     spectrum_ref[...] = power / (2.0 * LEVELS * (degree + 1.0))
 
 
+def in_hbm(x):
+    return pltpu.with_memory_space_constraint(x, pltpu.HBM)
+
+
 def exchange(x, axes):
     return lax.all_to_all(x, axes, split_axis=0, concat_axis=0, tiled=True)
 
@@ -256,24 +288,25 @@
     lev = lax.axis_index(("x", "core")).astype(jnp.int32)
     lat_ref = lat.reshape(1)
     waves = lax.dynamic_slice_in_dim(slot_wavenumber, (lat * LEVS + lev) * 2, 2)
-    kept_row = kept_waves.reshape(1, BAND)
     chunk = (LATS, 4, DATA + 2 * LANES)
 
-    sent, order = pl.pallas_call(
+    sent, order, kept = pl.pallas_call(
         fourier_kernel,
         in_specs=[SMEM, HBM, HBM, HBM, HBM, HBM],
-        out_specs=[VMEM, VMEM],
+        out_specs=[VMEM, VMEM, VMEM],
         out_shape=[
             jax.ShapeDtypeStruct((LEVS, 2 * ROWS, LANES), BF16),
             jax.ShapeDtypeStruct((1, MM), jnp.int32),
+            jax.ShapeDtypeStruct((ROWS, 1), jnp.int32),
         ],
         scratch_shapes=[
-            pltpu.VMEM((1, BAND), jnp.int32),
-            pltpu.VMEM((1, NLAT // 2), F32),
+            pltpu.SMEM((BAND,), jnp.int32),
+            pltpu.SMEM((NLAT // 2,), F32),
             pltpu.VMEM((8, LANES), jnp.int32),
             pltpu.VMEM((BAND, LEV, NLON), BF16),
-            pltpu.VMEM((STEPS, NLON, 2 * BLOCK), BF16),
-            pltpu.VMEM((ROWS, NLON), BF16),
+            pltpu.VMEM((STEPS, QUARTER, 2 * BLOCK), BF16),
+            pltpu.VMEM((2, 2 * ROWS, QUARTER), BF16),
+            pltpu.VMEM((4 * ROWS, QUARTER), BF16),
             pltpu.VMEM((2 * ROWS, MM), F32),
             pltpu.SemaphoreType.DMA((4 + STEPS,)),
         ],
@@ -281,11 +314,11 @@
         name="fourier",
     )(
         lat_ref,
-        kept_row,
-        weights.reshape(1, NLAT // 2),
-        slot_wavenumber.reshape(8, LANES),
-        grid_fields.transpose(1, 0, 2),
-        jnp.asarray(forward_table),
+        in_hbm(kept_waves),
+        in_hbm(weights),
+        in_hbm(slot_wavenumber.reshape(8, LANES)),
+        in_hbm(grid_fields.transpose(1, 0, 2)),
+        in_hbm(jnp.asarray(forward_table)),
     )
     arrived = exchange(sent, ("x", "core"))
     gathered = pl.pallas_call(
@@ -329,10 +362,9 @@
             jax.ShapeDtypeStruct((BAND, LEV, NLON), F32),
             jax.ShapeDtypeStruct((8, LANES), F32),
         ],
-        scratch_shapes=[pltpu.VMEM((ROWS, NLON), F32)],
         compiler_params=PARAMS,
         name="grid",
-    )(lat_ref, kept_row, order, returned, jnp.asarray(inverse_table))
+    )(lat_ref, kept, order, returned, jnp.asarray(inverse_table))
     return (
         grid_out.transpose(1, 0, 2),
         spectral.reshape(2, 2, LEVELS, 2, HALF),

time: 125 us -> 118 us (0.944)
  Pallas kernels: 19.2 us -> 11.6 us
    pallas_call x1, Pallas kernels: 8.42 us -> 3.03 us  [body(): pl.pallas_call(grid_kernel, in_specs=[SMEM, VMEM, VMEM, VMEM, VMEM], out_...]
    pallas_call x1, Pallas kernels: 5.49 us -> 4.07 us  [body(): pl.pallas_call(fourier_kernel, in_specs=[SMEM, HBM, HBM, HBM, HBM, HBM],...]
    unnamed x12 -> x10, local copies, waits for them, and re-layouts: 2.36 us -> 3.25 us
  transfers between devices with their start and end apart: 2 -> 2, of which waited for: 2 -> 2; matrix products, arithmetic and copies ran while one was open for 2% -> 3% of each run, Pallas kernels for 0% -> 0%
where the time goes in v3:
time: 118 us; the launch traced here: 117 us
  blocking collectives  50.7 us (43%)
  waiting for transfers between devices  25.7 us (22%)
  starting transfers between devices  22.2 us (19%)
  Pallas kernels  11.6 us (10%)
  local copies, waits for them, and re-layouts  6.3 us (5%)
    all_to_all x2, blocking collectives, exchange(): return lax.all_to_all(x, axes, split_axis=0, concat_axis=0, tiled=True)  50.7 us
    all_to_all x2, waiting for transfers between devices, exchange(): return lax.all_to_all(x, axes, split_axis=0, concat_axis=0, tiled=True)  25.7 us
    all_to_all x2, starting transfers between devices, exchange(): return lax.all_to_all(x, axes, split_axis=0, concat_axis=0, tiled=True)  22.2 us
    pallas_call x1, Pallas kernels, body(): pl.pallas_call(fourier_kernel, in_specs=[SMEM, HBM, HBM, HBM, HBM, HBM],...  4.07 us
    unnamed x10, local copies, waits for them, and re-layouts  3.25 us
    pallas_call x1, Pallas kernels, body(): pl.pallas_call(grid_kernel, in_specs=[SMEM, VMEM, VMEM, VMEM, VMEM], out_...  3.03 us
  transfers between devices with their start and end apart: 2, of which 2 were waited for; matrix products, arithmetic and copies ran while one was open for 3% of the time, Pallas kernels for 0%

profile of v3, /device:TPU:1, one launch (start us, length us, event | category | flops | bytes accessed | tf_op | source)
XLA Modules:
  0.0 117.2 jit_solution(6046678796329916941)
XLA Ops:
  0.6 0.0 copy-start.4
  0.6 4.1 %fourier.1 = (bf16[8,160,128]{2,1,0:T(8,128)(2,1)S(1)}, s32[1,1024]{1,0:T(1,128)S(1)}, s32[80,1]{1,0:T(8,128)S(1)}) custom-call(s32[1]{0:T(128)} %bitcast.lat_ref, s32[20]{0:T(128)} %kept_hbm.1, f32[640]{0:T(1024)} %weights_hbm.1, s32[8,128]{1,0:T(8,128)} %bitcast.8, bf16[20,4,2688]{2,1,0:T(4,128)(2,1)} %bitcast.7, bf16[4,672,512]{2,1,0:T(8,128)(2,1)} %constant.31.clone.table_hbm), custom_call_target="tpu_custom_call" | custom-call | tf_op jit(solution)/shard_map/fourier/pallas_call | solution.py:293
  4.7 16.8 %all_to_all.20.y_ref = bf16[8,160,128]{2,1,0:T(8,128)(2,1)S(1)} all-to-all(bf16[8,160,128]{2,1,0:T(8,128)(2,1)S(1)} %get-tuple-element.12), channel_id=1, replica_groups=mesh['y'=4,'z'=16,'x'=4,'core'=2] {'x','core'}, dimensions={0} | all-to-all | bytes 655360 | tf_op jit(solution)/shard_map/all_to_all | solution.py:282
  21.5 1.5 %gather.1 = bf16[64,4,640]{2,1,0:T(4,128)(2,1)} custom-call(bf16[8,160,128]{2,1,0:T(8,128)(2,1)S(1)} %all_to_all.20.y_ref), custom_call_target="tpu_custom_call" | custom-call | tf_op jit(solution)/shard_map/gather/pallas_call | solution.py:324
  23.0 14.8 %all-to-all-start.1 = ((bf16[64,4,640]{2,1,0:T(4,128)(2,1)}), bf16[64,4,640]{2,1,0:T(4,128)(2,1)S(1)}, u32[]{:S(2)}, u32[]{:S(2)}) async-start(bf16[64,4,640]{2,1,0:T(4,128)(2,1)} %gather.1), calls=%async_computation.1 | async-start | bytes 655360 | tf_op jit(solution)/shard_map/all_to_all | solution.py:282
  37.8 0.8 dynamic_slice.3.waves_ref
  38.6 0.0 copy-done.4
  38.6 0.1 broadcast_in_dim.3
  38.7 0.1 reshape_reshape.4.diffusion_ref
  38.8 0.0 copy-start
  38.8 20.1 %all-to-all-done.1.z_ref = bf16[64,4,640]{2,1,0:T(4,128)(2,1)S(1)} async-done(((bf16[64,4,640]{2,1,0:T(4,128)(2,1)}), bf16[64,4,640]{2,1,0:T(4,128)(2,1)S(1)}, u32[]{:S(2)}, u32[]{:S(2)}) %all-to-all-start.1) | async-done | bytes 327712 | tf_op jit(solution)/shard_map/all_to_all | solution.py:282
  58.9 0.0 copy-start.1
  58.9 1.7 %copy-done.1 = bf16[2,2,640,512]{3,2,1,0:T(8,128)(2,1)S(1)} copy-done((bf16[2,2,640,512]{3,2,1,0:T(8,128)(2,1)S(1)}, bf16[2,2,640,512]{3,2,1,0:T(8,128)(2,1)}, u32[]{:S(2)}) %copy-start.1) | copy-done | bytes 2621464
  60.6 2.0 %legendre.1 = (f32[2,2,64,512]{3,2,1,0:T(8,128)S(1)}, bf16[64,4,896]{2,1,0:T(4,128)(2,1)S(1)}) custom-call(s32[2]{0:T(128)S(1)} %dynamic_slice.3.waves_ref, f32[64,1]{1,0:T(8,128)S(1)} %reshape_reshape.4.diffusion_ref, bf16[64,4,640]{2,1,0:T(4,128)(2,1)S(1)} %all-to-all-done.1.z_ref, bf16[2,2,640,512]{3,2,1,0:T(8,128)(2,1)S(1)} %copy-done.1), custom_call_target="tpu_custom_call" | custom-call | tf_op jit(solution)/shard_map/legendre/pallas_call | solution.py:334
  62.7 0.0 copy-start.3
  62.7 0.8 copy-done.3
  63.5 33.9 %all_to_all.21.z_ref = bf16[64,4,896]{2,1,0:T(4,128)(2,1)S(1)} all-to-all(bf16[64,4,896]{2,1,0:T(4,128)(2,1)S(1)} %get-tuple-element.13), channel_id=1, replica_groups=mesh['y'=4,'z'=16,'x'=4,'core'=2] {'y','z'}, dimensions={0} | all-to-all | bytes 917504 | tf_op jit(solution)/shard_map/all_to_all | solution.py:282
  97.4 1.0 scatter.1
  98.3 0.0 copy-start.2
  98.3 0.7 copy-done.2
  99.1 7.4 %all-to-all-start.3 = ((bf16[8,176,128]{2,1,0:T(8,128)(2,1)}), bf16[8,176,128]{2,1,0:T(8,128)(2,1)S(1)}, u32[]{:S(2)}, u32[]{:S(2)}) async-start(bf16[8,176,128]{2,1,0:T(8,128)(2,1)} %copy-done.2), calls=%async_computation.3 | async-start | bytes 720896 | tf_op jit(solution)/shard_map/all_to_all | solution.py:282
  106.4 2.1 %reshape.20 = f32[2,2,32,2,512]{4,3,2,1,0:T(2,128)} reshape(f32[2,2,64,512]{3,2,1,0:T(8,128)} %copy-done.3) | data formatting | bytes 1048576 | tf_op jit(solution)/shard_map/reshape | solution.py:370
  108.6 5.6 %all-to-all-done.3.y_ref = bf16[8,176,128]{2,1,0:T(8,128)(2,1)S(1)} async-done(((bf16[8,176,128]{2,1,0:T(8,128)(2,1)}), bf16[8,176,128]{2,1,0:T(8,128)(2,1)S(1)}, u32[]{:S(2)}, u32[]{:S(2)}) %all-to-all-start.3) | async-done | bytes 360480 | tf_op jit(solution)/shard_map/all_to_all | solution.py:282
  114.2 0.0 copy-done
  114.2 3.0 %grid.1 = (f32[20,4,2688]{2,1,0:T(4,128)}, f32[8,128]{1,0:T(8,128)}) custom-call(s32[1]{0:T(128)} %bitcast.lat_ref, s32[80,1]{1,0:T(8,128)S(1)} %get-tuple-element.10.kept_ref, s32[1,1024]{1,0:T(1,128)S(1)} %get-tuple-element.11.order_ref, bf16[8,176,128]{2,1,0:T(8,128)(2,1)S(1)} %all-to-all-done.3.y_ref, bf16[4,512,672]{2,1,0:T(8,128)(2,1)S(1)} %copy-done), custom_call_target="tpu_custom_call" | custom-call | tf_op jit(solution)/shard_map/grid/pallas_call | solution.py:357
Async XLA Ops:
  0.6 38.0 %copy-start.4 = (f32[32]{0:T(128)S(1)}, f32[32]{0:T(128)}, u32[]{:S(2)}) copy-start(f32[32]{0:T(128)} %param.13) | copy-start | bytes 388
  23.0 35.8 %all-to-all-start.1 = ((bf16[64,4,640]{2,1,0:T(4,128)(2,1)}), bf16[64,4,640]{2,1,0:T(4,128)(2,1)S(1)}, u32[]{:S(2)}, u32[]{:S(2)}) async-start(bf16[64,4,640]{2,1,0:T(4,128)(2,1)} %gather.1), calls=%async_computation.1 | async-start | bytes 655360 | tf_op jit(solution)/shard_map/all_to_all | solution.py:282
  38.8 75.4 %copy-start = (bf16[4,512,672]{2,1,0:T(8,128)(2,1)S(1)}, bf16[4,512,672]{2,1,0:T(8,128)(2,1)}, u32[]{:S(2)}) copy-start(bf16[4,512,672]{2,1,0:T(8,128)(2,1)} %constant.32.clone.table_ref) | copy-start | bytes 8257540
  58.9 1.7 %copy-start.1 = (bf16[2,2,640,512]{3,2,1,0:T(8,128)(2,1)S(1)}, bf16[2,2,640,512]{3,2,1,0:T(8,128)(2,1)}, u32[]{:S(2)}) copy-start(bf16[2,2,640,512]{3,2,1,0:T(8,128)(2,1)} %table_ref.2) | copy-start | bytes 7864324
  62.7 0.8 copy-start.3
  98.3 0.7 copy-start.2
  99.1 15.1 %all-to-all-start.3 = ((bf16[8,176,128]{2,1,0:T(8,128)(2,1)}), bf16[8,176,128]{2,1,0:T(8,128)(2,1)S(1)}, u32[]{:S(2)}, u32[]{:S(2)}) async-start(bf16[8,176,128]{2,1,0:T(8,128)(2,1)} %copy-done.2), calls=%async_computation.3 | async-start | bytes 720896 | tf_op jit(solution)/shard_map/all_to_all | solution.py:282

commit v4 on v3

--- a/solution.py
+++ b/solution.py
@@ -182,7 +182,15 @@
         o_ref[b, 2 * ROWS :, :] = both
 
 
-def legendre_kernel(waves_ref, diffusion_ref, z_ref, table_ref, spectral_ref, o_ref, comb):
+def legendre_kernel(
+    device_ref, slots_hbm, diffusion_hbm, z_ref, table_ref, spectral_ref, o_ref, slots_s, diffusion_s, comb, sems
+):
+    copies = [
+        pltpu.make_async_copy(slots_hbm, slots_s, sems.at[0]),
+        pltpu.make_async_copy(diffusion_hbm, diffusion_s, sems.at[1]),
+    ]
+    for copy in copies:
+        copy.start()
     for group in range(NORTH * TILES // 4):
         north, south = [], []
         for u in range(4 * group, 4 * group + 4):
@@ -194,21 +202,28 @@
         south = jnp.concatenate(south, axis=0)
         comb[0, 16 * group : 16 * group + 16, :] = north + south
         comb[1, 16 * group : 16 * group + 16, :] = north - south
-    column = iota((64, HALF), 1)
+    for copy in copies:
+        copy.wait()
+    column = iota((2 * LEVELS, HALF), 1)
+    level = iota((2 * LEVELS, 1), 0) // 2
+    diffusion = jnp.zeros((2 * LEVELS, 1), F32)
+    for i in range(LEVELS):
+        diffusion = jnp.where(level == i, diffusion_s[i], diffusion)
     power = [jnp.zeros((1, HALF), F32), jnp.zeros((1, HALF), F32)]
     halves = []
     for q in range(2):
         left = comb[q].T.astype(BF16)
         parts = []
         for t in range(2):
-            wave = waves_ref[t]
+            wave = slots_s[device_ref[0] * 2 + t]
             raw = jnp.dot(left[64 * t : 64 * t + 64], table_ref[t, q], preferred_element_type=F32)
             degree = wave + 2 * column + q
             spectral = jnp.where(degree < MM, raw, 0.0)
-            spectral_ref[t, q] = spectral
+            for level in range(LEVELS):
+                spectral_ref[t, q, level] = spectral[2 * level : 2 * level + 2]
             degree = degree.astype(F32)
             ratio = degree * (degree + 1.0) / (MM * (MM + 1.0))
-            damped = (spectral / (1.0 + diffusion_ref[...] * ratio * ratio)).astype(BF16)
+            damped = (spectral / (1.0 + diffusion * ratio * ratio)).astype(BF16)
             parts.append(
                 lax.dot_general(
                     table_ref[t, q], damped, (((1,), (1,)), ((), ())), preferred_element_type=F32
@@ -240,7 +255,10 @@
         o_ref[LATS - 1 - a, :, lanes] = south[4 * u : 4 * u + 4].astype(BF16)
 
 
-def grid_kernel(lat_ref, kept_ref, order_ref, y_ref, table_ref, o_ref, spectrum_ref):
+def grid_kernel(lat_ref, kept_ref, order_ref, y_ref, table_hbm, o_ref, spectrum_ref, table_v, sems):
+    blocks = [pltpu.make_async_copy(table_hbm.at[i], table_v.at[i], sems.at[i]) for i in range(STEPS)]
+    for copy in blocks:
+        copy.start()
     kept = kept_ref[...]
     choice = row_choice(lat_ref[0] >= NORTH)
     back = jnp.concatenate([y_ref[b, : 2 * ROWS, :] for b in range(LEVS)], axis=1)
@@ -258,7 +276,8 @@
             left = jnp.concatenate([left, jnp.concatenate([-imaginary, real], axis=1)], axis=0)
         if step == 3:
             left = jnp.concatenate([left, jnp.concatenate([imaginary, -real], axis=1)], axis=0)
-        parts.append(jnp.dot(left.astype(BF16), table_ref[step], preferred_element_type=F32))
+        blocks[step].wait()
+        parts.append(jnp.dot(left.astype(BF16), table_v[step], preferred_element_type=F32))
     odd = parts[1] + parts[3]
     plus, minus = parts[0] + parts[2], parts[0] - parts[2]
     quarters = [plus + odd[:ROWS], minus + odd[ROWS:], plus - odd[:ROWS], minus - odd[ROWS:]]
@@ -287,7 +306,6 @@
     lat = lax.axis_index(("y", "z")).astype(jnp.int32)
     lev = lax.axis_index(("x", "core")).astype(jnp.int32)
     lat_ref = lat.reshape(1)
-    waves = lax.dynamic_slice_in_dim(slot_wavenumber, (lat * LEVS + lev) * 2, 2)
     chunk = (LATS, 4, DATA + 2 * LANES)
 
     sent, order, kept = pl.pallas_call(
@@ -333,16 +351,21 @@
     gathered = exchange(gathered, ("y", "z"))
     spectral, back = pl.pallas_call(
         legendre_kernel,
-        in_specs=[SMEM, VMEM, VMEM, VMEM],
+        in_specs=[SMEM, HBM, HBM, VMEM, VMEM],
         out_specs=[VMEM, VMEM],
         out_shape=[
-            jax.ShapeDtypeStruct((2, 2, 2 * LEVELS, HALF), F32),
+            jax.ShapeDtypeStruct((2, 2, LEVELS, 2, HALF), F32),
             jax.ShapeDtypeStruct(chunk, BF16),
         ],
-        scratch_shapes=[pltpu.VMEM((2, NLAT // 2, LANES), F32)],
+        scratch_shapes=[
+            pltpu.SMEM((MM,), jnp.int32),
+            pltpu.SMEM((LEVELS,), F32),
+            pltpu.VMEM((2, NLAT // 2, LANES), F32),
+            pltpu.SemaphoreType.DMA((2,)),
+        ],
         compiler_params=PARAMS,
         name="legendre",
-    )(waves, jnp.repeat(diffusion, 2).reshape(2 * LEVELS, 1), gathered, legendre)
+    )((lat * LEVS + lev).reshape(1), in_hbm(slot_wavenumber), in_hbm(diffusion), gathered, legendre)
     back = exchange(back, ("y", "z"))
     scattered = pl.pallas_call(
         scatter_kernel,
@@ -356,18 +379,22 @@
     returned = exchange(scattered, ("x", "core"))
     grid_out, spectrum = pl.pallas_call(
         grid_kernel,
-        in_specs=[SMEM, VMEM, VMEM, VMEM, VMEM],
+        in_specs=[SMEM, VMEM, VMEM, VMEM, HBM],
         out_specs=[VMEM, VMEM],
         out_shape=[
             jax.ShapeDtypeStruct((BAND, LEV, NLON), F32),
             jax.ShapeDtypeStruct((8, LANES), F32),
         ],
+        scratch_shapes=[
+            pltpu.VMEM((STEPS, 2 * BLOCK, QUARTER), BF16),
+            pltpu.SemaphoreType.DMA((STEPS,)),
+        ],
         compiler_params=PARAMS,
         name="grid",
-    )(lat_ref, kept, order, returned, jnp.asarray(inverse_table))
+    )(lat_ref, kept, order, returned, in_hbm(jnp.asarray(inverse_table)))
     return (
         grid_out.transpose(1, 0, 2),
-        spectral.reshape(2, 2, LEVELS, 2, HALF),
+        spectral,
         spectrum.reshape(MM),
     )
 

time: 118 us -> 116 us (0.983)
  blocking collectives: 50.7 us -> 64.9 us
  starting transfers between devices: 22.2 us -> 14.8 us
  local copies, waits for them, and re-layouts: 6.3 us -> 0.01 us
  waiting for transfers between devices: 25.7 us -> 21 us
  Pallas kernels: 11.6 us -> 14.2 us
    all_to_all x2 -> x3, blocking collectives: 50.7 us -> 64.9 us  [exchange(): return lax.all_to_all(x, axes, split_axis=0, concat_axis=0, tiled=True)]
    all_to_all x2 -> x1, starting transfers between devices: 22.2 us -> 14.8 us  [exchange(): return lax.all_to_all(x, axes, split_axis=0, concat_axis=0, tiled=True)]
    all_to_all x2 -> x1, waiting for transfers between devices: 25.7 us -> 21 us  [exchange(): return lax.all_to_all(x, axes, split_axis=0, concat_axis=0, tiled=True)]
    unnamed x10 -> x2, local copies, waits for them, and re-layouts: 3.25 us -> 0.01 us
    pallas_call x2, Pallas kernels: 5.08 us -> 7.49 us  [the longest x1 4.87 us: body(): pl.pallas_call(grid_kernel, in_specs=[SMEM, VMEM, VMEM, VMEM, HBM], out_s...]
    reshape x1 -> x0, local copies, waits for them, and re-layouts: 2.14 us -> none  [body(): spectral.reshape(2, 2, LEVELS, 2, HALF)]
  transfers between devices with their start and end apart: 2 -> 1, of which waited for: 2 -> 1; matrix products, arithmetic and copies ran while one was open for 3% -> 0% of each run, Pallas kernels for 0% -> 0%
where the time goes in v4:
time: 116 us
  blocking collectives  64.9 us (56%)
  waiting for transfers between devices  21 us (18%)
  starting transfers between devices  14.8 us (13%)
  Pallas kernels  14.2 us (12%)
    all_to_all x3, blocking collectives, exchange(): return lax.all_to_all(x, axes, split_axis=0, concat_axis=0, tiled=True)  64.9 us
    all_to_all x1, waiting for transfers between devices, exchange(): return lax.all_to_all(x, axes, split_axis=0, concat_axis=0, tiled=True)  21 us
    all_to_all x1, starting transfers between devices, exchange(): return lax.all_to_all(x, axes, split_axis=0, concat_axis=0, tiled=True)  14.8 us
    pallas_call x1, Pallas kernels, body(): pl.pallas_call(grid_kernel, in_specs=[SMEM, VMEM, VMEM, VMEM, HBM], out_s...  4.87 us
    pallas_call x1, Pallas kernels, body(): pl.pallas_call(fourier_kernel, in_specs=[SMEM, HBM, HBM, HBM, HBM, HBM],...  4.23 us
    pallas_call x1, Pallas kernels, body(): pl.pallas_call(legendre_kernel, in_specs=[SMEM, HBM, HBM, VMEM, VMEM], ou...  2.62 us
  transfers between devices with their start and end apart: 1, of which 1 were waited for; matrix products, arithmetic and copies ran while one was open for 0% of the time, Pallas kernels for 0%

profile of v4, /device:TPU:1, one launch (start us, length us, event | category | flops | bytes accessed | tf_op | source)
XLA Modules:
  0.0 115.6 jit_solution(14121288732032373302)
XLA Ops:
  0.6 0.0 copy-start
  0.6 4.2 %fourier.1 = (bf16[8,160,128]{2,1,0:T(8,128)(2,1)S(1)}, s32[1,1024]{1,0:T(1,128)S(1)}, s32[80,1]{1,0:T(8,128)S(1)}) custom-call(s32[1]{0:T(128)} %bitcast.lat_ref, s32[20]{0:T(128)} %kept_hbm.1, f32[640]{0:T(1024)} %weights_hbm.1, s32[8,128]{1,0:T(8,128)} %bitcast.7, bf16[20,4,2688]{2,1,0:T(4,128)(2,1)} %bitcast.6, bf16[4,672,512]{2,1,0:T(8,128)(2,1)} %constant.27.clone.table_hbm), custom_call_target="tpu_custom_call" | custom-call | tf_op jit(solution)/shard_map/fourier/pallas_call | solution.py:311
  4.9 16.7 %all_to_all.20.y_ref = bf16[8,160,128]{2,1,0:T(8,128)(2,1)S(1)} all-to-all(bf16[8,160,128]{2,1,0:T(8,128)(2,1)S(1)} %get-tuple-element.12), channel_id=1, replica_groups=mesh['y'=4,'z'=16,'x'=4,'core'=2] {'x','core'}, dimensions={0} | all-to-all | bytes 655360 | tf_op jit(solution)/shard_map/all_to_all | solution.py:301
  21.6 1.5 %gather.1 = bf16[64,4,640]{2,1,0:T(4,128)(2,1)} custom-call(bf16[8,160,128]{2,1,0:T(8,128)(2,1)S(1)} %all_to_all.20.y_ref), custom_call_target="tpu_custom_call" | custom-call | tf_op jit(solution)/shard_map/gather/pallas_call | solution.py:342
  23.2 14.8 %all-to-all-start.1 = ((bf16[64,4,640]{2,1,0:T(4,128)(2,1)}), bf16[64,4,640]{2,1,0:T(4,128)(2,1)S(1)}, u32[]{:S(2)}, u32[]{:S(2)}) async-start(bf16[64,4,640]{2,1,0:T(4,128)(2,1)} %gather.1), calls=%async_computation.1 | async-start | bytes 655360 | tf_op jit(solution)/shard_map/all_to_all | solution.py:301
  38.0 21.0 %all-to-all-done.1.z_ref = bf16[64,4,640]{2,1,0:T(4,128)(2,1)S(1)} async-done(((bf16[64,4,640]{2,1,0:T(4,128)(2,1)}), bf16[64,4,640]{2,1,0:T(4,128)(2,1)S(1)}, u32[]{:S(2)}, u32[]{:S(2)}) %all-to-all-start.1) | async-done | bytes 327712 | tf_op jit(solution)/shard_map/all_to_all | solution.py:301
  59.0 0.0 copy-done
  59.0 2.6 %legendre.1 = (f32[2,2,32,2,512]{4,3,2,1,0:T(2,128)}, bf16[64,4,896]{2,1,0:T(4,128)(2,1)S(1)}) custom-call(s32[1]{0:T(128)} %bitcast.3.device_ref, s32[1024]{0:T(1024)} %slots_hbm.1, f32[32]{0:T(128)} %diffusion_hbm.1, bf16[64,4,640]{2,1,0:T(4,128)(2,1)S(1)} %all-to-all-done.1.z_ref, bf16[2,2,640,512]{3,2,1,0:T(8,128)(2,1)S(1)} %copy-done), custom_call_target="tpu_custom_call" | custom-call | tf_op jit(solution)/shard_map/legendre/pallas_call | solution.py:352
  61.7 33.9 %all_to_all.21.z_ref = bf16[64,4,896]{2,1,0:T(4,128)(2,1)S(1)} all-to-all(bf16[64,4,896]{2,1,0:T(4,128)(2,1)S(1)} %get-tuple-element.13), channel_id=1, replica_groups=mesh['y'=4,'z'=16,'x'=4,'core'=2] {'y','z'}, dimensions={0} | all-to-all | bytes 917504 | tf_op jit(solution)/shard_map/all_to_all | solution.py:301
  95.6 1.0 scatter.1
  96.5 14.2 %all_to_all.22.y_ref = bf16[8,176,128]{2,1,0:T(8,128)(2,1)S(1)} all-to-all(bf16[8,176,128]{2,1,0:T(8,128)(2,1)S(1)} %scatter.1), channel_id=1, replica_groups=mesh['y'=4,'z'=16,'x'=4,'core'=2] {'x','core'}, dimensions={0} | all-to-all | bytes 720896 | tf_op jit(solution)/shard_map/all_to_all | solution.py:301
  110.7 4.9 %grid.1 = (f32[20,4,2688]{2,1,0:T(4,128)}, f32[8,128]{1,0:T(8,128)}) custom-call(s32[1]{0:T(128)} %bitcast.lat_ref, s32[80,1]{1,0:T(8,128)S(1)} %get-tuple-element.10.kept_ref, s32[1,1024]{1,0:T(1,128)S(1)} %get-tuple-element.11.order_ref, bf16[8,176,128]{2,1,0:T(8,128)(2,1)S(1)} %all_to_all.22.y_ref, bf16[4,512,672]{2,1,0:T(8,128)(2,1)} %constant.28.clone.table_hbm), custom_call_target="tpu_custom_call" | custom-call | tf_op jit(solution)/shard_map/grid/pallas_call | solution.py:380
Async XLA Ops:
  0.6 58.4 %copy-start = (bf16[2,2,640,512]{3,2,1,0:T(8,128)(2,1)S(1)}, bf16[2,2,640,512]{3,2,1,0:T(8,128)(2,1)}, u32[]{:S(2)}) copy-start(bf16[2,2,640,512]{3,2,1,0:T(8,128)(2,1)} %table_ref.1) | copy-start | bytes 7864324
  23.2 35.8 %all-to-all-start.1 = ((bf16[64,4,640]{2,1,0:T(4,128)(2,1)}), bf16[64,4,640]{2,1,0:T(4,128)(2,1)S(1)}, u32[]{:S(2)}, u32[]{:S(2)}) async-start(bf16[64,4,640]{2,1,0:T(4,128)(2,1)} %gather.1), calls=%async_computation.1 | async-start | bytes 655360 | tf_op jit(solution)/shard_map/all_to_all | solution.py:301

commit v5 on v4

--- a/solution.py
+++ b/solution.py
@@ -20,6 +20,8 @@
 ROWS = BAND * LEV
 LATS = 64
 LEVS = 8
+YS = 4
+ZS = 16
 NORTH = LATS // 2
 QUARTER = NLON // 4
 STEPS = 4
@@ -169,27 +171,44 @@
 
 def scatter_kernel(z_ref, o_ref, rows):
     rows[...] = z_ref[...].astype(F32)
-    for j in range(BAND):
-        block = rows[:, j % 4, (j // 4) * LANES : (j // 4 + 1) * LANES]
-        turned = jnp.concatenate([block[:, :LATS], block[:, LATS:]], axis=0).T
-        for b in range(LEVS):
-            o_ref[b, 8 * j : 8 * j + 8, :] = turned[8 * b : 8 * b + 8].astype(BF16)
-    power = jnp.sum(rows[:, :, DATA:], axis=0)
+    for y in range(YS):
+        for j in range(TILES):
+            block = []
+            for part in range(4):
+                row, tile = (part * TILES + j) % 4, y * TILES + (part * TILES + j) // 4
+                block.append(rows[:, row, tile * LANES : (tile + 1) * LANES])
+            block = jnp.concatenate(block, axis=0)
+            turned = jnp.concatenate([block[:, :LATS], block[:, LATS:]], axis=0).T
+            for b in range(LEVS):
+                o_ref[y * LEVS + b, 16 + 8 * j : 24 + 8 * j, :] = turned[8 * b : 8 * b + 8].astype(BF16)
+    power = jnp.sum(rows[:, :, YS * DATA :], axis=0)
     power = jnp.concatenate([power[:, :LANES], power[:, LANES:]], axis=0)
     high = power.astype(BF16)
     both = jnp.concatenate([high.astype(F32), power - high.astype(F32)], axis=0).astype(BF16)
-    for b in range(LEVS):
-        o_ref[b, 2 * ROWS :, :] = both
+    for peer in range(YS * LEVS):
+        o_ref[peer, :16, :] = both
+
+
+def swap_lanes(even, odd, width):
+    high = iota(even.shape, 1) // width % 2 == 1
+    return (
+        jnp.where(high, pltpu.roll(odd, width, 1), even),
+        jnp.where(high, odd, pltpu.roll(even, LANES - width, 1)),
+    )
 
 
 def legendre_kernel(
-    device_ref, slots_hbm, diffusion_hbm, z_ref, table_ref, spectral_ref, o_ref, slots_s, diffusion_s, comb, sems
+    device_ref, slots_hbm, diffusion_hbm, z_ref, table_hbm, spectral_ref, o_ref, slots_s, diffusion_s, table_v, comb, sems
 ):
     copies = [
         pltpu.make_async_copy(slots_hbm, slots_s, sems.at[0]),
         pltpu.make_async_copy(diffusion_hbm, diffusion_s, sems.at[1]),
     ]
-    for copy in copies:
+    tables = [
+        [pltpu.make_async_copy(table_hbm.at[t, q], table_v.at[t, q], sems.at[2 + 2 * t + q]) for t in range(2)]
+        for q in range(2)
+    ]
+    for copy in copies + tables[0] + tables[1]:
         copy.start()
     for group in range(NORTH * TILES // 4):
         north, south = [], []
@@ -215,8 +234,9 @@
         left = comb[q].T.astype(BF16)
         parts = []
         for t in range(2):
+            tables[q][t].wait()
             wave = slots_s[device_ref[0] * 2 + t]
-            raw = jnp.dot(left[64 * t : 64 * t + 64], table_ref[t, q], preferred_element_type=F32)
+            raw = jnp.dot(left[64 * t : 64 * t + 64], table_v[t, q], preferred_element_type=F32)
             degree = wave + 2 * column + q
             spectral = jnp.where(degree < MM, raw, 0.0)
             for level in range(LEVELS):
@@ -226,7 +246,7 @@
             damped = (spectral / (1.0 + diffusion * ratio * ratio)).astype(BF16)
             parts.append(
                 lax.dot_general(
-                    table_ref[t, q], damped, (((1,), (1,)), ((), ())), preferred_element_type=F32
+                    table_v[t, q], damped, (((1,), (1,)), ((), ())), preferred_element_type=F32
                 )
             )
             energy = jnp.sum(spectral * spectral, axis=0, keepdims=True)
@@ -244,24 +264,28 @@
         choice = jnp.where(to == 2 * source + odd, 1.0, 0.0).astype(BF16)
         natural += jnp.dot(quarters, choice, preferred_element_type=F32)
     natural = natural[:4].astype(BF16)
-    for a in range(LATS):
-        o_ref[a, :, DATA:] = natural
-    north = halves[0] + halves[1]
-    south = halves[0] - halves[1]
-    for u in range(NORTH * TILES):
-        a, tile = divmod(u, TILES)
-        lanes = slice(tile * LANES, (tile + 1) * LANES)
-        o_ref[a, :, lanes] = north[4 * u : 4 * u + 4].astype(BF16)
-        o_ref[LATS - 1 - a, :, lanes] = south[4 * u : 4 * u + 4].astype(BF16)
-
-
-def grid_kernel(lat_ref, kept_ref, order_ref, y_ref, table_hbm, o_ref, spectrum_ref, table_v, sems):
-    blocks = [pltpu.make_async_copy(table_hbm.at[i], table_v.at[i], sems.at[i]) for i in range(STEPS)]
-    for copy in blocks:
-        copy.start()
+    for z in range(ZS):
+        o_ref[z, :, YS * DATA :] = natural
+    for half, side in enumerate((halves[0] + halves[1], halves[0] - halves[1])):
+        for u in range(NORTH * TILES):
+            a, tile = divmod(u, TILES)
+            y, z = divmod(LATS - 1 - a if half else a, ZS)
+            place = (y * TILES + tile) * LANES
+            o_ref[z, :, place : place + LANES] = side[4 * u : 4 * u + 4].astype(BF16)
+
+
+def grid_kernel(lat_ref, kept_ref, order_ref, y_ref, table_ref, o_ref, spectrum_ref):
     kept = kept_ref[...]
     choice = row_choice(lat_ref[0] >= NORTH)
-    back = jnp.concatenate([y_ref[b, : 2 * ROWS, :] for b in range(LEVS)], axis=1)
+    back = []
+    for b in range(LEVS):
+        parts = [y_ref[y * LEVS + b, 16:, :].astype(F32) for y in range(YS)]
+        parts[0], parts[1] = swap_lanes(parts[0], parts[1], ZS)
+        parts[2], parts[3] = swap_lanes(parts[2], parts[3], ZS)
+        parts[0], parts[2] = swap_lanes(parts[0], parts[2], 2 * ZS)
+        parts[1], parts[3] = swap_lanes(parts[1], parts[3], 2 * ZS)
+        back.append(jnp.concatenate(parts, axis=0).astype(BF16))
+    back = jnp.concatenate(back, axis=1)
     rows = lax.dot_general(choice, back, (((0,), (0,)), ((), ())), preferred_element_type=F32).astype(BF16)
     parts = []
     for step in range(STEPS):
@@ -276,8 +300,7 @@
             left = jnp.concatenate([left, jnp.concatenate([-imaginary, real], axis=1)], axis=0)
         if step == 3:
             left = jnp.concatenate([left, jnp.concatenate([imaginary, -real], axis=1)], axis=0)
-        blocks[step].wait()
-        parts.append(jnp.dot(left.astype(BF16), table_v[step], preferred_element_type=F32))
+        parts.append(jnp.dot(left.astype(BF16), table_ref[step], preferred_element_type=F32))
     odd = parts[1] + parts[3]
     plus, minus = parts[0] + parts[2], parts[0] - parts[2]
     quarters = [plus + odd[:ROWS], minus + odd[ROWS:], plus - odd[:ROWS], minus - odd[ROWS:]]
@@ -285,8 +308,8 @@
     for j in range(BAND):
         o_ref[j] = points[LEV * j : LEV * (j + 1), :]
     power = jnp.zeros((16, LANES), F32)
-    for b in range(LEVS):
-        power += y_ref[b, 2 * ROWS :, :].astype(F32)
+    for peer in range(YS * LEVS):
+        power += y_ref[peer, :16, :].astype(F32)
     power = power[:8] + power[8:]
     power = jnp.concatenate([power[i // 2 + 4 * (i % 2)][None] for i in range(8)], axis=0)
     degree = (iota((8, LANES), 0) * LANES + iota((8, LANES), 1)).astype(F32)
@@ -306,7 +329,7 @@
     lat = lax.axis_index(("y", "z")).astype(jnp.int32)
     lev = lax.axis_index(("x", "core")).astype(jnp.int32)
     lat_ref = lat.reshape(1)
-    chunk = (LATS, 4, DATA + 2 * LANES)
+    chunk = (ZS, 4, YS * DATA + 2 * LANES)
 
     sent, order, kept = pl.pallas_call(
         fourier_kernel,
@@ -351,7 +374,7 @@
     gathered = exchange(gathered, ("y", "z"))
     spectral, back = pl.pallas_call(
         legendre_kernel,
-        in_specs=[SMEM, HBM, HBM, VMEM, VMEM],
+        in_specs=[SMEM, HBM, HBM, VMEM, HBM],
         out_specs=[VMEM, VMEM],
         out_shape=[
             jax.ShapeDtypeStruct((2, 2, LEVELS, 2, HALF), F32),
@@ -360,38 +383,35 @@
         scratch_shapes=[
             pltpu.SMEM((MM,), jnp.int32),
             pltpu.SMEM((LEVELS,), F32),
+            pltpu.VMEM((2, 2, NLAT // 2, HALF), BF16),
             pltpu.VMEM((2, NLAT // 2, LANES), F32),
-            pltpu.SemaphoreType.DMA((2,)),
+            pltpu.SemaphoreType.DMA((6,)),
         ],
         compiler_params=PARAMS,
         name="legendre",
-    )((lat * LEVS + lev).reshape(1), in_hbm(slot_wavenumber), in_hbm(diffusion), gathered, legendre)
-    back = exchange(back, ("y", "z"))
+    )((lat * LEVS + lev).reshape(1), in_hbm(slot_wavenumber), in_hbm(diffusion), gathered, in_hbm(legendre))
+    back = exchange(back, ("z",))
     scattered = pl.pallas_call(
         scatter_kernel,
         in_specs=[VMEM],
         out_specs=VMEM,
-        out_shape=jax.ShapeDtypeStruct((LEVS, 2 * ROWS + 16, LANES), BF16),
+        out_shape=jax.ShapeDtypeStruct((YS * LEVS, 16 + 2 * ROWS // YS, LANES), BF16),
         scratch_shapes=[pltpu.VMEM(chunk, F32)],
         compiler_params=PARAMS,
         name="scatter",
     )(back)
-    returned = exchange(scattered, ("x", "core"))
+    returned = exchange(scattered, ("y", "x", "core"))
     grid_out, spectrum = pl.pallas_call(
         grid_kernel,
-        in_specs=[SMEM, VMEM, VMEM, VMEM, HBM],
+        in_specs=[SMEM, VMEM, VMEM, VMEM, VMEM],
         out_specs=[VMEM, VMEM],
         out_shape=[
             jax.ShapeDtypeStruct((BAND, LEV, NLON), F32),
             jax.ShapeDtypeStruct((8, LANES), F32),
         ],
-        scratch_shapes=[
-            pltpu.VMEM((STEPS, 2 * BLOCK, QUARTER), BF16),
-            pltpu.SemaphoreType.DMA((STEPS,)),
-        ],
         compiler_params=PARAMS,
         name="grid",
-    )(lat_ref, kept, order, returned, in_hbm(jnp.asarray(inverse_table)))
+    )(lat_ref, kept, order, returned, jnp.asarray(inverse_table))
     return (
         grid_out.transpose(1, 0, 2),
         spectral,

time: 116 us -> 111 us (0.957)
  blocking collectives: 64.9 us -> 60.3 us
    all_to_all x3, blocking collectives: 64.9 us -> 60.3 us  [exchange(): return lax.all_to_all(x, axes, split_axis=0, concat_axis=0, tiled=True)]
where the time goes in v5:
time: 111 us
  blocking collectives  60.3 us (54%)
  waiting for transfers between devices  21 us (19%)
  starting transfers between devices  14.8 us (13%)
  Pallas kernels  14.1 us (13%)
    all_to_all x3, blocking collectives, exchange(): return lax.all_to_all(x, axes, split_axis=0, concat_axis=0, tiled=True)  60.3 us
    all_to_all x1, waiting for transfers between devices, exchange(): return lax.all_to_all(x, axes, split_axis=0, concat_axis=0, tiled=True)  21 us
    all_to_all x1, starting transfers between devices, exchange(): return lax.all_to_all(x, axes, split_axis=0, concat_axis=0, tiled=True)  14.8 us
    pallas_call x1, Pallas kernels, body(): pl.pallas_call(legendre_kernel, in_specs=[SMEM, HBM, HBM, VMEM, HBM], out...  4.41 us
    pallas_call x1, Pallas kernels, body(): pl.pallas_call(fourier_kernel, in_specs=[SMEM, HBM, HBM, HBM, HBM, HBM],...  4.07 us
    pallas_call x1, Pallas kernels, body(): pl.pallas_call(grid_kernel, in_specs=[SMEM, VMEM, VMEM, VMEM, VMEM], out_...  3.23 us
  transfers between devices with their start and end apart: 1, of which 1 were waited for; matrix products, arithmetic and copies ran while one was open for 0% of the time, Pallas kernels for 0%

profile of v5, /device:TPU:1, one launch (start us, length us, event | category | flops | bytes accessed | tf_op | source)
XLA Modules:
  0.0 110.9 jit_solution(12269454492714555)
XLA Ops:
  0.6 4.1 %fourier.1 = (bf16[8,160,128]{2,1,0:T(8,128)(2,1)S(1)}, s32[1,1024]{1,0:T(1,128)S(1)}, s32[80,1]{1,0:T(8,128)S(1)}) custom-call(s32[1]{0:T(128)} %bitcast.lat_ref, s32[20]{0:T(128)} %kept_hbm.1, f32[640]{0:T(1024)} %weights_hbm.1, s32[8,128]{1,0:T(8,128)} %bitcast.7, bf16[20,4,2688]{2,1,0:T(4,128)(2,1)} %bitcast.6, bf16[4,672,512]{2,1,0:T(8,128)(2,1)} %constant.27.clone.table_hbm), custom_call_target="tpu_custom_call" | custom-call | tf_op jit(solution)/shard_map/fourier/pallas_call | solution.py:334
  4.7 16.7 %all_to_all.20.y_ref = bf16[8,160,128]{2,1,0:T(8,128)(2,1)S(1)} all-to-all(bf16[8,160,128]{2,1,0:T(8,128)(2,1)S(1)} %get-tuple-element.12), channel_id=1, replica_groups=mesh['y'=4,'z'=16,'x'=4,'core'=2] {'x','core'}, dimensions={0} | all-to-all | bytes 655360 | tf_op jit(solution)/shard_map/all_to_all | solution.py:324
  21.5 1.5 %gather.1 = bf16[64,4,640]{2,1,0:T(4,128)(2,1)} custom-call(bf16[8,160,128]{2,1,0:T(8,128)(2,1)S(1)} %all_to_all.20.y_ref), custom_call_target="tpu_custom_call" | custom-call | tf_op jit(solution)/shard_map/gather/pallas_call | solution.py:365
  23.0 14.8 %all-to-all-start.1 = ((bf16[64,4,640]{2,1,0:T(4,128)(2,1)}), bf16[64,4,640]{2,1,0:T(4,128)(2,1)S(1)}, u32[]{:S(2)}, u32[]{:S(2)}) async-start(bf16[64,4,640]{2,1,0:T(4,128)(2,1)} %gather.1), calls=%async_computation.1 | async-start | bytes 655360 | tf_op jit(solution)/shard_map/all_to_all | solution.py:324
  37.8 0.0 copy-start
  37.8 21.0 %all-to-all-done.1.z_ref = bf16[64,4,640]{2,1,0:T(4,128)(2,1)S(1)} async-done(((bf16[64,4,640]{2,1,0:T(4,128)(2,1)}), bf16[64,4,640]{2,1,0:T(4,128)(2,1)S(1)}, u32[]{:S(2)}, u32[]{:S(2)}) %all-to-all-start.1) | async-done | bytes 327712 | tf_op jit(solution)/shard_map/all_to_all | solution.py:324
  58.9 4.4 %legendre.1 = (f32[2,2,32,2,512]{4,3,2,1,0:T(2,128)}, bf16[16,4,2816]{2,1,0:T(4,128)(2,1)S(1)}) custom-call(s32[1]{0:T(128)} %bitcast.3.device_ref, s32[1024]{0:T(1024)} %slots_hbm.1, f32[32]{0:T(128)} %diffusion_hbm.1, bf16[64,4,640]{2,1,0:T(4,128)(2,1)S(1)} %all-to-all-done.1.z_ref, bf16[2,2,640,512]{3,2,1,0:T(8,128)(2,1)} %table_hbm.2), custom_call_target="tpu_custom_call" | custom-call | tf_op jit(solution)/shard_map/legendre/pallas_call | solution.py:375
  63.3 21.6 %all_to_all.21.z_ref = bf16[16,4,2816]{2,1,0:T(4,128)(2,1)S(1)} all-to-all(bf16[16,4,2816]{2,1,0:T(4,128)(2,1)S(1)} %get-tuple-element.13), channel_id=1, replica_groups=mesh['y'=4,'z'=16,'x'=4,'core'=2] {'z'}, dimensions={0} | all-to-all | bytes 720896 | tf_op jit(solution)/shard_map/all_to_all | solution.py:324
  84.9 0.9 scatter.1
  85.8 21.9 %all_to_all.22.y_ref = bf16[32,56,128]{2,1,0:T(8,128)(2,1)S(1)} all-to-all(bf16[32,56,128]{2,1,0:T(8,128)(2,1)S(1)} %scatter.1), channel_id=1, replica_groups=mesh['y'=4,'z'=16,'x'=4,'core'=2] {'y','x','core'}, dimensions={0} | all-to-all | bytes 917504 | tf_op jit(solution)/shard_map/all_to_all | solution.py:324
  107.7 0.0 copy-done
  107.7 3.2 %grid.1 = (f32[20,4,2688]{2,1,0:T(4,128)}, f32[8,128]{1,0:T(8,128)}) custom-call(s32[1]{0:T(128)} %bitcast.lat_ref, s32[80,1]{1,0:T(8,128)S(1)} %get-tuple-element.10.kept_ref, s32[1,1024]{1,0:T(1,128)S(1)} %get-tuple-element.11.order_ref, bf16[32,56,128]{2,1,0:T(8,128)(2,1)S(1)} %all_to_all.22.y_ref, bf16[4,512,672]{2,1,0:T(8,128)(2,1)S(1)} %copy-done), custom_call_target="tpu_custom_call" | custom-call | tf_op jit(solution)/shard_map/grid/pallas_call | solution.py:404
Async XLA Ops:
  23.0 35.8 %all-to-all-start.1 = ((bf16[64,4,640]{2,1,0:T(4,128)(2,1)}), bf16[64,4,640]{2,1,0:T(4,128)(2,1)S(1)}, u32[]{:S(2)}, u32[]{:S(2)}) async-start(bf16[64,4,640]{2,1,0:T(4,128)(2,1)} %gather.1), calls=%async_computation.1 | async-start | bytes 655360 | tf_op jit(solution)/shard_map/all_to_all | solution.py:324
  37.8 69.9 %copy-start = (bf16[4,512,672]{2,1,0:T(8,128)(2,1)S(1)}, bf16[4,512,672]{2,1,0:T(8,128)(2,1)}, u32[]{:S(2)}) copy-start(bf16[4,512,672]{2,1,0:T(8,128)(2,1)} %constant.28.clone.table_ref) | copy-start | bytes 8257540

commit v6 on v5

--- a/solution.py
+++ b/solution.py
@@ -35,7 +35,7 @@
 VMEM = pl.BlockSpec(memory_space=pltpu.VMEM)
 HBM = pl.BlockSpec(memory_space=pltpu.HBM)
 SMEM = pl.BlockSpec(memory_space=pltpu.SMEM)
-PARAMS = pltpu.CompilerParams(vmem_limit_bytes=48 * 1024 * 1024)
+PARAMS = pltpu.CompilerParams(vmem_limit_bytes=20 * 1024 * 1024)
 
 
 def dft_tables():
@@ -94,7 +94,7 @@
 
 
 def fourier_kernel(
-    lat_ref, kept_hbm, weights_hbm, slots_hbm, x_hbm, table_hbm, o_ref, order_ref, kept_ref, kept_s, weights_s, slots_v, x_v,
+    device_ref, kept_hbm, weights_hbm, slots_hbm, x_hbm, table_hbm, later_hbm, o_ref, order_ref, kept_ref, later_ref, kept_s, weights_s, slots_v, x_v,
     table_v, even, odd, acc, sems
 ):
     small = [
@@ -104,9 +104,10 @@
         pltpu.make_async_copy(weights_hbm, weights_s, sems.at[3]),
     ]
     blocks = [pltpu.make_async_copy(table_hbm.at[i], table_v.at[i], sems.at[4 + i]) for i in range(STEPS)]
-    for copy in small + blocks:
+    later = pltpu.make_async_copy(later_hbm, later_ref, sems.at[4 + STEPS])
+    for copy in small + blocks + [later]:
         copy.start()
-    lat = lat_ref[0]
+    lat = device_ref[0] // LEVS
     small[0].wait()
     order = slot_order(slots_v[...])
     order_ref[...] = order
@@ -157,6 +158,7 @@
     moved = jnp.dot(choice, acc[...].astype(BF16), preferred_element_type=F32).astype(BF16)
     for b in range(LEVS):
         o_ref[b] = moved[:, b * LANES : (b + 1) * LANES]
+    later.wait()
 
 
 def gather_kernel(y_ref, o_ref, rows):
@@ -198,17 +200,15 @@
 
 
 def legendre_kernel(
-    device_ref, slots_hbm, diffusion_hbm, z_ref, table_hbm, spectral_ref, o_ref, slots_s, diffusion_s, table_v, comb, sems
+    device_ref, slots_hbm, diffusion_hbm, z_ref, table_ref, later_hbm, spectral_ref, o_ref, later_ref, slots_s, diffusion_s,
+    comb, sems
 ):
     copies = [
         pltpu.make_async_copy(slots_hbm, slots_s, sems.at[0]),
         pltpu.make_async_copy(diffusion_hbm, diffusion_s, sems.at[1]),
     ]
-    tables = [
-        [pltpu.make_async_copy(table_hbm.at[t, q], table_v.at[t, q], sems.at[2 + 2 * t + q]) for t in range(2)]
-        for q in range(2)
-    ]
-    for copy in copies + tables[0] + tables[1]:
+    later = pltpu.make_async_copy(later_hbm, later_ref, sems.at[2])
+    for copy in copies + [later]:
         copy.start()
     for group in range(NORTH * TILES // 4):
         north, south = [], []
@@ -234,9 +234,8 @@
         left = comb[q].T.astype(BF16)
         parts = []
         for t in range(2):
-            tables[q][t].wait()
             wave = slots_s[device_ref[0] * 2 + t]
-            raw = jnp.dot(left[64 * t : 64 * t + 64], table_v[t, q], preferred_element_type=F32)
+            raw = jnp.dot(left[64 * t : 64 * t + 64], table_ref[t, q], preferred_element_type=F32)
             degree = wave + 2 * column + q
             spectral = jnp.where(degree < MM, raw, 0.0)
             for level in range(LEVELS):
@@ -246,7 +245,7 @@
             damped = (spectral / (1.0 + diffusion * ratio * ratio)).astype(BF16)
             parts.append(
                 lax.dot_general(
-                    table_v[t, q], damped, (((1,), (1,)), ((), ())), preferred_element_type=F32
+                    table_ref[t, q], damped, (((1,), (1,)), ((), ())), preferred_element_type=F32
                 )
             )
             energy = jnp.sum(spectral * spectral, axis=0, keepdims=True)
@@ -272,11 +271,12 @@
             y, z = divmod(LATS - 1 - a if half else a, ZS)
             place = (y * TILES + tile) * LANES
             o_ref[z, :, place : place + LANES] = side[4 * u : 4 * u + 4].astype(BF16)
-
-
-def grid_kernel(lat_ref, kept_ref, order_ref, y_ref, table_ref, o_ref, spectrum_ref):
+    later.wait()
+
+
+def grid_kernel(device_ref, kept_ref, order_ref, y_ref, table_ref, o_ref, spectrum_ref):
     kept = kept_ref[...]
-    choice = row_choice(lat_ref[0] >= NORTH)
+    choice = row_choice(device_ref[0] >= NORTH * LEVS)
     back = []
     for b in range(LEVS):
         parts = [y_ref[y * LEVS + b, 16:, :].astype(F32) for y in range(YS)]
@@ -320,25 +320,28 @@
     return pltpu.with_memory_space_constraint(x, pltpu.HBM)
 
 
+def in_vmem(x):
+    return pltpu.with_memory_space_constraint(x, pltpu.VMEM)
+
+
 def exchange(x, axes):
     return lax.all_to_all(x, axes, split_axis=0, concat_axis=0, tiled=True)
 
 
 def body(grid_fields, legendre, weights, kept_waves, slot_wavenumber, diffusion):
     forward_table, inverse_table = dft_tables()
-    lat = lax.axis_index(("y", "z")).astype(jnp.int32)
-    lev = lax.axis_index(("x", "core")).astype(jnp.int32)
-    lat_ref = lat.reshape(1)
+    device = lax.axis_index(("y", "z", "x", "core")).astype(jnp.int32).reshape(1)
     chunk = (ZS, 4, YS * DATA + 2 * LANES)
 
-    sent, order, kept = pl.pallas_call(
+    sent, order, kept, legendre = pl.pallas_call(
         fourier_kernel,
-        in_specs=[SMEM, HBM, HBM, HBM, HBM, HBM],
-        out_specs=[VMEM, VMEM, VMEM],
+        in_specs=[SMEM, HBM, HBM, HBM, HBM, HBM, HBM],
+        out_specs=[VMEM, VMEM, VMEM, VMEM],
         out_shape=[
             jax.ShapeDtypeStruct((LEVS, 2 * ROWS, LANES), BF16),
             jax.ShapeDtypeStruct((1, MM), jnp.int32),
             jax.ShapeDtypeStruct((ROWS, 1), jnp.int32),
+            pltpu.VMEM(legendre.shape, BF16),
         ],
         scratch_shapes=[
             pltpu.SMEM((BAND,), jnp.int32),
@@ -349,17 +352,18 @@
             pltpu.VMEM((2, 2 * ROWS, QUARTER), BF16),
             pltpu.VMEM((4 * ROWS, QUARTER), BF16),
             pltpu.VMEM((2 * ROWS, MM), F32),
-            pltpu.SemaphoreType.DMA((4 + STEPS,)),
+            pltpu.SemaphoreType.DMA((5 + STEPS,)),
         ],
         compiler_params=PARAMS,
         name="fourier",
     )(
-        lat_ref,
+        device,
         in_hbm(kept_waves),
         in_hbm(weights),
         in_hbm(slot_wavenumber.reshape(8, LANES)),
         in_hbm(grid_fields.transpose(1, 0, 2)),
         in_hbm(jnp.asarray(forward_table)),
+        in_hbm(legendre),
     )
     arrived = exchange(sent, ("x", "core"))
     gathered = pl.pallas_call(
@@ -372,24 +376,24 @@
         name="gather",
     )(arrived)
     gathered = exchange(gathered, ("y", "z"))
-    spectral, back = pl.pallas_call(
+    spectral, back, table = pl.pallas_call(
         legendre_kernel,
-        in_specs=[SMEM, HBM, HBM, VMEM, HBM],
-        out_specs=[VMEM, VMEM],
+        in_specs=[SMEM, HBM, HBM, VMEM, VMEM, HBM],
+        out_specs=[VMEM, VMEM, VMEM],
         out_shape=[
             jax.ShapeDtypeStruct((2, 2, LEVELS, 2, HALF), F32),
             jax.ShapeDtypeStruct(chunk, BF16),
+            pltpu.VMEM((STEPS, 2 * BLOCK, QUARTER), BF16),
         ],
         scratch_shapes=[
             pltpu.SMEM((MM,), jnp.int32),
             pltpu.SMEM((LEVELS,), F32),
-            pltpu.VMEM((2, 2, NLAT // 2, HALF), BF16),
             pltpu.VMEM((2, NLAT // 2, LANES), F32),
-            pltpu.SemaphoreType.DMA((6,)),
+            pltpu.SemaphoreType.DMA((3,)),
         ],
         compiler_params=PARAMS,
         name="legendre",
-    )((lat * LEVS + lev).reshape(1), in_hbm(slot_wavenumber), in_hbm(diffusion), gathered, in_hbm(legendre))
+    )(device, in_hbm(slot_wavenumber), in_hbm(diffusion), gathered, in_vmem(legendre), in_hbm(jnp.asarray(inverse_table)))
     back = exchange(back, ("z",))
     scattered = pl.pallas_call(
         scatter_kernel,
@@ -411,7 +415,7 @@
         ],
         compiler_params=PARAMS,
         name="grid",
-    )(lat_ref, kept, order, returned, jnp.asarray(inverse_table))
+    )(device, kept, order, returned, in_vmem(table))
     return (
         grid_out.transpose(1, 0, 2),
         spectral,

time: 111 us -> 109 us (0.982)
  blocking collectives: 60.3 us -> 95.9 us
  waiting for transfers between devices: 21 us -> 0 us
  starting transfers between devices: 14.8 us -> 0 us
  Pallas kernels: 14.1 us -> 12 us
    all_to_all x3 -> x4, blocking collectives: 60.3 us -> 95.9 us  [exchange(): return lax.all_to_all(x, axes, split_axis=0, concat_axis=0, tiled=True)]
    all_to_all x1 -> x0, waiting for transfers between devices: 21 us -> none  [exchange(): return lax.all_to_all(x, axes, split_axis=0, concat_axis=0, tiled=True)]
    all_to_all x1 -> x0, starting transfers between devices: 14.8 us -> none  [exchange(): return lax.all_to_all(x, axes, split_axis=0, concat_axis=0, tiled=True)]
    pallas_call x2, Pallas kernels: 8.48 us -> 7.06 us  [the longest x1 4.08 us: body(): pl.pallas_call(fourier_kernel, in_specs=[SMEM, HBM, HBM, HBM, HBM, HBM, H...]
  transfers between devices with their start and end apart: 1 -> 0, of which waited for: 1 -> 0; matrix products, arithmetic and copies ran while one was open for 0% -> 0% of each run, Pallas kernels for 0% -> 0%
where the time goes in v6:
time: 109 us
  blocking collectives  95.9 us (88%)
  Pallas kernels  12 us (11%)
    all_to_all x4, blocking collectives, exchange(): return lax.all_to_all(x, axes, split_axis=0, concat_axis=0, tiled=True)  95.9 us
    pallas_call x1, Pallas kernels, body(): pl.pallas_call(fourier_kernel, in_specs=[SMEM, HBM, HBM, HBM, HBM, HBM, H...  4.08 us
    pallas_call x1, Pallas kernels, body(): pl.pallas_call(grid_kernel, in_specs=[SMEM, VMEM, VMEM, VMEM, VMEM], out_...  3.23 us
    pallas_call x1, Pallas kernels, body(): pl.pallas_call(legendre_kernel, in_specs=[SMEM, HBM, HBM, VMEM, VMEM, HBM...  2.98 us

profile of v6, /device:TPU:1, one launch (start us, length us, event | category | flops | bytes accessed | tf_op | source)
XLA Modules:
  0.0 108.6 jit_solution(12859265634558068567)
XLA Ops:
  0.6 4.1 %fourier.1 = (bf16[8,160,128]{2,1,0:T(8,128)(2,1)S(1)}, s32[1,1024]{1,0:T(1,128)S(1)}, s32[80,1]{1,0:T(8,128)S(1)}, bf16[2,2,640,512]{3,2,1,0:T(8,128)(2,1)S(1)}) custom-call(s32[1]{0:T(128)} %bitcast.device_ref, s32[20]{0:T(128)} %kept_hbm.1, f32[640]{0:T(1024)} %weights_hbm.1, s32[8,128]{1,0:T(8,128)} %bitcast.6, bf16[20,4,2688]{2,1,0:T(4,128)(2,1)} %bitcast.5, ...), custom_call_target="tpu_custom_call" | custom-call | tf_op jit(solution)/shard_map/fourier/pallas_call | solution.py:336
  4.7 16.8 %all_to_all.20.y_ref = bf16[8,160,128]{2,1,0:T(8,128)(2,1)S(1)} all-to-all(bf16[8,160,128]{2,1,0:T(8,128)(2,1)S(1)} %get-tuple-element.14), channel_id=1, replica_groups=mesh['y'=4,'z'=16,'x'=4,'core'=2] {'x','core'}, dimensions={0} | all-to-all | bytes 655360 | tf_op jit(solution)/shard_map/all_to_all | solution.py:328
  21.5 0.8 gather.1
  22.3 35.6 %all_to_all.21.z_ref = bf16[64,4,640]{2,1,0:T(4,128)(2,1)S(1)} all-to-all(bf16[64,4,640]{2,1,0:T(4,128)(2,1)S(1)} %gather.1), channel_id=1, replica_groups=mesh['y'=4,'z'=16,'x'=4,'core'=2] {'y','z'}, dimensions={0} | all-to-all | bytes 655360 | tf_op jit(solution)/shard_map/all_to_all | solution.py:328
  57.9 3.0 %legendre.1 = (f32[2,2,32,2,512]{4,3,2,1,0:T(2,128)}, bf16[16,4,2816]{2,1,0:T(4,128)(2,1)S(1)}, bf16[4,512,672]{2,1,0:T(8,128)(2,1)S(1)}) custom-call(s32[1]{0:T(128)} %bitcast.device_ref, s32[1024]{0:T(1024)} %slots_hbm.1, f32[32]{0:T(128)} %diffusion_hbm.1, bf16[64,4,640]{2,1,0:T(4,128)(2,1)S(1)} %all_to_all.21.z_ref, ...), custom_call_target="tpu_custom_call" | custom-call | tf_op jit(solution)/shard_map/legendre/pallas_call | solution.py:379
  60.9 21.6 %all_to_all.22.z_ref = bf16[16,4,2816]{2,1,0:T(4,128)(2,1)S(1)} all-to-all(bf16[16,4,2816]{2,1,0:T(4,128)(2,1)S(1)} %get-tuple-element.16), channel_id=1, replica_groups=mesh['y'=4,'z'=16,'x'=4,'core'=2] {'z'}, dimensions={0} | all-to-all | bytes 720896 | tf_op jit(solution)/shard_map/all_to_all | solution.py:328
  82.5 0.9 scatter.1
  83.4 21.9 %all_to_all.23.y_ref = bf16[32,56,128]{2,1,0:T(8,128)(2,1)S(1)} all-to-all(bf16[32,56,128]{2,1,0:T(8,128)(2,1)S(1)} %scatter.1), channel_id=1, replica_groups=mesh['y'=4,'z'=16,'x'=4,'core'=2] {'y','x','core'}, dimensions={0} | all-to-all | bytes 917504 | tf_op jit(solution)/shard_map/all_to_all | solution.py:328
  105.4 3.2 %grid.1 = (f32[20,4,2688]{2,1,0:T(4,128)}, f32[8,128]{1,0:T(8,128)}) custom-call(s32[1]{0:T(128)} %bitcast.device_ref, s32[80,1]{1,0:T(8,128)S(1)} %get-tuple-element.12.kept_ref, s32[1,1024]{1,0:T(1,128)S(1)} %get-tuple-element.13.order_ref, bf16[32,56,128]{2,1,0:T(8,128)(2,1)S(1)} %all_to_all.23.y_ref, bf16[4,512,672]{2,1,0:T(8,128)(2,1)S(1)} %get-tuple-element.17.table_ref), custom_call_target="tpu_custom_call" | custom-call | tf_op jit(solution)/shard_map/grid/pallas_call | solution.py:408

commit v7 on v6

--- a/solution.py
+++ b/solution.py
@@ -22,6 +22,7 @@
 LEVS = 8
 YS = 4
 ZS = 16
+CHUNK = 2 * ROWS // YS
 NORTH = LATS // 2
 QUARTER = NLON // 4
 STEPS = 4
@@ -91,6 +92,23 @@
     band = jnp.where(southern, BAND - 1 - band, band)
     wanted = (to % 2) * ROWS + band * LEV + to // 2 % LEV
     return jnp.where(source == wanted, 1.0, 0.0).astype(BF16)
+
+
+def swap_lanes(even, odd, width):
+    high = iota(even.shape, 1) // width % 2 == 1
+    return (
+        jnp.where(high, pltpu.roll(odd, width, 1), even),
+        jnp.where(high, odd, pltpu.roll(even, LANES - width, 1)),
+    )
+
+
+def swap_parts(parts):
+    parts = list(parts)
+    parts[0], parts[1] = swap_lanes(parts[0], parts[1], ZS)
+    parts[2], parts[3] = swap_lanes(parts[2], parts[3], ZS)
+    parts[0], parts[2] = swap_lanes(parts[0], parts[2], 2 * ZS)
+    parts[1], parts[3] = swap_lanes(parts[1], parts[3], 2 * ZS)
+    return parts
 
 
 def fourier_kernel(
@@ -110,7 +128,7 @@
     lat = device_ref[0] // LEVS
     small[0].wait()
     order = slot_order(slots_v[...])
-    order_ref[...] = order
+    order_ref[...] = jnp.concatenate([order[:, b * LANES : (b + 1) * LANES] for b in range(LEVS)], axis=0).T
     small[2].wait()
     small[3].wait()
     kept = latitude_column([kept_s[j] for j in range(BAND)], jnp.int32(0))
@@ -155,19 +173,24 @@
         else:
             acc[...] += part
     choice = row_choice(lat >= NORTH)
-    moved = jnp.dot(choice, acc[...].astype(BF16), preferred_element_type=F32).astype(BF16)
+    moved = jnp.dot(choice, acc[...].astype(BF16), preferred_element_type=F32)
     for b in range(LEVS):
-        o_ref[b] = moved[:, b * LANES : (b + 1) * LANES]
+        block = moved[:, b * LANES : (b + 1) * LANES]
+        parts = swap_parts([block[i * CHUNK : (i + 1) * CHUNK] for i in range(YS)])
+        for y in range(YS):
+            o_ref[y * LEVS + b] = parts[y].astype(BF16)
     later.wait()
 
 
 def gather_kernel(y_ref, o_ref, rows):
-    for j in range(BAND):
-        block = jnp.concatenate([y_ref[b, 8 * j : 8 * j + 8, :].astype(F32) for b in range(LEVS)], axis=0)
-        turned = block.T
-        rows[:, j % 4, (j // 4) * LANES : (j // 4 + 1) * LANES] = jnp.concatenate(
-            [turned[:LATS], turned[LATS:]], axis=1
-        )
+    for y in range(YS):
+        for j in range(TILES):
+            block = [y_ref[y * LEVS + b, 8 * j : 8 * j + 8, :].astype(F32) for b in range(LEVS)]
+            turned = jnp.concatenate(block, axis=0).T
+            turned = jnp.concatenate([turned[:LATS], turned[LATS:]], axis=1)
+            for part in range(4):
+                row, tile = (part * TILES + j) % 4, y * TILES + (part * TILES + j) // 4
+                rows[:, row, tile * LANES : (tile + 1) * LANES] = turned[part * ZS : (part + 1) * ZS]
     o_ref[...] = rows[...].astype(BF16)
 
 
@@ -182,26 +205,16 @@
             block = jnp.concatenate(block, axis=0)
             turned = jnp.concatenate([block[:, :LATS], block[:, LATS:]], axis=0).T
             for b in range(LEVS):
-                o_ref[y * LEVS + b, 16 + 8 * j : 24 + 8 * j, :] = turned[8 * b : 8 * b + 8].astype(BF16)
+                o_ref[y * LEVS + b, 8 + 8 * j : 16 + 8 * j, :] = turned[8 * b : 8 * b + 8].astype(BF16)
     power = jnp.sum(rows[:, :, YS * DATA :], axis=0)
     power = jnp.concatenate([power[:, :LANES], power[:, LANES:]], axis=0)
-    high = power.astype(BF16)
-    both = jnp.concatenate([high.astype(F32), power - high.astype(F32)], axis=0).astype(BF16)
     for peer in range(YS * LEVS):
-        o_ref[peer, :16, :] = both
-
-
-def swap_lanes(even, odd, width):
-    high = iota(even.shape, 1) // width % 2 == 1
-    return (
-        jnp.where(high, pltpu.roll(odd, width, 1), even),
-        jnp.where(high, odd, pltpu.roll(even, LANES - width, 1)),
-    )
+        o_ref[peer, :8, :] = power.astype(BF16)
 
 
 def legendre_kernel(
-    device_ref, slots_hbm, diffusion_hbm, z_ref, table_ref, later_hbm, spectral_ref, o_ref, later_ref, slots_s, diffusion_s,
-    comb, sems
+    device_ref, slots_hbm, diffusion_hbm, z_ref, table_ref, later_hbm, spectral_hbm, o_ref, later_ref, slots_s, diffusion_s,
+    spectral_v, comb, sems
 ):
     copies = [
         pltpu.make_async_copy(slots_hbm, slots_s, sems.at[0]),
@@ -214,15 +227,17 @@
         north, south = [], []
         for u in range(4 * group, 4 * group + 4):
             a, tile = divmod(u, TILES)
-            lanes = slice(tile * LANES, (tile + 1) * LANES)
-            north.append(z_ref[a, :, lanes].astype(F32))
-            south.append(z_ref[LATS - 1 - a, :, lanes].astype(F32))
+            for side, lat in (north, a), (south, LATS - 1 - a):
+                y, z = divmod(lat, ZS)
+                place = (y * TILES + tile) * LANES
+                side.append(z_ref[z, :, place : place + LANES].astype(F32))
         north = jnp.concatenate(north, axis=0)
         south = jnp.concatenate(south, axis=0)
         comb[0, 16 * group : 16 * group + 16, :] = north + south
         comb[1, 16 * group : 16 * group + 16, :] = north - south
     for copy in copies:
         copy.wait()
+    copies = [later]
     column = iota((2 * LEVELS, HALF), 1)
     level = iota((2 * LEVELS, 1), 0) // 2
     diffusion = jnp.zeros((2 * LEVELS, 1), F32)
@@ -239,7 +254,9 @@
             degree = wave + 2 * column + q
             spectral = jnp.where(degree < MM, raw, 0.0)
             for level in range(LEVELS):
-                spectral_ref[t, q, level] = spectral[2 * level : 2 * level + 2]
+                spectral_v[t, q, level] = spectral[2 * level : 2 * level + 2]
+            copies.append(pltpu.make_async_copy(spectral_v.at[t, q], spectral_hbm.at[t, q], sems.at[3 + 2 * t + q]))
+            copies[-1].start()
             degree = degree.astype(F32)
             ratio = degree * (degree + 1.0) / (MM * (MM + 1.0))
             damped = (spectral / (1.0 + diffusion * ratio * ratio)).astype(BF16)
@@ -271,27 +288,25 @@
             y, z = divmod(LATS - 1 - a if half else a, ZS)
             place = (y * TILES + tile) * LANES
             o_ref[z, :, place : place + LANES] = side[4 * u : 4 * u + 4].astype(BF16)
-    later.wait()
-
-
-def grid_kernel(device_ref, kept_ref, order_ref, y_ref, table_ref, o_ref, spectrum_ref):
+    for copy in copies:
+        copy.wait()
+
+
+def grid_kernel(device_ref, kept_ref, order_ref, y_ref, table_ref, o_hbm, spectrum_ref, points_v, sems):
     kept = kept_ref[...]
     choice = row_choice(device_ref[0] >= NORTH * LEVS)
     back = []
     for b in range(LEVS):
-        parts = [y_ref[y * LEVS + b, 16:, :].astype(F32) for y in range(YS)]
-        parts[0], parts[1] = swap_lanes(parts[0], parts[1], ZS)
-        parts[2], parts[3] = swap_lanes(parts[2], parts[3], ZS)
-        parts[0], parts[2] = swap_lanes(parts[0], parts[2], 2 * ZS)
-        parts[1], parts[3] = swap_lanes(parts[1], parts[3], 2 * ZS)
+        parts = swap_parts([y_ref[y * LEVS + b, 8:, :].astype(F32) for y in range(YS)])
         back.append(jnp.concatenate(parts, axis=0).astype(BF16))
     back = jnp.concatenate(back, axis=1)
     rows = lax.dot_general(choice, back, (((0,), (0,)), ((), ())), preferred_element_type=F32).astype(BF16)
+    numbers = [jnp.broadcast_to(order_ref[:, b : b + 1], (LANES, BLOCK)) for b in range(LEVS)]
     parts = []
     for step in range(STEPS):
-        numbered = lax.dot_general(
-            rows, slot_choice(order_ref[...], step), (((1,), (1,)), ((), ())), preferred_element_type=F32
-        )
+        number = iota((LANES, BLOCK), 1) * STEPS + step
+        choice = jnp.concatenate([jnp.where(n == number, 1.0, 0.0).astype(BF16) for n in numbers], axis=0)
+        numbered = jnp.dot(rows, choice, preferred_element_type=F32)
         mask = class_mask(kept, step)
         real = jnp.where(mask, numbered[:ROWS], 0.0)
         imaginary = jnp.where(mask, numbered[ROWS:], 0.0)
@@ -303,17 +318,25 @@
         parts.append(jnp.dot(left.astype(BF16), table_ref[step], preferred_element_type=F32))
     odd = parts[1] + parts[3]
     plus, minus = parts[0] + parts[2], parts[0] - parts[2]
-    quarters = [plus + odd[:ROWS], minus + odd[ROWS:], plus - odd[:ROWS], minus - odd[ROWS:]]
-    points = jnp.concatenate(quarters, axis=1) * math.sqrt(NLON / MM)
-    for j in range(BAND):
-        o_ref[j] = points[LEV * j : LEV * (j + 1), :]
-    power = jnp.zeros((16, LANES), F32)
+    copies = []
+    for group in range(ROWS // 16):
+        place = slice(16 * group, 16 * group + 16)
+        turned = slice(ROWS + 16 * group, ROWS + 16 * group + 16)
+        quarters = [plus[place] + odd[place], minus[place] + odd[turned], plus[place] - odd[place], minus[place] - odd[turned]]
+        points = jnp.concatenate(quarters, axis=1) * math.sqrt(NLON / MM)
+        bands = pl.ds(4 * group, 4)
+        for i in range(4):
+            points_v[4 * group + i] = points[LEV * i : LEV * (i + 1)]
+        copies.append(pltpu.make_async_copy(points_v.at[bands], o_hbm.at[bands], sems.at[group]))
+        copies[-1].start()
+    power = jnp.zeros((8, LANES), F32)
     for peer in range(YS * LEVS):
-        power += y_ref[peer, :16, :].astype(F32)
-    power = power[:8] + power[8:]
+        power += y_ref[peer, :8, :].astype(F32)
     power = jnp.concatenate([power[i // 2 + 4 * (i % 2)][None] for i in range(8)], axis=0)
     degree = (iota((8, LANES), 0) * LANES + iota((8, LANES), 1)).astype(F32)
     spectrum_ref[...] = power / (2.0 * LEVELS * (degree + 1.0))
+    for copy in copies:
+        copy.wait()
 
 
 def in_hbm(x):
@@ -338,8 +361,8 @@
         in_specs=[SMEM, HBM, HBM, HBM, HBM, HBM, HBM],
         out_specs=[VMEM, VMEM, VMEM, VMEM],
         out_shape=[
-            jax.ShapeDtypeStruct((LEVS, 2 * ROWS, LANES), BF16),
-            jax.ShapeDtypeStruct((1, MM), jnp.int32),
+            jax.ShapeDtypeStruct((YS * LEVS, CHUNK, LANES), BF16),
+            jax.ShapeDtypeStruct((LANES, LEVS), jnp.int32),
             jax.ShapeDtypeStruct((ROWS, 1), jnp.int32),
             pltpu.VMEM(legendre.shape, BF16),
         ],
@@ -365,21 +388,21 @@
         in_hbm(jnp.asarray(forward_table)),
         in_hbm(legendre),
     )
-    arrived = exchange(sent, ("x", "core"))
+    arrived = exchange(sent, ("y", "x", "core"))
     gathered = pl.pallas_call(
         gather_kernel,
         in_specs=[VMEM],
         out_specs=VMEM,
-        out_shape=jax.ShapeDtypeStruct((LATS, 4, DATA), BF16),
-        scratch_shapes=[pltpu.VMEM((LATS, 4, DATA), F32)],
+        out_shape=jax.ShapeDtypeStruct((ZS, 4, YS * DATA), BF16),
+        scratch_shapes=[pltpu.VMEM((ZS, 4, YS * DATA), F32)],
         compiler_params=PARAMS,
         name="gather",
     )(arrived)
-    gathered = exchange(gathered, ("y", "z"))
+    gathered = exchange(gathered, ("z",))
     spectral, back, table = pl.pallas_call(
         legendre_kernel,
         in_specs=[SMEM, HBM, HBM, VMEM, VMEM, HBM],
-        out_specs=[VMEM, VMEM, VMEM],
+        out_specs=[HBM, VMEM, VMEM],
         out_shape=[
             jax.ShapeDtypeStruct((2, 2, LEVELS, 2, HALF), F32),
             jax.ShapeDtypeStruct(chunk, BF16),
@@ -388,8 +411,9 @@
         scratch_shapes=[
             pltpu.SMEM((MM,), jnp.int32),
             pltpu.SMEM((LEVELS,), F32),
+            pltpu.VMEM((2, 2, LEVELS, 2, HALF), F32),
             pltpu.VMEM((2, NLAT // 2, LANES), F32),
-            pltpu.SemaphoreType.DMA((3,)),
+            pltpu.SemaphoreType.DMA((7,)),
         ],
         compiler_params=PARAMS,
         name="legendre",
@@ -399,7 +423,7 @@
         scatter_kernel,
         in_specs=[VMEM],
         out_specs=VMEM,
-        out_shape=jax.ShapeDtypeStruct((YS * LEVS, 16 + 2 * ROWS // YS, LANES), BF16),
+        out_shape=jax.ShapeDtypeStruct((YS * LEVS, 8 + CHUNK, LANES), BF16),
         scratch_shapes=[pltpu.VMEM(chunk, F32)],
         compiler_params=PARAMS,
         name="scatter",
@@ -408,10 +432,14 @@
     grid_out, spectrum = pl.pallas_call(
         grid_kernel,
         in_specs=[SMEM, VMEM, VMEM, VMEM, VMEM],
-        out_specs=[VMEM, VMEM],
+        out_specs=[HBM, VMEM],
         out_shape=[
             jax.ShapeDtypeStruct((BAND, LEV, NLON), F32),
             jax.ShapeDtypeStruct((8, LANES), F32),
+        ],
+        scratch_shapes=[
+            pltpu.VMEM((BAND, LEV, NLON), F32),
+            pltpu.SemaphoreType.DMA((ROWS // 16,)),
         ],
         compiler_params=PARAMS,
         name="grid",

time: 109 us -> 110 us (level)
  no operation moved by 1% of the time
where the time goes in v7:
time: 110 us
  blocking collectives  96.7 us (88%)
  Pallas kernels  12.1 us (11%)
    all_to_all x4, blocking collectives, exchange(): return lax.all_to_all(x, axes, split_axis=0, concat_axis=0, tiled=True)  96.7 us
    pallas_call x1, Pallas kernels, body(): pl.pallas_call(fourier_kernel, in_specs=[SMEM, HBM, HBM, HBM, HBM, HBM, H...  4.27 us
    pallas_call x1, Pallas kernels, body(): pl.pallas_call(grid_kernel, in_specs=[SMEM, VMEM, VMEM, VMEM, VMEM], out_...  3.64 us
    pallas_call x1, Pallas kernels, body(): pl.pallas_call(legendre_kernel, in_specs=[SMEM, HBM, HBM, VMEM, VMEM, HBM...  2.56 us

profile of v7, /device:TPU:1, one launch (start us, length us, event | category | flops | bytes accessed | tf_op | source)
XLA Modules:
  0.0 109.5 jit_solution(18251671590048777735)
XLA Ops:
  0.6 4.3 %fourier.1 = (bf16[32,40,128]{2,1,0:T(8,128)(2,1)S(1)}, s32[128,8]{1,0:T(8,128)S(1)}, s32[80,1]{1,0:T(8,128)S(1)}, bf16[2,2,640,512]{3,2,1,0:T(8,128)(2,1)S(1)}) custom-call(s32[1]{0:T(128)} %bitcast.device_ref, s32[20]{0:T(128)} %kept_hbm.1, f32[640]{0:T(1024)} %weights_hbm.1, s32[8,128]{1,0:T(8,128)} %bitcast.6, bf16[20,4,2688]{2,1,0:T(4,128)(2,1)} %bitcast.5, ...), custom_call_target="tpu_custom_call" | custom-call | tf_op jit(solution)/shard_map/fourier/pallas_call | solution.py:359
  4.9 19.2 %all_to_all.20.y_ref = bf16[32,40,128]{2,1,0:T(8,128)(2,1)S(1)} all-to-all(bf16[32,40,128]{2,1,0:T(8,128)(2,1)S(1)} %get-tuple-element.14), channel_id=1, replica_groups=mesh['y'=4,'z'=16,'x'=4,'core'=2] {'y','x','core'}, dimensions={0} | all-to-all | bytes 655360 | tf_op jit(solution)/shard_map/all_to_all | solution.py:351
  24.1 0.8 gather.1
  24.9 29.0 %all_to_all.21.z_ref = bf16[16,4,2560]{2,1,0:T(4,128)(2,1)S(1)} all-to-all(bf16[16,4,2560]{2,1,0:T(4,128)(2,1)S(1)} %gather.1), channel_id=1, replica_groups=mesh['y'=4,'z'=16,'x'=4,'core'=2] {'z'}, dimensions={0} | all-to-all | bytes 655360 | tf_op jit(solution)/shard_map/all_to_all | solution.py:351
  53.9 2.6 %legendre.1 = (f32[2,2,32,2,512]{4,3,2,1,0:T(2,128)}, bf16[16,4,2816]{2,1,0:T(4,128)(2,1)S(1)}, bf16[4,512,672]{2,1,0:T(8,128)(2,1)S(1)}) custom-call(s32[1]{0:T(128)} %bitcast.device_ref, s32[1024]{0:T(1024)} %slots_hbm.1, f32[32]{0:T(128)} %diffusion_hbm.1, bf16[16,4,2560]{2,1,0:T(4,128)(2,1)S(1)} %all_to_all.21.z_ref, ...), custom_call_target="tpu_custom_call" | custom-call | tf_op jit(solution)/shard_map/legendre/pallas_call | solution.py:402
  56.4 27.4 %all_to_all.22.z_ref = bf16[16,4,2816]{2,1,0:T(4,128)(2,1)S(1)} all-to-all(bf16[16,4,2816]{2,1,0:T(4,128)(2,1)S(1)} %get-tuple-element.16), channel_id=1, replica_groups=mesh['y'=4,'z'=16,'x'=4,'core'=2] {'z'}, dimensions={0} | all-to-all | bytes 720896 | tf_op jit(solution)/shard_map/all_to_all | solution.py:351
  83.8 0.9 scatter.1
  84.7 21.2 %all_to_all.23.y_ref = bf16[32,48,128]{2,1,0:T(8,128)(2,1)S(1)} all-to-all(bf16[32,48,128]{2,1,0:T(8,128)(2,1)S(1)} %scatter.1), channel_id=1, replica_groups=mesh['y'=4,'z'=16,'x'=4,'core'=2] {'y','x','core'}, dimensions={0} | all-to-all | bytes 786432 | tf_op jit(solution)/shard_map/all_to_all | solution.py:351
  105.9 3.6 %grid.1 = (f32[20,4,2688]{2,1,0:T(4,128)}, f32[8,128]{1,0:T(8,128)}) custom-call(s32[1]{0:T(128)} %bitcast.device_ref, s32[80,1]{1,0:T(8,128)S(1)} %get-tuple-element.12.kept_ref, s32[128,8]{1,0:T(8,128)S(1)} %get-tuple-element.13.order_ref, bf16[32,48,128]{2,1,0:T(8,128)(2,1)S(1)} %all_to_all.23.y_ref, bf16[4,512,672]{2,1,0:T(8,128)(2,1)S(1)} %get-tuple-element.17.table_ref), custom_call_target="tpu_custom_call" | custom-call | tf_op jit(solution)/shard_map/grid/pallas_call | solution.py:432

commit v8 on v7

--- a/solution.py
+++ b/solution.py
@@ -46,8 +46,11 @@
     norm_scale = np.float32(1.0 / math.sqrt(NLON))
     cosine = (np.cos(angles) * norm_scale).astype(ml_dtypes.bfloat16)
     sine = (-np.sin(angles) * norm_scale).astype(ml_dtypes.bfloat16)
-    both = np.stack([cosine, sine], axis=1).reshape(QUARTER, 2, BLOCK, STEPS)
-    forward = np.ascontiguousarray(both.transpose(3, 0, 1, 2)).reshape(STEPS, QUARTER, 2 * BLOCK)
+    rising = np.arange(LANES)
+    places = np.concatenate([rising, BLOCK - 1 - rising])
+    numbers = places[None, :] * STEPS + np.arange(STEPS)[:, None]
+    forward = np.stack([cosine[:, numbers], sine[:, numbers]], axis=2)
+    forward = np.ascontiguousarray(forward.transpose(1, 0, 2, 3)).reshape(STEPS, QUARTER, 2 * BLOCK)
     inverse = np.ascontiguousarray(forward.transpose(0, 2, 1))
     return forward, inverse
 
@@ -56,19 +59,19 @@
     return lax.broadcasted_iota(jnp.int32, shape, dim)
 
 
-def slot_choice(order, step):
-    number = iota((BLOCK, MM), 0) * STEPS + step
-    return jnp.where(order == number, 1.0, 0.0).astype(BF16)
+def pair_number(shape, dim):
+    place = iota(shape, dim)
+    return place % LANES * STEPS + place // LANES
 
 
 def slot_order(slots):
     digits = jnp.concatenate([slots // 32, slots % 32], axis=0).astype(F32).astype(BF16)
-    source = iota((LANES, MM), 0)
-    to = iota((LANES, MM), 1)
-    choice = jnp.where(source == to % 8 * 16 + to // LANES * 2 + to // LATS % 2, 1.0, 0.0).astype(BF16)
+    source = iota((LANES, HALF), 0)
+    to = iota((LANES, HALF), 1)
+    choice = jnp.where(source == to % 8 * 16 + to // LATS * 2, 1.0, 0.0).astype(BF16)
     moved = jnp.dot(digits, choice, preferred_element_type=F32)
-    row = iota((16, MM), 0)
-    mine = row % 8 == iota((16, MM), 1) % LATS // 8
+    row = iota((16, HALF), 0)
+    mine = row % 8 == iota((16, HALF), 1) % LATS // 8
     value = jnp.where(mine, moved * jnp.where(row < 8, 32.0, 1.0), 0.0)
     return jnp.sum(value, axis=0, keepdims=True).astype(jnp.int32)
 
@@ -82,7 +85,13 @@
 
 
 def class_mask(kept, step):
-    return iota((ROWS, BLOCK), 1) * STEPS + step < kept
+    place = iota((ROWS, BLOCK), 1)
+    place = jnp.where(place < LANES, place, BLOCK + LANES - 1 - place)
+    return place * STEPS + step < kept
+
+
+def lower_of_pair(wave):
+    return jnp.minimum(wave, MM - 1 - wave)
 
 
 def row_choice(southern):
@@ -102,6 +111,11 @@
     )
 
 
+def sort_pair(order, first, second):
+    flip = jnp.broadcast_to(order >= HALF, first.shape)
+    return jnp.where(flip, second, first), jnp.where(flip, first, second)
+
+
 def swap_parts(parts):
     parts = list(parts)
     parts[0], parts[1] = swap_lanes(parts[0], parts[1], ZS)
@@ -112,8 +126,8 @@
 
 
 def fourier_kernel(
-    device_ref, kept_hbm, weights_hbm, slots_hbm, x_hbm, table_hbm, later_hbm, o_ref, order_ref, kept_ref, later_ref, kept_s, weights_s, slots_v, x_v,
-    table_v, even, odd, acc, sems
+    device_ref, kept_hbm, weights_hbm, slots_hbm, x_hbm, table_hbm, later_hbm, o_ref, order_ref, column_ref, kept_ref, later_ref, kept_s, weights_s, slots_v, x_v,
+    table_v, even, odd, both, sems
 ):
     small = [
         pltpu.make_async_copy(slots_hbm, slots_v, sems.at[0]),
@@ -128,7 +142,10 @@
     lat = device_ref[0] // LEVS
     small[0].wait()
     order = slot_order(slots_v[...])
-    order_ref[...] = jnp.concatenate([order[:, b * LANES : (b + 1) * LANES] for b in range(LEVS)], axis=0).T
+    order_ref[...] = order
+    lower = lower_of_pair(order)
+    columns = [lower[:, i * LANES : (i + 1) * LANES] for i in range(4)]
+    column_ref[...] = jnp.concatenate(columns + columns, axis=0).T
     small[2].wait()
     small[3].wait()
     kept = latitude_column([kept_s[j] for j in range(BAND)], jnp.int32(0))
@@ -167,18 +184,21 @@
             imaginary = first[:, BLOCK:] - second[:, :BLOCK]
         scale = jnp.where(class_mask(kept, step), weight, 0.0)
         fourier = jnp.concatenate([real * scale, imaginary * scale], axis=0).astype(BF16)
-        part = jnp.dot(fourier, slot_choice(order, step), preferred_element_type=F32)
-        if step == 0:
-            acc[...] = part
-        else:
-            acc[...] += part
+        both[: 2 * ROWS, step * LANES : (step + 1) * LANES] = fourier[:, :LANES]
+        both[2 * ROWS :, (3 - step) * LANES : (4 - step) * LANES] = fourier[:, LANES:]
+    choice = jnp.where(lower == pair_number((HALF, HALF), 0), 1.0, 0.0).astype(BF16)
+    moved = jnp.dot(both[...], choice, preferred_element_type=F32)
+    moved = sort_pair(order, moved[: 2 * ROWS], moved[2 * ROWS :])
     choice = row_choice(lat >= NORTH)
-    moved = jnp.dot(choice, acc[...].astype(BF16), preferred_element_type=F32)
-    for b in range(LEVS):
-        block = moved[:, b * LANES : (b + 1) * LANES]
-        parts = swap_parts([block[i * CHUNK : (i + 1) * CHUNK] for i in range(YS)])
-        for y in range(YS):
-            o_ref[y * LEVS + b] = parts[y].astype(BF16)
+    moved = jnp.concatenate([half.astype(BF16) for half in moved], axis=1)
+    moved = jnp.dot(choice, moved, preferred_element_type=F32)
+    for i in range(LEVS // 2):
+        place = i * LANES
+        pair = swap_lanes(moved[:, place : place + LANES], moved[:, HALF + place : HALF + place + LANES], LATS)
+        for b, block in zip((2 * i, 2 * i + 1), pair):
+            parts = swap_parts([block[k * CHUNK : (k + 1) * CHUNK] for k in range(YS)])
+            for y in range(YS):
+                o_ref[y * LEVS + b] = parts[y].astype(BF16)
     later.wait()
 
 
@@ -292,24 +312,33 @@
         copy.wait()
 
 
-def grid_kernel(device_ref, kept_ref, order_ref, y_ref, table_ref, o_hbm, spectrum_ref, points_v, sems):
+def grid_kernel(device_ref, kept_ref, order_ref, column_ref, y_ref, table_ref, o_ref, spectrum_ref):
     kept = kept_ref[...]
     choice = row_choice(device_ref[0] >= NORTH * LEVS)
-    back = []
-    for b in range(LEVS):
-        parts = swap_parts([y_ref[y * LEVS + b, 8:, :].astype(F32) for y in range(YS)])
-        back.append(jnp.concatenate(parts, axis=0).astype(BF16))
-    back = jnp.concatenate(back, axis=1)
+    firsts, seconds = [], []
+    for i in range(LEVS // 2):
+        pair = []
+        for b in (2 * i, 2 * i + 1):
+            parts = swap_parts([y_ref[y * LEVS + b, 8:, :].astype(F32) for y in range(YS)])
+            pair.append(jnp.concatenate(parts, axis=0))
+        first, second = swap_lanes(pair[0], pair[1], LATS)
+        firsts.append(first)
+        seconds.append(second)
+    back = sort_pair(order_ref[...], jnp.concatenate(firsts, axis=1), jnp.concatenate(seconds, axis=1))
+    back = jnp.concatenate([half.astype(BF16) for half in back], axis=1)
     rows = lax.dot_general(choice, back, (((0,), (0,)), ((), ())), preferred_element_type=F32).astype(BF16)
-    numbers = [jnp.broadcast_to(order_ref[:, b : b + 1], (LANES, BLOCK)) for b in range(LEVS)]
+    rows = jnp.concatenate([rows[:, :HALF], rows[:, HALF:]], axis=0)
+    number = pair_number((LANES, HALF), 1)
+    choice = [jnp.where(column_ref[:, i : i + 1] == number, 1.0, 0.0).astype(BF16) for i in range(HALF // LANES)]
+    numbered = jnp.dot(rows, jnp.concatenate(choice, axis=0), preferred_element_type=F32)
     parts = []
     for step in range(STEPS):
-        number = iota((LANES, BLOCK), 1) * STEPS + step
-        choice = jnp.concatenate([jnp.where(n == number, 1.0, 0.0).astype(BF16) for n in numbers], axis=0)
-        numbered = jnp.dot(rows, choice, preferred_element_type=F32)
+        low = numbered[: 2 * ROWS, step * LANES : (step + 1) * LANES]
+        high = numbered[2 * ROWS :, (3 - step) * LANES : (4 - step) * LANES]
+        found = jnp.concatenate([low, high], axis=1)
         mask = class_mask(kept, step)
-        real = jnp.where(mask, numbered[:ROWS], 0.0)
-        imaginary = jnp.where(mask, numbered[ROWS:], 0.0)
+        real = jnp.where(mask, found[:ROWS], 0.0)
+        imaginary = jnp.where(mask, found[ROWS:], 0.0)
         left = jnp.concatenate([real, imaginary], axis=1)
         if step == 1:
             left = jnp.concatenate([left, jnp.concatenate([-imaginary, real], axis=1)], axis=0)
@@ -318,25 +347,19 @@
         parts.append(jnp.dot(left.astype(BF16), table_ref[step], preferred_element_type=F32))
     odd = parts[1] + parts[3]
     plus, minus = parts[0] + parts[2], parts[0] - parts[2]
-    copies = []
     for group in range(ROWS // 16):
         place = slice(16 * group, 16 * group + 16)
         turned = slice(ROWS + 16 * group, ROWS + 16 * group + 16)
         quarters = [plus[place] + odd[place], minus[place] + odd[turned], plus[place] - odd[place], minus[place] - odd[turned]]
         points = jnp.concatenate(quarters, axis=1) * math.sqrt(NLON / MM)
-        bands = pl.ds(4 * group, 4)
         for i in range(4):
-            points_v[4 * group + i] = points[LEV * i : LEV * (i + 1)]
-        copies.append(pltpu.make_async_copy(points_v.at[bands], o_hbm.at[bands], sems.at[group]))
-        copies[-1].start()
+            o_ref[4 * group + i] = points[LEV * i : LEV * (i + 1)]
     power = jnp.zeros((8, LANES), F32)
     for peer in range(YS * LEVS):
         power += y_ref[peer, :8, :].astype(F32)
     power = jnp.concatenate([power[i // 2 + 4 * (i % 2)][None] for i in range(8)], axis=0)
     degree = (iota((8, LANES), 0) * LANES + iota((8, LANES), 1)).astype(F32)
     spectrum_ref[...] = power / (2.0 * LEVELS * (degree + 1.0))
-    for copy in copies:
-        copy.wait()
 
 
 def in_hbm(x):
@@ -356,13 +379,14 @@
     device = lax.axis_index(("y", "z", "x", "core")).astype(jnp.int32).reshape(1)
     chunk = (ZS, 4, YS * DATA + 2 * LANES)
 
-    sent, order, kept, legendre = pl.pallas_call(
+    sent, order, column, kept, legendre = pl.pallas_call(
         fourier_kernel,
         in_specs=[SMEM, HBM, HBM, HBM, HBM, HBM, HBM],
-        out_specs=[VMEM, VMEM, VMEM, VMEM],
+        out_specs=[VMEM, VMEM, VMEM, VMEM, VMEM],
         out_shape=[
             jax.ShapeDtypeStruct((YS * LEVS, CHUNK, LANES), BF16),
-            jax.ShapeDtypeStruct((LANES, LEVS), jnp.int32),
+            jax.ShapeDtypeStruct((1, HALF), jnp.int32),
+            jax.ShapeDtypeStruct((LANES, 8), jnp.int32),
             jax.ShapeDtypeStruct((ROWS, 1), jnp.int32),
             pltpu.VMEM(legendre.shape, BF16),
         ],
@@ -374,7 +398,7 @@
             pltpu.VMEM((STEPS, QUARTER, 2 * BLOCK), BF16),
             pltpu.VMEM((2, 2 * ROWS, QUARTER), BF16),
             pltpu.VMEM((4 * ROWS, QUARTER), BF16),
-            pltpu.VMEM((2 * ROWS, MM), F32),
+            pltpu.VMEM((4 * ROWS, HALF), BF16),
             pltpu.SemaphoreType.DMA((5 + STEPS,)),
         ],
         compiler_params=PARAMS,
@@ -431,19 +455,15 @@
     returned = exchange(scattered, ("y", "x", "core"))
     grid_out, spectrum = pl.pallas_call(
         grid_kernel,
-        in_specs=[SMEM, VMEM, VMEM, VMEM, VMEM],
-        out_specs=[HBM, VMEM],
+        in_specs=[SMEM, VMEM, VMEM, VMEM, VMEM, VMEM],
+        out_specs=[VMEM, VMEM],
         out_shape=[
             jax.ShapeDtypeStruct((BAND, LEV, NLON), F32),
             jax.ShapeDtypeStruct((8, LANES), F32),
         ],
-        scratch_shapes=[
-            pltpu.VMEM((BAND, LEV, NLON), F32),
-            pltpu.SemaphoreType.DMA((ROWS // 16,)),
-        ],
         compiler_params=PARAMS,
         name="grid",
-    )(device, kept, order, returned, in_vmem(table))
+    )(device, kept, order, column, returned, in_vmem(table))
     return (
         grid_out.transpose(1, 0, 2),
         spectral,

time: 110 us -> 109 us (level)
  no operation moved by 1% of the time
where the time goes in v8:
time: 109 us; the launch traced here: 108 us
  blocking collectives  96.7 us (89%)
  Pallas kernels  11 us (10%)
    all_to_all x4, blocking collectives, exchange(): return lax.all_to_all(x, axes, split_axis=0, concat_axis=0, tiled=True)  96.7 us
    pallas_call x1, Pallas kernels, body(): pl.pallas_call(fourier_kernel, in_specs=[SMEM, HBM, HBM, HBM, HBM, HBM, H...  4.22 us
    pallas_call x1, Pallas kernels, body(): pl.pallas_call(grid_kernel, in_specs=[SMEM, VMEM, VMEM, VMEM, VMEM, VMEM]...  2.59 us
    pallas_call x1, Pallas kernels, body(): pl.pallas_call(legendre_kernel, in_specs=[SMEM, HBM, HBM, VMEM, VMEM, HBM...  2.53 us

profile of v8, /device:TPU:1, one launch (start us, length us, event | category | flops | bytes accessed | tf_op | source)
XLA Modules:
  0.0 108.4 jit_solution(14383082222681359271)
XLA Ops:
  0.6 4.2 %fourier.1 = (bf16[32,40,128]{2,1,0:T(8,128)(2,1)S(1)}, s32[1,512]{1,0:T(1,128)S(1)}, s32[128,8]{1,0:T(8,128)S(1)}, s32[80,1]{1,0:T(8,128)S(1)}, bf16[2,2,640,512]{3,2,1,0:T(8,128)(2,1)S(1)}) custom-call(s32[1]{0:T(128)} %bitcast.device_ref, s32[20]{0:T(128)} %kept_hbm.1, f32[640]{0:T(1024)} %weights_hbm.1, s32[8,128]{1,0:T(8,128)} %bitcast.6, ...), custom_call_target="tpu_custom_call" | custom-call | tf_op jit(solution)/shard_map/fourier/pallas_call | solution.py:382
  4.9 19.2 %all_to_all.20.y_ref = bf16[32,40,128]{2,1,0:T(8,128)(2,1)S(1)} all-to-all(bf16[32,40,128]{2,1,0:T(8,128)(2,1)S(1)} %get-tuple-element.16), channel_id=1, replica_groups=mesh['y'=4,'z'=16,'x'=4,'core'=2] {'y','x','core'}, dimensions={0} | all-to-all | bytes 655360 | tf_op jit(solution)/shard_map/all_to_all | solution.py:374
  24.0 0.8 gather.1
  24.8 29.0 %all_to_all.21.z_ref = bf16[16,4,2560]{2,1,0:T(4,128)(2,1)S(1)} all-to-all(bf16[16,4,2560]{2,1,0:T(4,128)(2,1)S(1)} %gather.1), channel_id=1, replica_groups=mesh['y'=4,'z'=16,'x'=4,'core'=2] {'z'}, dimensions={0} | all-to-all | bytes 655360 | tf_op jit(solution)/shard_map/all_to_all | solution.py:374
  53.8 2.5 %legendre.1 = (f32[2,2,32,2,512]{4,3,2,1,0:T(2,128)}, bf16[16,4,2816]{2,1,0:T(4,128)(2,1)S(1)}, bf16[4,512,672]{2,1,0:T(8,128)(2,1)S(1)}) custom-call(s32[1]{0:T(128)} %bitcast.device_ref, s32[1024]{0:T(1024)} %slots_hbm.1, f32[32]{0:T(128)} %diffusion_hbm.1, bf16[16,4,2560]{2,1,0:T(4,128)(2,1)S(1)} %all_to_all.21.z_ref, ...), custom_call_target="tpu_custom_call" | custom-call | tf_op jit(solution)/shard_map/legendre/pallas_call | solution.py:426
  56.3 27.4 %all_to_all.22.z_ref = bf16[16,4,2816]{2,1,0:T(4,128)(2,1)S(1)} all-to-all(bf16[16,4,2816]{2,1,0:T(4,128)(2,1)S(1)} %get-tuple-element.18), channel_id=1, replica_groups=mesh['y'=4,'z'=16,'x'=4,'core'=2] {'z'}, dimensions={0} | all-to-all | bytes 720896 | tf_op jit(solution)/shard_map/all_to_all | solution.py:374
  83.7 0.9 scatter.1
  84.6 21.2 %all_to_all.23.y_ref = bf16[32,48,128]{2,1,0:T(8,128)(2,1)S(1)} all-to-all(bf16[32,48,128]{2,1,0:T(8,128)(2,1)S(1)} %scatter.1), channel_id=1, replica_groups=mesh['y'=4,'z'=16,'x'=4,'core'=2] {'y','x','core'}, dimensions={0} | all-to-all | bytes 786432 | tf_op jit(solution)/shard_map/all_to_all | solution.py:374
  105.8 2.6 %grid.1 = (f32[20,4,2688]{2,1,0:T(4,128)}, f32[8,128]{1,0:T(8,128)}) custom-call(s32[1]{0:T(128)} %bitcast.device_ref, s32[80,1]{1,0:T(8,128)S(1)} %get-tuple-element.13.kept_ref, s32[1,512]{1,0:T(1,128)S(1)} %get-tuple-element.14.order_ref, s32[128,8]{1,0:T(8,128)S(1)} %get-tuple-element.15.column_ref, bf16[32,48,128]{2,1,0:T(8,128)(2,1)S(1)} %all_to_all.23.y_ref, ...), custom_call_target="tpu_custom_call" | custom-call | tf_op jit(solution)/shard_map/grid/pallas_call | solution.py:456

commit v9 on v8

--- a/solution.py
+++ b/solution.py
@@ -126,7 +126,8 @@
 
 
 def fourier_kernel(
-    device_ref, kept_hbm, weights_hbm, slots_hbm, x_hbm, table_hbm, later_hbm, o_ref, order_ref, column_ref, kept_ref, later_ref, kept_s, weights_s, slots_v, x_v,
+    device_ref, kept_hbm, weights_hbm, diffusion_hbm, slots_hbm, x_hbm, table_hbm, o_ref, order_ref, column_ref,
+    kept_ref, wave_ref, diffusion_ref, kept_s, weights_s, diffusion_s, slots_v, x_v,
     table_v, even, odd, both, sems
 ):
     small = [
@@ -134,20 +135,30 @@
         pltpu.make_async_copy(x_hbm, x_v, sems.at[1]),
         pltpu.make_async_copy(kept_hbm, kept_s, sems.at[2]),
         pltpu.make_async_copy(weights_hbm, weights_s, sems.at[3]),
+        pltpu.make_async_copy(diffusion_hbm, diffusion_s, sems.at[4 + STEPS]),
     ]
     blocks = [pltpu.make_async_copy(table_hbm.at[i], table_v.at[i], sems.at[4 + i]) for i in range(STEPS)]
-    later = pltpu.make_async_copy(later_hbm, later_ref, sems.at[4 + STEPS])
-    for copy in small + blocks + [later]:
+    for copy in small + blocks:
         copy.start()
     lat = device_ref[0] // LEVS
     small[0].wait()
-    order = slot_order(slots_v[...])
+    slots = slots_v[...]
+    mine = iota((8, LANES), 0) * LANES + iota((8, LANES), 1) == device_ref[0] * 2
+    mine = jnp.sum(jnp.where(mine, slots.astype(F32), 0.0), axis=0, keepdims=True)
+    wave_ref[...] = jnp.broadcast_to(jnp.sum(mine, axis=1, keepdims=True).astype(jnp.int32), (1, LANES))
+    order = slot_order(slots)
     order_ref[...] = order
     lower = lower_of_pair(order)
     columns = [lower[:, i * LANES : (i + 1) * LANES] for i in range(4)]
     column_ref[...] = jnp.concatenate(columns + columns, axis=0).T
     small[2].wait()
     small[3].wait()
+    small[4].wait()
+    level = iota((2 * LEVELS, 1), 0) // 2
+    diffusion = jnp.zeros((2 * LEVELS, 1), F32)
+    for i in range(LEVELS):
+        diffusion = jnp.where(level == i, diffusion_s[i], diffusion)
+    diffusion_ref[...] = diffusion
     kept = latitude_column([kept_s[j] for j in range(BAND)], jnp.int32(0))
     kept_ref[...] = kept
     latitudes = [lat * BAND + j for j in range(BAND)]
@@ -199,7 +210,6 @@
             parts = swap_parts([block[k * CHUNK : (k + 1) * CHUNK] for k in range(YS)])
             for y in range(YS):
                 o_ref[y * LEVS + b] = parts[y].astype(BF16)
-    later.wait()
 
 
 def gather_kernel(y_ref, o_ref, rows):
@@ -233,16 +243,9 @@
 
 
 def legendre_kernel(
-    device_ref, slots_hbm, diffusion_hbm, z_ref, table_ref, later_hbm, spectral_hbm, o_ref, later_ref, slots_s, diffusion_s,
-    spectral_v, comb, sems
+    wave_ref, diffusion_ref, z_ref, table_ref, spectral_hbm, o_ref, spectral_v, comb, sems
 ):
-    copies = [
-        pltpu.make_async_copy(slots_hbm, slots_s, sems.at[0]),
-        pltpu.make_async_copy(diffusion_hbm, diffusion_s, sems.at[1]),
-    ]
-    later = pltpu.make_async_copy(later_hbm, later_ref, sems.at[2])
-    for copy in copies + [later]:
-        copy.start()
+    copies = []
     for group in range(NORTH * TILES // 4):
         north, south = [], []
         for u in range(4 * group, 4 * group + 4):
@@ -255,27 +258,23 @@
         south = jnp.concatenate(south, axis=0)
         comb[0, 16 * group : 16 * group + 16, :] = north + south
         comb[1, 16 * group : 16 * group + 16, :] = north - south
-    for copy in copies:
-        copy.wait()
-    copies = [later]
     column = iota((2 * LEVELS, HALF), 1)
-    level = iota((2 * LEVELS, 1), 0) // 2
-    diffusion = jnp.zeros((2 * LEVELS, 1), F32)
-    for i in range(LEVELS):
-        diffusion = jnp.where(level == i, diffusion_s[i], diffusion)
+    diffusion = diffusion_ref[...]
+    waves = [wave_ref[...], MM - 1 - wave_ref[...]]
+    waves = [jnp.concatenate([wave] * (HALF // LANES), axis=1) for wave in waves]
     power = [jnp.zeros((1, HALF), F32), jnp.zeros((1, HALF), F32)]
     halves = []
     for q in range(2):
         left = comb[q].T.astype(BF16)
         parts = []
         for t in range(2):
-            wave = slots_s[device_ref[0] * 2 + t]
+            wave = waves[t]
             raw = jnp.dot(left[64 * t : 64 * t + 64], table_ref[t, q], preferred_element_type=F32)
             degree = wave + 2 * column + q
             spectral = jnp.where(degree < MM, raw, 0.0)
             for level in range(LEVELS):
                 spectral_v[t, q, level] = spectral[2 * level : 2 * level + 2]
-            copies.append(pltpu.make_async_copy(spectral_v.at[t, q], spectral_hbm.at[t, q], sems.at[3 + 2 * t + q]))
+            copies.append(pltpu.make_async_copy(spectral_v.at[t, q], spectral_hbm.at[t, q], sems.at[2 * t + q]))
             copies[-1].start()
             degree = degree.astype(F32)
             ratio = degree * (degree + 1.0) / (MM * (MM + 1.0))
@@ -287,7 +286,10 @@
             )
             energy = jnp.sum(spectral * spectral, axis=0, keepdims=True)
             first = wave + q
-            moved = pltpu.roll(jnp.broadcast_to(energy, (8, HALF)), first // 2 % HALF, 1)[:1]
+            moved = jnp.broadcast_to(energy, (8, HALF))
+            for bit in range(9):
+                moved = jnp.where(first // 2**bit // 2 % 2 == 1, pltpu.roll(moved, 2**bit, 1), moved)
+            moved = moved[:1]
             for odd in range(2):
                 power[odd] += jnp.where(first % 2 == odd, moved, 0.0)
         halves.append(jnp.concatenate(parts, axis=1))
@@ -366,10 +368,6 @@
     return pltpu.with_memory_space_constraint(x, pltpu.HBM)
 
 
-def in_vmem(x):
-    return pltpu.with_memory_space_constraint(x, pltpu.VMEM)
-
-
 def exchange(x, axes):
     return lax.all_to_all(x, axes, split_axis=0, concat_axis=0, tiled=True)
 
@@ -379,20 +377,22 @@
     device = lax.axis_index(("y", "z", "x", "core")).astype(jnp.int32).reshape(1)
     chunk = (ZS, 4, YS * DATA + 2 * LANES)
 
-    sent, order, column, kept, legendre = pl.pallas_call(
+    sent, order, column, kept, wave, diffusion = pl.pallas_call(
         fourier_kernel,
         in_specs=[SMEM, HBM, HBM, HBM, HBM, HBM, HBM],
-        out_specs=[VMEM, VMEM, VMEM, VMEM, VMEM],
+        out_specs=[VMEM] * 6,
         out_shape=[
             jax.ShapeDtypeStruct((YS * LEVS, CHUNK, LANES), BF16),
             jax.ShapeDtypeStruct((1, HALF), jnp.int32),
             jax.ShapeDtypeStruct((LANES, 8), jnp.int32),
             jax.ShapeDtypeStruct((ROWS, 1), jnp.int32),
-            pltpu.VMEM(legendre.shape, BF16),
+            jax.ShapeDtypeStruct((1, LANES), jnp.int32),
+            jax.ShapeDtypeStruct((2 * LEVELS, 1), F32),
         ],
         scratch_shapes=[
             pltpu.SMEM((BAND,), jnp.int32),
             pltpu.SMEM((NLAT // 2,), F32),
+            pltpu.SMEM((LEVELS,), F32),
             pltpu.VMEM((8, LANES), jnp.int32),
             pltpu.VMEM((BAND, LEV, NLON), BF16),
             pltpu.VMEM((STEPS, QUARTER, 2 * BLOCK), BF16),
@@ -407,10 +407,10 @@
         device,
         in_hbm(kept_waves),
         in_hbm(weights),
+        in_hbm(diffusion),
         in_hbm(slot_wavenumber.reshape(8, LANES)),
         in_hbm(grid_fields.transpose(1, 0, 2)),
         in_hbm(jnp.asarray(forward_table)),
-        in_hbm(legendre),
     )
     arrived = exchange(sent, ("y", "x", "core"))
     gathered = pl.pallas_call(
@@ -423,25 +423,22 @@
         name="gather",
     )(arrived)
     gathered = exchange(gathered, ("z",))
-    spectral, back, table = pl.pallas_call(
+    spectral, back = pl.pallas_call(
         legendre_kernel,
-        in_specs=[SMEM, HBM, HBM, VMEM, VMEM, HBM],
-        out_specs=[HBM, VMEM, VMEM],
+        in_specs=[VMEM, VMEM, VMEM, VMEM],
+        out_specs=[HBM, VMEM],
         out_shape=[
             jax.ShapeDtypeStruct((2, 2, LEVELS, 2, HALF), F32),
             jax.ShapeDtypeStruct(chunk, BF16),
-            pltpu.VMEM((STEPS, 2 * BLOCK, QUARTER), BF16),
         ],
         scratch_shapes=[
-            pltpu.SMEM((MM,), jnp.int32),
-            pltpu.SMEM((LEVELS,), F32),
             pltpu.VMEM((2, 2, LEVELS, 2, HALF), F32),
             pltpu.VMEM((2, NLAT // 2, LANES), F32),
-            pltpu.SemaphoreType.DMA((7,)),
+            pltpu.SemaphoreType.DMA((4,)),
         ],
         compiler_params=PARAMS,
         name="legendre",
-    )(device, in_hbm(slot_wavenumber), in_hbm(diffusion), gathered, in_vmem(legendre), in_hbm(jnp.asarray(inverse_table)))
+    )(wave, diffusion, gathered, legendre)
     back = exchange(back, ("z",))
     scattered = pl.pallas_call(
         scatter_kernel,
@@ -463,7 +460,7 @@
         ],
         compiler_params=PARAMS,
         name="grid",
-    )(device, kept, order, column, returned, in_vmem(table))
+    )(device, kept, order, column, returned, jnp.asarray(inverse_table))
     return (
         grid_out.transpose(1, 0, 2),
         spectral,

time: 109 us -> 108 us (level)
  no operation moved by 1% of the time
where the time goes in v9:
time: 108 us
  blocking collectives  96.7 us (90%)
  Pallas kernels  10.7 us (10%)
    all_to_all x4, blocking collectives, exchange(): return lax.all_to_all(x, axes, split_axis=0, concat_axis=0, tiled=True)  96.7 us
    pallas_call x1, Pallas kernels, body(): pl.pallas_call(fourier_kernel, in_specs=[SMEM, HBM, HBM, HBM, HBM, HBM, H...  4.37 us
    pallas_call x1, Pallas kernels, body(): pl.pallas_call(grid_kernel, in_specs=[SMEM, VMEM, VMEM, VMEM, VMEM, VMEM]...  2.6 us

profile of v9, /device:TPU:1, one launch (start us, length us, event | category | flops | bytes accessed | tf_op | source)
XLA Modules:
  0.0 108.1 jit_solution(18093063620958827535)
XLA Ops:
  0.6 0.0 copy-start.1
  0.7 4.4 %fourier.1 = (bf16[32,40,128]{2,1,0:T(8,128)(2,1)S(1)}, s32[1,512]{1,0:T(1,128)S(1)}, s32[128,8]{1,0:T(8,128)S(1)}, s32[80,1]{1,0:T(8,128)S(1)}, s32[1,128]{1,0:T(1,128)S(1)}, /*index=5*/f32[64,1]{1,0:T(8,128)S(1)}) custom-call(s32[1]{0:T(128)} %bitcast.device_ref, s32[20]{0:T(128)} %kept_hbm.1, f32[640]{0:T(1024)} %weights_hbm.1, f32[32]{0:T(128)} %diffusion_hbm.1, ...), custom_call_target="tpu_custom_call" | custom-call | tf_op jit(solution)/shard_map/fourier/pallas_call | solution.py:380
  5.0 19.2 %all_to_all.20.y_ref = bf16[32,40,128]{2,1,0:T(8,128)(2,1)S(1)} all-to-all(bf16[32,40,128]{2,1,0:T(8,128)(2,1)S(1)} %get-tuple-element.18), channel_id=1, replica_groups=mesh['y'=4,'z'=16,'x'=4,'core'=2] {'y','x','core'}, dimensions={0} | all-to-all | bytes 655360 | tf_op jit(solution)/shard_map/all_to_all | solution.py:372
  24.2 0.8 gather.1
  25.0 29.0 %all_to_all.21.z_ref = bf16[16,4,2560]{2,1,0:T(4,128)(2,1)S(1)} all-to-all(bf16[16,4,2560]{2,1,0:T(4,128)(2,1)S(1)} %gather.1), channel_id=1, replica_groups=mesh['y'=4,'z'=16,'x'=4,'core'=2] {'z'}, dimensions={0} | all-to-all | bytes 655360 | tf_op jit(solution)/shard_map/all_to_all | solution.py:372
  54.0 0.0 copy-start
  54.0 0.0 copy-done.1
  54.0 2.1 %legendre.1 = (f32[2,2,32,2,512]{4,3,2,1,0:T(2,128)}, bf16[16,4,2816]{2,1,0:T(4,128)(2,1)S(1)}) custom-call(s32[1,128]{1,0:T(1,128)S(1)} %get-tuple-element.16.wave_ref, f32[64,1]{1,0:T(8,128)S(1)} %get-tuple-element.17.diffusion_ref, bf16[16,4,2560]{2,1,0:T(4,128)(2,1)S(1)} %all_to_all.21.z_ref, bf16[2,2,640,512]{3,2,1,0:T(8,128)(2,1)S(1)} %copy-done.1), custom_call_target="tpu_custom_call" | custom-call | tf_op jit(solution)/shard_map/legendre/pallas_call | solution.py:426
  56.1 27.4 %all_to_all.22.z_ref = bf16[16,4,2816]{2,1,0:T(4,128)(2,1)S(1)} all-to-all(bf16[16,4,2816]{2,1,0:T(4,128)(2,1)S(1)} %get-tuple-element.19), channel_id=1, replica_groups=mesh['y'=4,'z'=16,'x'=4,'core'=2] {'z'}, dimensions={0} | all-to-all | bytes 720896 | tf_op jit(solution)/shard_map/all_to_all | solution.py:372
  83.4 0.9 scatter.1
  84.3 21.2 %all_to_all.23.y_ref = bf16[32,48,128]{2,1,0:T(8,128)(2,1)S(1)} all-to-all(bf16[32,48,128]{2,1,0:T(8,128)(2,1)S(1)} %scatter.1), channel_id=1, replica_groups=mesh['y'=4,'z'=16,'x'=4,'core'=2] {'y','x','core'}, dimensions={0} | all-to-all | bytes 786432 | tf_op jit(solution)/shard_map/all_to_all | solution.py:372
  105.5 0.0 copy-done
  105.5 2.6 %grid.1 = (f32[20,4,2688]{2,1,0:T(4,128)}, f32[8,128]{1,0:T(8,128)}) custom-call(s32[1]{0:T(128)} %bitcast.device_ref, s32[80,1]{1,0:T(8,128)S(1)} %get-tuple-element.13.kept_ref, s32[1,512]{1,0:T(1,128)S(1)} %get-tuple-element.14.order_ref, s32[128,8]{1,0:T(8,128)S(1)} %get-tuple-element.15.column_ref, bf16[32,48,128]{2,1,0:T(8,128)(2,1)S(1)} %all_to_all.23.y_ref, ...), custom_call_target="tpu_custom_call" | custom-call | tf_op jit(solution)/shard_map/grid/pallas_call | solution.py:453
Async XLA Ops:
  0.6 53.3 %copy-start.1 = (bf16[2,2,640,512]{3,2,1,0:T(8,128)(2,1)S(1)}, bf16[2,2,640,512]{3,2,1,0:T(8,128)(2,1)}, u32[]{:S(2)}) copy-start(bf16[2,2,640,512]{3,2,1,0:T(8,128)(2,1)} %table_ref.2) | copy-start | bytes 7864324
  54.0 51.6 %copy-start = (bf16[4,512,672]{2,1,0:T(8,128)(2,1)S(1)}, bf16[4,512,672]{2,1,0:T(8,128)(2,1)}, u32[]{:S(2)}) copy-start(bf16[4,512,672]{2,1,0:T(8,128)(2,1)} %constant.28.clone.table_ref) | copy-start | bytes 8257540

commit v10 on v9

--- a/solution.py
+++ b/solution.py
@@ -68,10 +68,11 @@
     digits = jnp.concatenate([slots // 32, slots % 32], axis=0).astype(F32).astype(BF16)
     source = iota((LANES, HALF), 0)
     to = iota((LANES, HALF), 1)
-    choice = jnp.where(source == to % 8 * 16 + to // LATS * 2, 1.0, 0.0).astype(BF16)
+    choice = jnp.where(source == to // YS % 8 * 16 + to // LATS * 2, 1.0, 0.0).astype(BF16)
     moved = jnp.dot(digits, choice, preferred_element_type=F32)
     row = iota((16, HALF), 0)
-    mine = row % 8 == iota((16, HALF), 1) % LATS // 8
+    lane = iota((16, HALF), 1)
+    mine = row % 8 == lane % YS * 2 + lane // 32 % 2
     value = jnp.where(mine, moved * jnp.where(row < 8, 32.0, 1.0), 0.0)
     return jnp.sum(value, axis=0, keepdims=True).astype(jnp.int32)
 
@@ -97,7 +98,7 @@
 def row_choice(southern):
     to = iota((2 * ROWS, 2 * ROWS), 0)
     source = iota((2 * ROWS, 2 * ROWS), 1)
-    band = to // (2 * LEV)
+    band = to % CHUNK // (2 * LEV) * YS + to // CHUNK
     band = jnp.where(southern, BAND - 1 - band, band)
     wanted = (to % 2) * ROWS + band * LEV + to // 2 % LEV
     return jnp.where(source == wanted, 1.0, 0.0).astype(BF16)
@@ -118,10 +119,10 @@
 
 def swap_parts(parts):
     parts = list(parts)
-    parts[0], parts[1] = swap_lanes(parts[0], parts[1], ZS)
-    parts[2], parts[3] = swap_lanes(parts[2], parts[3], ZS)
-    parts[0], parts[2] = swap_lanes(parts[0], parts[2], 2 * ZS)
-    parts[1], parts[3] = swap_lanes(parts[1], parts[3], 2 * ZS)
+    parts[0], parts[1] = swap_lanes(parts[0], parts[1], 1)
+    parts[2], parts[3] = swap_lanes(parts[2], parts[3], 1)
+    parts[0], parts[2] = swap_lanes(parts[0], parts[2], 2)
+    parts[1], parts[3] = swap_lanes(parts[1], parts[3], 2)
     return parts
 
 
@@ -212,31 +213,25 @@
                 o_ref[y * LEVS + b] = parts[y].astype(BF16)
 
 
-def gather_kernel(y_ref, o_ref, rows):
+def gather_kernel(y_ref, o_ref):
     for y in range(YS):
         for j in range(TILES):
             block = [y_ref[y * LEVS + b, 8 * j : 8 * j + 8, :].astype(F32) for b in range(LEVS)]
-            turned = jnp.concatenate(block, axis=0).T
+            turned = jnp.concatenate(block, axis=0).astype(BF16).T.astype(F32)
             turned = jnp.concatenate([turned[:LATS], turned[LATS:]], axis=1)
-            for part in range(4):
-                row, tile = (part * TILES + j) % 4, y * TILES + (part * TILES + j) // 4
-                rows[:, row, tile * LANES : (tile + 1) * LANES] = turned[part * ZS : (part + 1) * ZS]
-    o_ref[...] = rows[...].astype(BF16)
-
-
-def scatter_kernel(z_ref, o_ref, rows):
-    rows[...] = z_ref[...].astype(F32)
+            place = (y * TILES + j) * LANES
+            o_ref[:, :, place : place + LANES] = turned.reshape(ZS, 4, LANES).astype(BF16)
+
+
+def scatter_kernel(z_ref, o_ref):
     for y in range(YS):
         for j in range(TILES):
-            block = []
-            for part in range(4):
-                row, tile = (part * TILES + j) % 4, y * TILES + (part * TILES + j) // 4
-                block.append(rows[:, row, tile * LANES : (tile + 1) * LANES])
-            block = jnp.concatenate(block, axis=0)
-            turned = jnp.concatenate([block[:, :LATS], block[:, LATS:]], axis=0).T
+            place = (y * TILES + j) * LANES
+            block = z_ref[:, :, place : place + LANES].astype(F32).reshape(LATS, LANES)
+            turned = jnp.concatenate([block[:, :LATS], block[:, LATS:]], axis=0).astype(BF16).T.astype(F32)
             for b in range(LEVS):
                 o_ref[y * LEVS + b, 8 + 8 * j : 16 + 8 * j, :] = turned[8 * b : 8 * b + 8].astype(BF16)
-    power = jnp.sum(rows[:, :, YS * DATA :], axis=0)
+    power = jnp.sum(z_ref[:, :, YS * DATA :].astype(F32), axis=0)
     power = jnp.concatenate([power[:, :LANES], power[:, LANES:]], axis=0)
     for peer in range(YS * LEVS):
         o_ref[peer, :8, :] = power.astype(BF16)
@@ -418,7 +413,6 @@
         in_specs=[VMEM],
         out_specs=VMEM,
         out_shape=jax.ShapeDtypeStruct((ZS, 4, YS * DATA), BF16),
-        scratch_shapes=[pltpu.VMEM((ZS, 4, YS * DATA), F32)],
         compiler_params=PARAMS,
         name="gather",
     )(arrived)
@@ -445,7 +439,6 @@
         in_specs=[VMEM],
         out_specs=VMEM,
         out_shape=jax.ShapeDtypeStruct((YS * LEVS, 8 + CHUNK, LANES), BF16),
-        scratch_shapes=[pltpu.VMEM(chunk, F32)],
         compiler_params=PARAMS,
         name="scatter",
     )(back)

time: 108 us -> 108 us (level)
  no operation moved by 1% of the time
where the time goes in v10:
time: 108 us
  blocking collectives  96.7 us (90%)
  Pallas kernels  10.2 us (9%)
    all_to_all x4, blocking collectives, exchange(): return lax.all_to_all(x, axes, split_axis=0, concat_axis=0, tiled=True)  96.7 us
    pallas_call x1, Pallas kernels, body(): pl.pallas_call(fourier_kernel, in_specs=[SMEM, HBM, HBM, HBM, HBM, HBM, H...  4.39 us
    pallas_call x1, Pallas kernels, body(): pl.pallas_call(grid_kernel, in_specs=[SMEM, VMEM, VMEM, VMEM, VMEM, VMEM]...  2.65 us

profile of v10, /device:TPU:1, one launch (start us, length us, event | category | flops | bytes accessed | tf_op | source)
XLA Modules:
  0.0 107.7 jit_solution(12854120334779216737)
XLA Ops:
  0.6 0.0 copy-start.1
  0.7 4.4 %fourier.1 = (bf16[32,40,128]{2,1,0:T(8,128)(2,1)S(1)}, s32[1,512]{1,0:T(1,128)S(1)}, s32[128,8]{1,0:T(8,128)S(1)}, s32[80,1]{1,0:T(8,128)S(1)}, s32[1,128]{1,0:T(1,128)S(1)}, /*index=5*/f32[64,1]{1,0:T(8,128)S(1)}) custom-call(s32[1]{0:T(128)} %bitcast.device_ref, s32[20]{0:T(128)} %kept_hbm.1, f32[640]{0:T(1024)} %weights_hbm.1, f32[32]{0:T(128)} %diffusion_hbm.1, ...), custom_call_target="tpu_custom_call" | custom-call | tf_op jit(solution)/shard_map/fourier/pallas_call | solution.py:375
  5.1 19.2 %all_to_all.20.y_ref = bf16[32,40,128]{2,1,0:T(8,128)(2,1)S(1)} all-to-all(bf16[32,40,128]{2,1,0:T(8,128)(2,1)S(1)} %get-tuple-element.18), channel_id=1, replica_groups=mesh['y'=4,'z'=16,'x'=4,'core'=2] {'y','x','core'}, dimensions={0} | all-to-all | bytes 655360 | tf_op jit(solution)/shard_map/all_to_all | solution.py:367
  24.2 0.4 gather.1
  24.6 29.0 %all_to_all.21.z_ref = bf16[16,4,2560]{2,1,0:T(4,128)(2,1)S(1)} all-to-all(bf16[16,4,2560]{2,1,0:T(4,128)(2,1)S(1)} %gather.1), channel_id=1, replica_groups=mesh['y'=4,'z'=16,'x'=4,'core'=2] {'z'}, dimensions={0} | all-to-all | bytes 655360 | tf_op jit(solution)/shard_map/all_to_all | solution.py:367
  53.6 0.0 copy-start
  53.6 0.0 copy-done.1
  53.6 2.1 %legendre.1 = (f32[2,2,32,2,512]{4,3,2,1,0:T(2,128)}, bf16[16,4,2816]{2,1,0:T(4,128)(2,1)S(1)}) custom-call(s32[1,128]{1,0:T(1,128)S(1)} %get-tuple-element.16.wave_ref, f32[64,1]{1,0:T(8,128)S(1)} %get-tuple-element.17.diffusion_ref, bf16[16,4,2560]{2,1,0:T(4,128)(2,1)S(1)} %all_to_all.21.z_ref, bf16[2,2,640,512]{3,2,1,0:T(8,128)(2,1)S(1)} %copy-done.1), custom_call_target="tpu_custom_call" | custom-call | tf_op jit(solution)/shard_map/legendre/pallas_call | solution.py:420
  55.7 27.4 %all_to_all.22.z_ref = bf16[16,4,2816]{2,1,0:T(4,128)(2,1)S(1)} all-to-all(bf16[16,4,2816]{2,1,0:T(4,128)(2,1)S(1)} %get-tuple-element.19), channel_id=1, replica_groups=mesh['y'=4,'z'=16,'x'=4,'core'=2] {'z'}, dimensions={0} | all-to-all | bytes 720896 | tf_op jit(solution)/shard_map/all_to_all | solution.py:367
  83.0 0.8 scatter.1
  83.8 21.2 %all_to_all.23.y_ref = bf16[32,48,128]{2,1,0:T(8,128)(2,1)S(1)} all-to-all(bf16[32,48,128]{2,1,0:T(8,128)(2,1)S(1)} %scatter.1), channel_id=1, replica_groups=mesh['y'=4,'z'=16,'x'=4,'core'=2] {'y','x','core'}, dimensions={0} | all-to-all | bytes 786432 | tf_op jit(solution)/shard_map/all_to_all | solution.py:367
  105.0 0.0 copy-done
  105.0 2.6 %grid.1 = (f32[20,4,2688]{2,1,0:T(4,128)}, f32[8,128]{1,0:T(8,128)}) custom-call(s32[1]{0:T(128)} %bitcast.device_ref, s32[80,1]{1,0:T(8,128)S(1)} %get-tuple-element.13.kept_ref, s32[1,512]{1,0:T(1,128)S(1)} %get-tuple-element.14.order_ref, s32[128,8]{1,0:T(8,128)S(1)} %get-tuple-element.15.column_ref, bf16[32,48,128]{2,1,0:T(8,128)(2,1)S(1)} %all_to_all.23.y_ref, ...), custom_call_target="tpu_custom_call" | custom-call | tf_op jit(solution)/shard_map/grid/pallas_call | solution.py:446
Async XLA Ops:
  0.6 52.9 %copy-start.1 = (bf16[2,2,640,512]{3,2,1,0:T(8,128)(2,1)S(1)}, bf16[2,2,640,512]{3,2,1,0:T(8,128)(2,1)}, u32[]{:S(2)}) copy-start(bf16[2,2,640,512]{3,2,1,0:T(8,128)(2,1)} %table_ref.2) | copy-start | bytes 7864324
  53.6 51.4 %copy-start = (bf16[4,512,672]{2,1,0:T(8,128)(2,1)S(1)}, bf16[4,512,672]{2,1,0:T(8,128)(2,1)}, u32[]{:S(2)}) copy-start(bf16[4,512,672]{2,1,0:T(8,128)(2,1)} %constant.28.clone.table_ref) | copy-start | bytes 8257540

commit v11 on v10

--- a/solution.py
+++ b/solution.py
@@ -64,17 +64,20 @@
     return place % LANES * STEPS + place // LANES
 
 
-def slot_order(slots):
-    digits = jnp.concatenate([slots // 32, slots % 32], axis=0).astype(F32).astype(BF16)
+def slot_moves():
     source = iota((LANES, HALF), 0)
     to = iota((LANES, HALF), 1)
     choice = jnp.where(source == to // YS % 8 * 16 + to // LATS * 2, 1.0, 0.0).astype(BF16)
-    moved = jnp.dot(digits, choice, preferred_element_type=F32)
     row = iota((16, HALF), 0)
     lane = iota((16, HALF), 1)
     mine = row % 8 == lane % YS * 2 + lane // 32 % 2
-    value = jnp.where(mine, moved * jnp.where(row < 8, 32.0, 1.0), 0.0)
-    return jnp.sum(value, axis=0, keepdims=True).astype(jnp.int32)
+    return choice, jnp.where(mine, jnp.where(row < 8, 32.0, 1.0), 0.0)
+
+
+def slot_order(slots, choice, digit):
+    digits = jnp.concatenate([slots // 32, slots % 32], axis=0).astype(F32).astype(BF16)
+    moved = jnp.dot(digits, choice, preferred_element_type=F32)
+    return jnp.sum(moved * digit, axis=0, keepdims=True).astype(jnp.int32)
 
 
 def latitude_column(scalars, zero):
@@ -95,9 +98,9 @@
     return jnp.minimum(wave, MM - 1 - wave)
 
 
-def row_choice(southern):
-    to = iota((2 * ROWS, 2 * ROWS), 0)
-    source = iota((2 * ROWS, 2 * ROWS), 1)
+def row_choice(southern, side):
+    to = iota((2 * ROWS, 2 * ROWS), side)
+    source = iota((2 * ROWS, 2 * ROWS), 1 - side)
     band = to % CHUNK // (2 * LEV) * YS + to // CHUNK
     band = jnp.where(southern, BAND - 1 - band, band)
     wanted = (to % 2) * ROWS + band * LEV + to // 2 % LEV
@@ -129,7 +132,7 @@
 def fourier_kernel(
     device_ref, kept_hbm, weights_hbm, diffusion_hbm, slots_hbm, x_hbm, table_hbm, o_ref, order_ref, column_ref,
     kept_ref, wave_ref, diffusion_ref, kept_s, weights_s, diffusion_s, slots_v, x_v,
-    table_v, even, odd, both, sems
+    table_v, even, odd, both, row_moves, moves, digit, sems
 ):
     small = [
         pltpu.make_async_copy(slots_hbm, slots_v, sems.at[0]),
@@ -142,28 +145,8 @@
     for copy in small + blocks:
         copy.start()
     lat = device_ref[0] // LEVS
-    small[0].wait()
-    slots = slots_v[...]
-    mine = iota((8, LANES), 0) * LANES + iota((8, LANES), 1) == device_ref[0] * 2
-    mine = jnp.sum(jnp.where(mine, slots.astype(F32), 0.0), axis=0, keepdims=True)
-    wave_ref[...] = jnp.broadcast_to(jnp.sum(mine, axis=1, keepdims=True).astype(jnp.int32), (1, LANES))
-    order = slot_order(slots)
-    order_ref[...] = order
-    lower = lower_of_pair(order)
-    columns = [lower[:, i * LANES : (i + 1) * LANES] for i in range(4)]
-    column_ref[...] = jnp.concatenate(columns + columns, axis=0).T
-    small[2].wait()
-    small[3].wait()
-    small[4].wait()
-    level = iota((2 * LEVELS, 1), 0) // 2
-    diffusion = jnp.zeros((2 * LEVELS, 1), F32)
-    for i in range(LEVELS):
-        diffusion = jnp.where(level == i, diffusion_s[i], diffusion)
-    diffusion_ref[...] = diffusion
-    kept = latitude_column([kept_s[j] for j in range(BAND)], jnp.int32(0))
-    kept_ref[...] = kept
-    latitudes = [lat * BAND + j for j in range(BAND)]
-    weight = latitude_column([weights_s[jnp.minimum(i, NLAT - 1 - i)] for i in latitudes], F32(0.0))
+    row_moves[...] = row_choice(lat >= NORTH, 0)
+    moves[...], digit[...] = slot_moves()
     small[1].wait()
 
     def put(ref, place, value):
@@ -180,8 +163,13 @@
         put(even.at[1], 16 * group, sums[0] - sums[1])
         put(odd, 16 * group, x[0] - x[2])
         put(odd, 16 * group + 2 * ROWS, x[1] - x[3])
+    for copy in small[:1] + small[2:] + blocks:
+        copy.wait()
+    kept = latitude_column([kept_s[j] for j in range(BAND)], jnp.int32(0))
+    kept_ref[...] = kept
+    latitudes = [lat * BAND + j for j in range(BAND)]
+    weight = latitude_column([weights_s[jnp.minimum(i, NLAT - 1 - i)] for i in latitudes], F32(0.0))
     for step in range(STEPS):
-        blocks[step].wait()
         if step % 2 == 0:
             raw = jnp.dot(even[step // 2], table_v[step], preferred_element_type=F32)
             raw = raw[:ROWS] + raw[ROWS:]
@@ -198,12 +186,25 @@
         fourier = jnp.concatenate([real * scale, imaginary * scale], axis=0).astype(BF16)
         both[: 2 * ROWS, step * LANES : (step + 1) * LANES] = fourier[:, :LANES]
         both[2 * ROWS :, (3 - step) * LANES : (4 - step) * LANES] = fourier[:, LANES:]
+    level = iota((2 * LEVELS, 1), 0) // 2
+    diffusion = jnp.zeros((2 * LEVELS, 1), F32)
+    for i in range(LEVELS):
+        diffusion = jnp.where(level == i, diffusion_s[i], diffusion)
+    diffusion_ref[...] = diffusion
+    slots = slots_v[...]
+    mine = iota((8, LANES), 0) * LANES + iota((8, LANES), 1) == device_ref[0] * 2
+    mine = jnp.sum(jnp.where(mine, slots.astype(F32), 0.0), axis=0, keepdims=True)
+    wave_ref[...] = jnp.broadcast_to(jnp.sum(mine, axis=1, keepdims=True).astype(jnp.int32), (1, LANES))
+    order = slot_order(slots, moves[...], digit[...])
+    order_ref[...] = order
+    lower = lower_of_pair(order)
+    columns = [lower[:, i * LANES : (i + 1) * LANES] for i in range(4)]
+    column_ref[...] = jnp.concatenate(columns + columns, axis=0).T
     choice = jnp.where(lower == pair_number((HALF, HALF), 0), 1.0, 0.0).astype(BF16)
     moved = jnp.dot(both[...], choice, preferred_element_type=F32)
     moved = sort_pair(order, moved[: 2 * ROWS], moved[2 * ROWS :])
-    choice = row_choice(lat >= NORTH)
     moved = jnp.concatenate([half.astype(BF16) for half in moved], axis=1)
-    moved = jnp.dot(choice, moved, preferred_element_type=F32)
+    moved = jnp.dot(row_moves[...], moved, preferred_element_type=F32)
     for i in range(LEVS // 2):
         place = i * LANES
         pair = swap_lanes(moved[:, place : place + LANES], moved[:, HALF + place : HALF + place + LANES], LATS)
@@ -228,7 +229,7 @@
         for j in range(TILES):
             place = (y * TILES + j) * LANES
             block = z_ref[:, :, place : place + LANES].astype(F32).reshape(LATS, LANES)
-            turned = jnp.concatenate([block[:, :LATS], block[:, LATS:]], axis=0).astype(BF16).T.astype(F32)
+            turned = jnp.concatenate([block[:, :LATS], block[:, LATS:]], axis=0).T
             for b in range(LEVS):
                 o_ref[y * LEVS + b, 8 + 8 * j : 16 + 8 * j, :] = turned[8 * b : 8 * b + 8].astype(BF16)
     power = jnp.sum(z_ref[:, :, YS * DATA :].astype(F32), axis=0)
@@ -260,7 +261,7 @@
     power = [jnp.zeros((1, HALF), F32), jnp.zeros((1, HALF), F32)]
     halves = []
     for q in range(2):
-        left = comb[q].T.astype(BF16)
+        left = comb[q].astype(BF16).T
         parts = []
         for t in range(2):
             wave = waves[t]
@@ -311,7 +312,7 @@
 
 def grid_kernel(device_ref, kept_ref, order_ref, column_ref, y_ref, table_ref, o_ref, spectrum_ref):
     kept = kept_ref[...]
-    choice = row_choice(device_ref[0] >= NORTH * LEVS)
+    choice = row_choice(device_ref[0] >= NORTH * LEVS, 1)
     firsts, seconds = [], []
     for i in range(LEVS // 2):
         pair = []
@@ -323,7 +324,7 @@
         seconds.append(second)
     back = sort_pair(order_ref[...], jnp.concatenate(firsts, axis=1), jnp.concatenate(seconds, axis=1))
     back = jnp.concatenate([half.astype(BF16) for half in back], axis=1)
-    rows = lax.dot_general(choice, back, (((0,), (0,)), ((), ())), preferred_element_type=F32).astype(BF16)
+    rows = jnp.dot(choice, back, preferred_element_type=F32).astype(BF16)
     rows = jnp.concatenate([rows[:, :HALF], rows[:, HALF:]], axis=0)
     number = pair_number((LANES, HALF), 1)
     choice = [jnp.where(column_ref[:, i : i + 1] == number, 1.0, 0.0).astype(BF16) for i in range(HALF // LANES)]
@@ -394,6 +395,9 @@
             pltpu.VMEM((2, 2 * ROWS, QUARTER), BF16),
             pltpu.VMEM((4 * ROWS, QUARTER), BF16),
             pltpu.VMEM((4 * ROWS, HALF), BF16),
+            pltpu.VMEM((2 * ROWS, 2 * ROWS), BF16),
+            pltpu.VMEM((LANES, HALF), BF16),
+            pltpu.VMEM((16, HALF), F32),
             pltpu.SemaphoreType.DMA((5 + STEPS,)),
         ],
         compiler_params=PARAMS,

time: 108 us -> 107 us (level)
  no operation moved by 1% of the time
where the time goes in v11:
time: 107 us
  blocking collectives  96.7 us (90%)
  Pallas kernels  9.36 us (9%)
    all_to_all x4, blocking collectives, exchange(): return lax.all_to_all(x, axes, split_axis=0, concat_axis=0, tiled=True)  96.7 us
    pallas_call x1, Pallas kernels, body(): pl.pallas_call(fourier_kernel, in_specs=[SMEM, HBM, HBM, HBM, HBM, HBM, H...  4.07 us
    pallas_call x1, Pallas kernels, body(): pl.pallas_call(grid_kernel, in_specs=[SMEM, VMEM, VMEM, VMEM, VMEM, VMEM]...  2.54 us

profile of v11, /device:TPU:1, one launch (start us, length us, event | category | flops | bytes accessed | tf_op | source)
XLA Modules:
  0.0 106.8 jit_solution(7599686089827251530)
XLA Ops:
  0.6 0.0 copy-start.1
  0.7 4.1 %fourier.1 = (bf16[32,40,128]{2,1,0:T(8,128)(2,1)S(1)}, s32[1,512]{1,0:T(1,128)S(1)}, s32[128,8]{1,0:T(8,128)S(1)}, s32[80,1]{1,0:T(8,128)S(1)}, s32[1,128]{1,0:T(1,128)S(1)}, /*index=5*/f32[64,1]{1,0:T(8,128)S(1)}) custom-call(s32[1]{0:T(128)} %bitcast.device_ref, s32[20]{0:T(128)} %kept_hbm.1, f32[640]{0:T(1024)} %weights_hbm.1, f32[32]{0:T(128)} %diffusion_hbm.1, ...), custom_call_target="tpu_custom_call" | custom-call | tf_op jit(solution)/shard_map/fourier/pallas_call | solution.py:376
  4.7 19.2 %all_to_all.20.y_ref = bf16[32,40,128]{2,1,0:T(8,128)(2,1)S(1)} all-to-all(bf16[32,40,128]{2,1,0:T(8,128)(2,1)S(1)} %get-tuple-element.18), channel_id=1, replica_groups=mesh['y'=4,'z'=16,'x'=4,'core'=2] {'y','x','core'}, dimensions={0} | all-to-all | bytes 655360 | tf_op jit(solution)/shard_map/all_to_all | solution.py:368
  23.9 0.4 gather.1
  24.3 29.0 %all_to_all.21.z_ref = bf16[16,4,2560]{2,1,0:T(4,128)(2,1)S(1)} all-to-all(bf16[16,4,2560]{2,1,0:T(4,128)(2,1)S(1)} %gather.1), channel_id=1, replica_groups=mesh['y'=4,'z'=16,'x'=4,'core'=2] {'z'}, dimensions={0} | all-to-all | bytes 655360 | tf_op jit(solution)/shard_map/all_to_all | solution.py:368
  53.2 0.0 copy-start
  53.2 0.0 copy-done.1
  53.2 1.9 %legendre.1 = (f32[2,2,32,2,512]{4,3,2,1,0:T(2,128)}, bf16[16,4,2816]{2,1,0:T(4,128)(2,1)S(1)}) custom-call(s32[1,128]{1,0:T(1,128)S(1)} %get-tuple-element.16.wave_ref, f32[64,1]{1,0:T(8,128)S(1)} %get-tuple-element.17.diffusion_ref, bf16[16,4,2560]{2,1,0:T(4,128)(2,1)S(1)} %all_to_all.21.z_ref, bf16[2,2,640,512]{3,2,1,0:T(8,128)(2,1)S(1)} %copy-done.1), custom_call_target="tpu_custom_call" | custom-call | tf_op jit(solution)/shard_map/legendre/pallas_call | solution.py:424
  55.1 27.4 %all_to_all.22.z_ref = bf16[16,4,2816]{2,1,0:T(4,128)(2,1)S(1)} all-to-all(bf16[16,4,2816]{2,1,0:T(4,128)(2,1)S(1)} %get-tuple-element.19), channel_id=1, replica_groups=mesh['y'=4,'z'=16,'x'=4,'core'=2] {'z'}, dimensions={0} | all-to-all | bytes 720896 | tf_op jit(solution)/shard_map/all_to_all | solution.py:368
  82.5 0.5 scatter.1
  83.0 21.2 %all_to_all.23.y_ref = bf16[32,48,128]{2,1,0:T(8,128)(2,1)S(1)} all-to-all(bf16[32,48,128]{2,1,0:T(8,128)(2,1)S(1)} %scatter.1), channel_id=1, replica_groups=mesh['y'=4,'z'=16,'x'=4,'core'=2] {'y','x','core'}, dimensions={0} | all-to-all | bytes 786432 | tf_op jit(solution)/shard_map/all_to_all | solution.py:368
  104.2 0.0 copy-done
  104.2 2.5 %grid.1 = (f32[20,4,2688]{2,1,0:T(4,128)}, f32[8,128]{1,0:T(8,128)}) custom-call(s32[1]{0:T(128)} %bitcast.device_ref, s32[80,1]{1,0:T(8,128)S(1)} %get-tuple-element.13.kept_ref, s32[1,512]{1,0:T(1,128)S(1)} %get-tuple-element.14.order_ref, s32[128,8]{1,0:T(8,128)S(1)} %get-tuple-element.15.column_ref, bf16[32,48,128]{2,1,0:T(8,128)(2,1)S(1)} %all_to_all.23.y_ref, ...), custom_call_target="tpu_custom_call" | custom-call | tf_op jit(solution)/shard_map/grid/pallas_call | solution.py:450
Async XLA Ops:
  0.6 52.6 %copy-start.1 = (bf16[2,2,640,512]{3,2,1,0:T(8,128)(2,1)S(1)}, bf16[2,2,640,512]{3,2,1,0:T(8,128)(2,1)}, u32[]{:S(2)}) copy-start(bf16[2,2,640,512]{3,2,1,0:T(8,128)(2,1)} %table_ref.2) | copy-start | bytes 7864324
  53.2 51.0 %copy-start = (bf16[4,512,672]{2,1,0:T(8,128)(2,1)S(1)}, bf16[4,512,672]{2,1,0:T(8,128)(2,1)}, u32[]{:S(2)}) copy-start(bf16[4,512,672]{2,1,0:T(8,128)(2,1)} %constant.28.clone.table_ref) | copy-start | bytes 8257540

commit v12 on v11

--- a/solution.py
+++ b/solution.py
@@ -51,7 +51,7 @@
     numbers = places[None, :] * STEPS + np.arange(STEPS)[:, None]
     forward = np.stack([cosine[:, numbers], sine[:, numbers]], axis=2)
     forward = np.ascontiguousarray(forward.transpose(1, 0, 2, 3)).reshape(STEPS, QUARTER, 2 * BLOCK)
-    inverse = np.ascontiguousarray(forward.transpose(0, 2, 1))
+    inverse = np.ascontiguousarray(forward.transpose(0, 2, 1)[[0, 2, 1, 3]])
     return forward, inverse
 
 
@@ -329,7 +329,7 @@
     number = pair_number((LANES, HALF), 1)
     choice = [jnp.where(column_ref[:, i : i + 1] == number, 1.0, 0.0).astype(BF16) for i in range(HALF // LANES)]
     numbered = jnp.dot(rows, jnp.concatenate(choice, axis=0), preferred_element_type=F32)
-    parts = []
+    lefts = []
     for step in range(STEPS):
         low = numbered[: 2 * ROWS, step * LANES : (step + 1) * LANES]
         high = numbered[2 * ROWS :, (3 - step) * LANES : (4 - step) * LANES]
@@ -342,9 +342,12 @@
             left = jnp.concatenate([left, jnp.concatenate([-imaginary, real], axis=1)], axis=0)
         if step == 3:
             left = jnp.concatenate([left, jnp.concatenate([imaginary, -real], axis=1)], axis=0)
-        parts.append(jnp.dot(left.astype(BF16), table_ref[step], preferred_element_type=F32))
-    odd = parts[1] + parts[3]
-    plus, minus = parts[0] + parts[2], parts[0] - parts[2]
+        lefts.append(left.astype(BF16))
+    table = table_ref[2:].reshape(4 * BLOCK, QUARTER)
+    odd = jnp.dot(jnp.concatenate([lefts[1], lefts[3]], axis=1), table, preferred_element_type=F32)
+    first = jnp.dot(lefts[0], table_ref[0], preferred_element_type=F32)
+    second = jnp.dot(lefts[2], table_ref[1], preferred_element_type=F32)
+    plus, minus = first + second, first - second
     for group in range(ROWS // 16):
         place = slice(16 * group, 16 * group + 16)
         turned = slice(ROWS + 16 * group, ROWS + 16 * group + 16)

time: 107 us -> 107 us (level)
  no operation moved by 1% of the time
where the time goes in v12:
time: 107 us
  blocking collectives  96.7 us (90%)
  Pallas kernels  9.26 us (9%)
    all_to_all x4, blocking collectives, exchange(): return lax.all_to_all(x, axes, split_axis=0, concat_axis=0, tiled=True)  96.7 us
    pallas_call x1, Pallas kernels, body(): pl.pallas_call(fourier_kernel, in_specs=[SMEM, HBM, HBM, HBM, HBM, HBM, H...  4.07 us
    pallas_call x1, Pallas kernels, body(): pl.pallas_call(grid_kernel, in_specs=[SMEM, VMEM, VMEM, VMEM, VMEM, VMEM]...  2.44 us

profile of v12, /device:TPU:1, one launch (start us, length us, event | category | flops | bytes accessed | tf_op | source)
XLA Modules:
  0.0 106.7 jit_solution(15424500002262600460)
XLA Ops:
  0.6 0.0 copy-start.1
  0.7 4.1 %fourier.1 = (bf16[32,40,128]{2,1,0:T(8,128)(2,1)S(1)}, s32[1,512]{1,0:T(1,128)S(1)}, s32[128,8]{1,0:T(8,128)S(1)}, s32[80,1]{1,0:T(8,128)S(1)}, s32[1,128]{1,0:T(1,128)S(1)}, /*index=5*/f32[64,1]{1,0:T(8,128)S(1)}) custom-call(s32[1]{0:T(128)} %bitcast.device_ref, s32[20]{0:T(128)} %kept_hbm.1, f32[640]{0:T(1024)} %weights_hbm.1, f32[32]{0:T(128)} %diffusion_hbm.1, ...), custom_call_target="tpu_custom_call" | custom-call | tf_op jit(solution)/shard_map/fourier/pallas_call | solution.py:379
  4.7 19.2 %all_to_all.20.y_ref = bf16[32,40,128]{2,1,0:T(8,128)(2,1)S(1)} all-to-all(bf16[32,40,128]{2,1,0:T(8,128)(2,1)S(1)} %get-tuple-element.18), channel_id=1, replica_groups=mesh['y'=4,'z'=16,'x'=4,'core'=2] {'y','x','core'}, dimensions={0} | all-to-all | bytes 655360 | tf_op jit(solution)/shard_map/all_to_all | solution.py:371
  23.9 0.4 gather.1
  24.3 29.0 %all_to_all.21.z_ref = bf16[16,4,2560]{2,1,0:T(4,128)(2,1)S(1)} all-to-all(bf16[16,4,2560]{2,1,0:T(4,128)(2,1)S(1)} %gather.1), channel_id=1, replica_groups=mesh['y'=4,'z'=16,'x'=4,'core'=2] {'z'}, dimensions={0} | all-to-all | bytes 655360 | tf_op jit(solution)/shard_map/all_to_all | solution.py:371
  53.2 0.0 copy-start
  53.2 0.0 copy-done.1
  53.2 1.9 %legendre.1 = (f32[2,2,32,2,512]{4,3,2,1,0:T(2,128)}, bf16[16,4,2816]{2,1,0:T(4,128)(2,1)S(1)}) custom-call(s32[1,128]{1,0:T(1,128)S(1)} %get-tuple-element.16.wave_ref, f32[64,1]{1,0:T(8,128)S(1)} %get-tuple-element.17.diffusion_ref, bf16[16,4,2560]{2,1,0:T(4,128)(2,1)S(1)} %all_to_all.21.z_ref, bf16[2,2,640,512]{3,2,1,0:T(8,128)(2,1)S(1)} %copy-done.1), custom_call_target="tpu_custom_call" | custom-call | tf_op jit(solution)/shard_map/legendre/pallas_call | solution.py:427
  55.1 27.4 %all_to_all.22.z_ref = bf16[16,4,2816]{2,1,0:T(4,128)(2,1)S(1)} all-to-all(bf16[16,4,2816]{2,1,0:T(4,128)(2,1)S(1)} %get-tuple-element.19), channel_id=1, replica_groups=mesh['y'=4,'z'=16,'x'=4,'core'=2] {'z'}, dimensions={0} | all-to-all | bytes 720896 | tf_op jit(solution)/shard_map/all_to_all | solution.py:371
  82.5 0.5 scatter.1
  83.0 21.2 %all_to_all.23.y_ref = bf16[32,48,128]{2,1,0:T(8,128)(2,1)S(1)} all-to-all(bf16[32,48,128]{2,1,0:T(8,128)(2,1)S(1)} %scatter.1), channel_id=1, replica_groups=mesh['y'=4,'z'=16,'x'=4,'core'=2] {'y','x','core'}, dimensions={0} | all-to-all | bytes 786432 | tf_op jit(solution)/shard_map/all_to_all | solution.py:371
  104.2 0.0 copy-done
  104.2 2.4 %grid.1 = (f32[20,4,2688]{2,1,0:T(4,128)}, f32[8,128]{1,0:T(8,128)}) custom-call(s32[1]{0:T(128)} %bitcast.device_ref, s32[80,1]{1,0:T(8,128)S(1)} %get-tuple-element.13.kept_ref, s32[1,512]{1,0:T(1,128)S(1)} %get-tuple-element.14.order_ref, s32[128,8]{1,0:T(8,128)S(1)} %get-tuple-element.15.column_ref, bf16[32,48,128]{2,1,0:T(8,128)(2,1)S(1)} %all_to_all.23.y_ref, ...), custom_call_target="tpu_custom_call" | custom-call | tf_op jit(solution)/shard_map/grid/pallas_call | solution.py:453
Async XLA Ops:
  0.6 52.6 %copy-start.1 = (bf16[2,2,640,512]{3,2,1,0:T(8,128)(2,1)S(1)}, bf16[2,2,640,512]{3,2,1,0:T(8,128)(2,1)}, u32[]{:S(2)}) copy-start(bf16[2,2,640,512]{3,2,1,0:T(8,128)(2,1)} %table_ref.2) | copy-start | bytes 7864324
  53.2 51.0 %copy-start = (bf16[4,512,672]{2,1,0:T(8,128)(2,1)S(1)}, bf16[4,512,672]{2,1,0:T(8,128)(2,1)}, u32[]{:S(2)}) copy-start(bf16[4,512,672]{2,1,0:T(8,128)(2,1)} %constant.28.clone.table_ref) | copy-start | bytes 8257540

commit v13 on v12

--- a/solution.py
+++ b/solution.py
@@ -52,6 +52,7 @@
     forward = np.stack([cosine[:, numbers], sine[:, numbers]], axis=2)
     forward = np.ascontiguousarray(forward.transpose(1, 0, 2, 3)).reshape(STEPS, QUARTER, 2 * BLOCK)
     inverse = np.ascontiguousarray(forward.transpose(0, 2, 1)[[0, 2, 1, 3]])
+    forward = np.stack([np.concatenate([forward[i], forward[i + 2]], axis=1) for i in range(2)])
     return forward, inverse
 
 
@@ -141,7 +142,7 @@
         pltpu.make_async_copy(weights_hbm, weights_s, sems.at[3]),
         pltpu.make_async_copy(diffusion_hbm, diffusion_s, sems.at[4 + STEPS]),
     ]
-    blocks = [pltpu.make_async_copy(table_hbm.at[i], table_v.at[i], sems.at[4 + i]) for i in range(STEPS)]
+    blocks = [pltpu.make_async_copy(table_hbm.at[i], table_v.at[i], sems.at[4 + i]) for i in range(2)]
     for copy in small + blocks:
         copy.start()
     lat = device_ref[0] // LEVS
@@ -169,13 +170,15 @@
     kept_ref[...] = kept
     latitudes = [lat * BAND + j for j in range(BAND)]
     weight = latitude_column([weights_s[jnp.minimum(i, NLAT - 1 - i)] for i in latitudes], F32(0.0))
+    turned = jnp.dot(odd[...], table_v[1], preferred_element_type=F32)
     for step in range(STEPS):
         if step % 2 == 0:
-            raw = jnp.dot(even[step // 2], table_v[step], preferred_element_type=F32)
+            columns = slice(step * BLOCK, step * BLOCK + 2 * BLOCK)
+            raw = jnp.dot(even[step // 2], table_v[0, :, columns], preferred_element_type=F32)
             raw = raw[:ROWS] + raw[ROWS:]
             real, imaginary = raw[:, :BLOCK], raw[:, BLOCK:]
         else:
-            raw = jnp.dot(odd[...], table_v[step], preferred_element_type=F32)
+            raw = turned[:, (step - 1) * BLOCK : (step + 1) * BLOCK]
             first = raw[:ROWS] + raw[ROWS : 2 * ROWS]
             second = raw[2 * ROWS : 3 * ROWS] + raw[3 * ROWS :]
             if step == 3:
@@ -394,7 +397,7 @@
             pltpu.SMEM((LEVELS,), F32),
             pltpu.VMEM((8, LANES), jnp.int32),
             pltpu.VMEM((BAND, LEV, NLON), BF16),
-            pltpu.VMEM((STEPS, QUARTER, 2 * BLOCK), BF16),
+            pltpu.VMEM((2, QUARTER, 4 * BLOCK), BF16),
             pltpu.VMEM((2, 2 * ROWS, QUARTER), BF16),
             pltpu.VMEM((4 * ROWS, QUARTER), BF16),
             pltpu.VMEM((4 * ROWS, HALF), BF16),

time: 107 us -> 107 us (level)
  no operation moved by 1% of the time
where the time goes in v13:
time: 107 us
  blocking collectives  96.7 us (90%)
  Pallas kernels  9.12 us (9%)
    all_to_all x4, blocking collectives, exchange(): return lax.all_to_all(x, axes, split_axis=0, concat_axis=0, tiled=True)  96.7 us
    pallas_call x1, Pallas kernels, body(): pl.pallas_call(fourier_kernel, in_specs=[SMEM, HBM, HBM, HBM, HBM, HBM, H...  3.92 us
    pallas_call x1, Pallas kernels, body(): pl.pallas_call(grid_kernel, in_specs=[SMEM, VMEM, VMEM, VMEM, VMEM, VMEM]...  2.45 us

profile of v13, /device:TPU:1, one launch (start us, length us, event | category | flops | bytes accessed | tf_op | source)
XLA Modules:
  0.0 106.5 jit_solution(2106134532698169295)
XLA Ops:
  0.6 0.0 copy-start.1
  0.7 3.9 %fourier.1 = (bf16[32,40,128]{2,1,0:T(8,128)(2,1)S(1)}, s32[1,512]{1,0:T(1,128)S(1)}, s32[128,8]{1,0:T(8,128)S(1)}, s32[80,1]{1,0:T(8,128)S(1)}, s32[1,128]{1,0:T(1,128)S(1)}, /*index=5*/f32[64,1]{1,0:T(8,128)S(1)}) custom-call(s32[1]{0:T(128)} %bitcast.device_ref, s32[20]{0:T(128)} %kept_hbm.1, f32[640]{0:T(1024)} %weights_hbm.1, f32[32]{0:T(128)} %diffusion_hbm.1, ...), custom_call_target="tpu_custom_call" | custom-call | tf_op jit(solution)/shard_map/fourier/pallas_call | solution.py:382
  4.6 19.2 %all_to_all.20.y_ref = bf16[32,40,128]{2,1,0:T(8,128)(2,1)S(1)} all-to-all(bf16[32,40,128]{2,1,0:T(8,128)(2,1)S(1)} %get-tuple-element.18), channel_id=1, replica_groups=mesh['y'=4,'z'=16,'x'=4,'core'=2] {'y','x','core'}, dimensions={0} | all-to-all | bytes 655360 | tf_op jit(solution)/shard_map/all_to_all | solution.py:374
  23.7 0.4 gather.1
  24.1 29.0 %all_to_all.21.z_ref = bf16[16,4,2560]{2,1,0:T(4,128)(2,1)S(1)} all-to-all(bf16[16,4,2560]{2,1,0:T(4,128)(2,1)S(1)} %gather.1), channel_id=1, replica_groups=mesh['y'=4,'z'=16,'x'=4,'core'=2] {'z'}, dimensions={0} | all-to-all | bytes 655360 | tf_op jit(solution)/shard_map/all_to_all | solution.py:374
  53.1 0.0 copy-start
  53.1 0.0 copy-done.1
  53.1 1.8 %legendre.1 = (f32[2,2,32,2,512]{4,3,2,1,0:T(2,128)}, bf16[16,4,2816]{2,1,0:T(4,128)(2,1)S(1)}) custom-call(s32[1,128]{1,0:T(1,128)S(1)} %get-tuple-element.16.wave_ref, f32[64,1]{1,0:T(8,128)S(1)} %get-tuple-element.17.diffusion_ref, bf16[16,4,2560]{2,1,0:T(4,128)(2,1)S(1)} %all_to_all.21.z_ref, bf16[2,2,640,512]{3,2,1,0:T(8,128)(2,1)S(1)} %copy-done.1), custom_call_target="tpu_custom_call" | custom-call | tf_op jit(solution)/shard_map/legendre/pallas_call | solution.py:430
  55.0 27.3 %all_to_all.22.z_ref = bf16[16,4,2816]{2,1,0:T(4,128)(2,1)S(1)} all-to-all(bf16[16,4,2816]{2,1,0:T(4,128)(2,1)S(1)} %get-tuple-element.19), channel_id=1, replica_groups=mesh['y'=4,'z'=16,'x'=4,'core'=2] {'z'}, dimensions={0} | all-to-all | bytes 720896 | tf_op jit(solution)/shard_map/all_to_all | solution.py:374
  82.3 0.5 scatter.1
  82.9 21.2 %all_to_all.23.y_ref = bf16[32,48,128]{2,1,0:T(8,128)(2,1)S(1)} all-to-all(bf16[32,48,128]{2,1,0:T(8,128)(2,1)S(1)} %scatter.1), channel_id=1, replica_groups=mesh['y'=4,'z'=16,'x'=4,'core'=2] {'y','x','core'}, dimensions={0} | all-to-all | bytes 786432 | tf_op jit(solution)/shard_map/all_to_all | solution.py:374
  104.1 0.0 copy-done
  104.1 2.5 %grid.1 = (f32[20,4,2688]{2,1,0:T(4,128)}, f32[8,128]{1,0:T(8,128)}) custom-call(s32[1]{0:T(128)} %bitcast.device_ref, s32[80,1]{1,0:T(8,128)S(1)} %get-tuple-element.13.kept_ref, s32[1,512]{1,0:T(1,128)S(1)} %get-tuple-element.14.order_ref, s32[128,8]{1,0:T(8,128)S(1)} %get-tuple-element.15.column_ref, bf16[32,48,128]{2,1,0:T(8,128)(2,1)S(1)} %all_to_all.23.y_ref, ...), custom_call_target="tpu_custom_call" | custom-call | tf_op jit(solution)/shard_map/grid/pallas_call | solution.py:456
Async XLA Ops:
  0.6 52.5 %copy-start.1 = (bf16[2,2,640,512]{3,2,1,0:T(8,128)(2,1)S(1)}, bf16[2,2,640,512]{3,2,1,0:T(8,128)(2,1)}, u32[]{:S(2)}) copy-start(bf16[2,2,640,512]{3,2,1,0:T(8,128)(2,1)} %table_ref.2) | copy-start | bytes 7864324
  53.1 51.0 %copy-start = (bf16[4,512,672]{2,1,0:T(8,128)(2,1)S(1)}, bf16[4,512,672]{2,1,0:T(8,128)(2,1)}, u32[]{:S(2)}) copy-start(bf16[4,512,672]{2,1,0:T(8,128)(2,1)} %constant.28.clone.table_ref) | copy-start | bytes 8257540

commit v14 on v13

--- a/solution.py
+++ b/solution.py
@@ -255,8 +255,8 @@
                 side.append(z_ref[z, :, place : place + LANES].astype(F32))
         north = jnp.concatenate(north, axis=0)
         south = jnp.concatenate(south, axis=0)
-        comb[0, 16 * group : 16 * group + 16, :] = north + south
-        comb[1, 16 * group : 16 * group + 16, :] = north - south
+        comb[0, 16 * group : 16 * group + 16, :] = (north + south).astype(BF16)
+        comb[1, 16 * group : 16 * group + 16, :] = (north - south).astype(BF16)
     column = iota((2 * LEVELS, HALF), 1)
     diffusion = diffusion_ref[...]
     waves = [wave_ref[...], MM - 1 - wave_ref[...]]
@@ -264,7 +264,7 @@
     power = [jnp.zeros((1, HALF), F32), jnp.zeros((1, HALF), F32)]
     halves = []
     for q in range(2):
-        left = comb[q].astype(BF16).T
+        left = comb[q].T
         parts = []
         for t in range(2):
             wave = waves[t]
@@ -437,7 +437,7 @@
         ],
         scratch_shapes=[
             pltpu.VMEM((2, 2, LEVELS, 2, HALF), F32),
-            pltpu.VMEM((2, NLAT // 2, LANES), F32),
+            pltpu.VMEM((2, NLAT // 2, LANES), BF16),
             pltpu.SemaphoreType.DMA((4,)),
         ],
         compiler_params=PARAMS,

time: 107 us -> 107 us (level)
  no operation moved by 1% of the time
where the time goes in v14:
time: 107 us
  blocking collectives  96.7 us (90%)
  Pallas kernels  9.19 us (9%)
    all_to_all x4, blocking collectives, exchange(): return lax.all_to_all(x, axes, split_axis=0, concat_axis=0, tiled=True)  96.7 us
    pallas_call x1, Pallas kernels, body(): pl.pallas_call(fourier_kernel, in_specs=[SMEM, HBM, HBM, HBM, HBM, HBM, H...  3.92 us
    pallas_call x1, Pallas kernels, body(): pl.pallas_call(grid_kernel, in_specs=[SMEM, VMEM, VMEM, VMEM, VMEM, VMEM]...  2.46 us

profile of v14, /device:TPU:1, one launch (start us, length us, event | category | flops | bytes accessed | tf_op | source)
XLA Modules:
  0.0 106.6 jit_solution(11536013488780276785)
XLA Ops:
  0.6 0.0 copy-start.1
  0.7 3.9 %fourier.1 = (bf16[32,40,128]{2,1,0:T(8,128)(2,1)S(1)}, s32[1,512]{1,0:T(1,128)S(1)}, s32[128,8]{1,0:T(8,128)S(1)}, s32[80,1]{1,0:T(8,128)S(1)}, s32[1,128]{1,0:T(1,128)S(1)}, /*index=5*/f32[64,1]{1,0:T(8,128)S(1)}) custom-call(s32[1]{0:T(128)} %bitcast.device_ref, s32[20]{0:T(128)} %kept_hbm.1, f32[640]{0:T(1024)} %weights_hbm.1, f32[32]{0:T(128)} %diffusion_hbm.1, ...), custom_call_target="tpu_custom_call" | custom-call | tf_op jit(solution)/shard_map/fourier/pallas_call | solution.py:382
  4.6 19.2 %all_to_all.20.y_ref = bf16[32,40,128]{2,1,0:T(8,128)(2,1)S(1)} all-to-all(bf16[32,40,128]{2,1,0:T(8,128)(2,1)S(1)} %get-tuple-element.18), channel_id=1, replica_groups=mesh['y'=4,'z'=16,'x'=4,'core'=2] {'y','x','core'}, dimensions={0} | all-to-all | bytes 655360 | tf_op jit(solution)/shard_map/all_to_all | solution.py:374
  23.7 0.4 gather.1
  24.1 29.0 %all_to_all.21.z_ref = bf16[16,4,2560]{2,1,0:T(4,128)(2,1)S(1)} all-to-all(bf16[16,4,2560]{2,1,0:T(4,128)(2,1)S(1)} %gather.1), channel_id=1, replica_groups=mesh['y'=4,'z'=16,'x'=4,'core'=2] {'z'}, dimensions={0} | all-to-all | bytes 655360 | tf_op jit(solution)/shard_map/all_to_all | solution.py:374
  53.1 0.0 copy-start
  53.1 0.0 copy-done.1
  53.1 1.9 %legendre.1 = (f32[2,2,32,2,512]{4,3,2,1,0:T(2,128)}, bf16[16,4,2816]{2,1,0:T(4,128)(2,1)S(1)}) custom-call(s32[1,128]{1,0:T(1,128)S(1)} %get-tuple-element.16.wave_ref, f32[64,1]{1,0:T(8,128)S(1)} %get-tuple-element.17.diffusion_ref, bf16[16,4,2560]{2,1,0:T(4,128)(2,1)S(1)} %all_to_all.21.z_ref, bf16[2,2,640,512]{3,2,1,0:T(8,128)(2,1)S(1)} %copy-done.1), custom_call_target="tpu_custom_call" | custom-call | tf_op jit(solution)/shard_map/legendre/pallas_call | solution.py:430
  55.0 27.4 %all_to_all.22.z_ref = bf16[16,4,2816]{2,1,0:T(4,128)(2,1)S(1)} all-to-all(bf16[16,4,2816]{2,1,0:T(4,128)(2,1)S(1)} %get-tuple-element.19), channel_id=1, replica_groups=mesh['y'=4,'z'=16,'x'=4,'core'=2] {'z'}, dimensions={0} | all-to-all | bytes 720896 | tf_op jit(solution)/shard_map/all_to_all | solution.py:374
  82.4 0.5 scatter.1
  82.9 21.2 %all_to_all.23.y_ref = bf16[32,48,128]{2,1,0:T(8,128)(2,1)S(1)} all-to-all(bf16[32,48,128]{2,1,0:T(8,128)(2,1)S(1)} %scatter.1), channel_id=1, replica_groups=mesh['y'=4,'z'=16,'x'=4,'core'=2] {'y','x','core'}, dimensions={0} | all-to-all | bytes 786432 | tf_op jit(solution)/shard_map/all_to_all | solution.py:374
  104.2 0.0 copy-done
  104.2 2.5 %grid.1 = (f32[20,4,2688]{2,1,0:T(4,128)}, f32[8,128]{1,0:T(8,128)}) custom-call(s32[1]{0:T(128)} %bitcast.device_ref, s32[80,1]{1,0:T(8,128)S(1)} %get-tuple-element.13.kept_ref, s32[1,512]{1,0:T(1,128)S(1)} %get-tuple-element.14.order_ref, s32[128,8]{1,0:T(8,128)S(1)} %get-tuple-element.15.column_ref, bf16[32,48,128]{2,1,0:T(8,128)(2,1)S(1)} %all_to_all.23.y_ref, ...), custom_call_target="tpu_custom_call" | custom-call | tf_op jit(solution)/shard_map/grid/pallas_call | solution.py:456
Async XLA Ops:
  0.6 52.5 %copy-start.1 = (bf16[2,2,640,512]{3,2,1,0:T(8,128)(2,1)S(1)}, bf16[2,2,640,512]{3,2,1,0:T(8,128)(2,1)}, u32[]{:S(2)}) copy-start(bf16[2,2,640,512]{3,2,1,0:T(8,128)(2,1)} %table_ref.2) | copy-start | bytes 7864324
  53.1 51.1 %copy-start = (bf16[4,512,672]{2,1,0:T(8,128)(2,1)S(1)}, bf16[4,512,672]{2,1,0:T(8,128)(2,1)}, u32[]{:S(2)}) copy-start(bf16[4,512,672]{2,1,0:T(8,128)(2,1)} %constant.28.clone.table_ref) | copy-start | bytes 8257540
